TPU v7x, 256 devices: a whole 4x4x8 slice. The times are simulated.
256 devices in a mesh: tok: 32 (over y, z), proto: 8 (over x, core).
Axes of the slice: x: 4, y: 4, z: 8, core: 2. Of those that a mesh axis runs over, the one named last changes fastest.
Arguments:
- teacher_patches: bfloat16 [16384, 256], P('tok'), as said below
- student_patches: bfloat16 [16384, 256], P('tok')
- prototypes: bfloat16 [65536, 256], P(('proto', 'tok'))
- mask_index: int32 [32, 512], P('tok'), may hold values from 0 to 511, each once within a row
- counts: int32 [32], P('tok'), may hold values from 1 to 256, 4096 in all
Outputs:
- grad_patches: float32 [16384, 256], P('tok')
- grad_prototypes: float32 [65536, 256], P(('proto', 'tok'))
Inputs may be any that keep to these rules, and one draw needn't show every extreme that they name: `teacher_patches`: teacher features and prototypes are real-valued. `mask_index`: each row is a permutation; only its first counts[d] entries are used. The counts sum to 4096; the largest is exactly 256.
All inputs are finite; a program needn't handle non-finite values. No bound on the sum of `counts` on one device may be relied on, other than what follows from the above.
Results may differ from a plain program's by a relative error of at most 0.0065.
Values may be sent and summed in bfloat16 or wider, within the bound.
No kernel may reach another device: no remote copies, remote signals or barrier semaphores. Data moves between devices by JAX's collectives and lax.ppermute only.
A program may use at most 128 MiB of HBM per device.

v0:
```python
import functools
import math

import jax
import jax.numpy as jnp
from jax import lax
from jax.experimental import pallas as pl
from jax.experimental.pallas import tpu as pltpu
from jax.sharding import Mesh, PartitionSpec as P

CAP = 256
BAL = 128
PROTO = 8
SLOTS = CAP // PROTO
ROWS = 4
TOK = ("y", "z")
LANES = 128
TEACHER_SCALE = 1.0 / 0.07
STUDENT_SCALE = 1.0 / 0.1
FAR_BELOW = -1e30
VMEM = 24 * 1024 * 1024
F32 = jnp.float32
BF16 = jnp.bfloat16
HIGH = lax.Precision.HIGHEST


def iota(shape, dim):
    return lax.broadcasted_iota(jnp.int32, shape, dim)


def dot_nt(a, b, precision=None):
    return lax.dot_general(
        a, b, (((1,), (1,)), ((), ())), precision=precision, preferred_element_type=F32
    )


def dot_tn(a, b, precision=None):
    return lax.dot_general(
        a, b, (((0,), (0,)), ((), ())), precision=precision, preferred_element_type=F32
    )


def dot_nn(a, b, precision=None):
    return jnp.dot(a, b, precision=precision, preferred_element_type=F32)


def blocks(tokens):
    return [(at // LANES, slice(at, min(at + LANES, tokens))) for at in range(0, tokens, LANES)]


def turned(rows, block, first_lane_only):
    at = iota((8, LANES), 0) == block
    if first_lane_only:
        at = at & (iota((8, LANES), 1) == 0)
    short = LANES - rows.shape[0]
    if short:
        rows = jnp.concatenate([rows, jnp.zeros((short, LANES), F32)], axis=0)
    return dot_nt(at.astype(F32), rows, HIGH)


def column(packed, block, size):
    at = (iota((8, LANES), 0) == block).astype(F32)
    return dot_tn(packed, at, HIGH)[:size]


def lse_over_first(values):
    top = jnp.max(values, axis=0)
    return top + jnp.log(jnp.sum(jnp.exp(values - top[None]), axis=0))


def row_offset(group, device):
    return lax.rem(group + device, PROTO)


def pick_kernel(
    count_ref, mask_ref, teacher_ref, student_ref, pay_ref, patch_ref, sem_ref,
):
    copies = [
        pltpu.make_async_copy(source, patch_ref.at[which], sem_ref.at[which])
        for which, source in enumerate((teacher_ref, student_ref))
    ]
    for copy in copies:
        copy.start()
    patches, width = teacher_ref.shape
    device = lax.axis_index("y") * pay_ref.shape[0] + lax.axis_index("z")
    offset = row_offset(lax.axis_index("proto"), device)
    at = (iota((SLOTS, patches), 1) == iota((SLOTS, patches), 0) * PROTO + offset).astype(BF16)
    mask = jnp.broadcast_to(mask_ref[...], (LANES, patches))
    high = dot_nt(at, (mask // 256).astype(F32).astype(BF16))
    low = dot_nt(at, (mask % 256).astype(F32).astype(BF16))
    chosen = (high * 256.0 + low + 0.5).astype(jnp.int32)
    lane = iota((SLOTS, LANES), 1)
    onehot = jnp.concatenate(
        [(lane + start == chosen).astype(F32).astype(BF16) for start in range(0, patches, LANES)],
        axis=1,
    )
    held = iota((SLOTS, width), 0) * PROTO + offset < count_ref[0]
    copies[0].wait()
    teach = jnp.where(held, dot_nn(onehot, patch_ref[0]), jnp.inf).astype(BF16)
    copies[1].wait()
    stud = dot_nn(onehot, patch_ref[1]).astype(BF16)
    both = jnp.concatenate([teach, stud], axis=0)
    pay_ref[...] = jnp.broadcast_to(both[None], pay_ref.shape)


def place_onehot(place, tokens):
    return (iota((tokens, place.shape[1]), 0).astype(F32) == place).astype(BF16)


def prototypes_kernel(place_ref, *refs):
    *pair_refs, protos_ref = refs
    share = pair_refs[0].shape[1]
    group = place_ref[0]
    core = lax.rem(group, 2)
    for away, pair_ref in enumerate(pair_refs):
        x = lax.rem(group // 2 + away, PROTO // 2)
        for other in range(2):
            start = pl.multiple_of((2 * x + (core + other) % 2) * share, share)
            protos_ref[pl.ds(start, share), :] = pair_ref[other]


def in_order(y, line_refs, pay_ref, first_slot):
    line = line_refs[0].shape[0]
    for away in range(ROWS):
        start = lax.rem(y + away, ROWS) * line
        pay_ref[pl.ds(start, line), :, :] = line_refs[away][:, first_slot : first_slot + SLOTS, :]
    devices, slots, width = pay_ref.shape
    return pay_ref[...].reshape(devices * slots, width)


def first_kernel(*refs):
    place_ref, *line_refs = refs[: ROWS + 1]
    protos_ref, teach_ref, place_out_ref, valid_ref, base_ref, col_ref, pay_ref = refs[ROWS + 1 :]
    arrived = in_order(place_ref[2], line_refs, pay_ref, 0).astype(F32)
    tokens = teach_ref.shape[0]
    slots, width = arrived.shape
    real = arrived < jnp.inf
    pick = (iota((8, width), 1) == 0).astype(BF16)
    flags = dot_nt(pick, real.astype(F32).astype(BF16))
    held = dot_nn(
        flags.astype(BF16), (iota((slots, LANES), 0) // SLOTS == iota((slots, LANES), 1)).astype(BF16)
    )
    before = dot_nn(
        held.astype(BF16), (iota((LANES, slots), 0) < iota((LANES, slots), 1) // SLOTS).astype(BF16)
    )[:1]
    bases = dot_nn(
        held.astype(BF16), (iota((LANES, LANES), 0) < iota((LANES, LANES), 1)).astype(BF16)
    )
    base_ref[...] = (bases + 0.5).astype(jnp.int32)
    inner = (iota((1, slots), 1) % SLOTS).astype(F32)
    place = jnp.where(flags[:1] > 0.5, before + inner, -1.0)
    place_out_ref[...] = jnp.broadcast_to(place, place_out_ref.shape)
    total = jnp.max(place, axis=1, keepdims=True) + 1.0
    order = iota((8, LANES), 0) * LANES + iota((8, LANES), 1)
    valid_ref[...] = (order.astype(F32) < total).astype(F32)
    onehot = place_onehot(place, tokens)
    teach = dot_nn(onehot, jnp.where(real, arrived, 0.0).astype(BF16)).astype(BF16)
    teach_ref[...] = teach
    step = 2 * LANES
    alive = iota((tokens, step), 0).astype(F32) < total
    rows = []
    for start in range(0, protos_ref.shape[0], step):
        scores = dot_nt(teach, protos_ref[start : start + step, :]) * TEACHER_SCALE
        scores = jnp.where(alive, scores, FAR_BELOW)
        top = jnp.max(scores, axis=0, keepdims=True)
        lse = top + jnp.log(jnp.sum(jnp.exp(scores - top), axis=0, keepdims=True))
        rows += [lse[:, :LANES], lse[:, LANES:]]
    col_ref[...] = jnp.broadcast_to(jnp.concatenate(rows, axis=0)[None], col_ref.shape)


def wide(packed):
    return jnp.concatenate([packed[i : i + 1, :] for i in range(packed.shape[0])], axis=1)


def exps_below_top(left_ref, protos_ref, scale, shift, out_ref):
    step = 2 * LANES
    for start in range(0, protos_ref.shape[0], step):
        scores = dot_nt(left_ref[...], protos_ref[start : start + step, :]) * scale
        if shift is not None:
            scores = scores + shift[:, start : start + step]
        out_ref[:, start : start + step] = scores
    tops = jnp.zeros((8, LANES), F32)
    totals = jnp.zeros((8, LANES), F32)
    starts = range(0, protos_ref.shape[0], LANES)
    for block, rows in blocks(left_ref.shape[0]):
        top = out_ref[rows, :LANES]
        for start in starts[1:]:
            top = jnp.maximum(top, out_ref[rows, start : start + LANES])
        top = jnp.broadcast_to(jnp.max(top, axis=1, keepdims=True), top.shape)
        sums = jnp.zeros_like(top)
        for start in starts:
            exps = jnp.exp(out_ref[rows, start : start + LANES] - top)
            out_ref[rows, start : start + LANES] = exps
            sums += exps
        tops += turned(top, block, True)
        totals += turned(sums, block, False)
    return tops, totals


def second_kernel(teach_ref, protos_ref, col_ref, stud_row_ref, exp_ref, top_ref, row_ref, stud_out_ref):
    col_pot = -wide(lse_over_first(col_ref[...]))
    tops, totals = exps_below_top(teach_ref, protos_ref, TEACHER_SCALE, col_pot, exp_ref)
    top_ref[...] = tops
    lses = tops + jnp.log(jnp.where(totals > 0.0, totals, 1.0))
    row_ref[...] = jnp.broadcast_to(lses[None], row_ref.shape)
    stud_out_ref[...] = stud_row_ref[...]


def weighted_columns(exp_ref, weight):
    chunks = exp_ref.shape[1] // LANES
    sums = [jnp.zeros((8, LANES), F32) for _ in range(chunks)]
    for block, rows in blocks(exp_ref.shape[0]):
        size = rows.stop - rows.start
        factor = column(weight, block, size)
        for chunk in range(chunks):
            part = exp_ref[rows, chunk * LANES : (chunk + 1) * LANES] * factor
            sums[chunk] += jnp.sum(part.reshape(size // 8, 8, LANES), axis=0)
    return jnp.concatenate([jnp.sum(part, axis=0, keepdims=True) for part in sums], axis=0)


def third_kernel(exp_ref, top_ref, valid_ref, row_ref, factor_ref, col_ref):
    row_pot = -lse_over_first(row_ref[...])
    factor = jnp.where(valid_ref[...] > 0.0, jnp.exp(top_ref[...] + row_pot), 0.0)
    factor_ref[...] = factor
    col_ref[...] = jnp.broadcast_to(weighted_columns(exp_ref, factor)[None], col_ref.shape)


def row_scale(valid_ref, sums):
    alive = valid_ref[...] > 0.0
    return jnp.where(alive, 1.0 / jnp.where(alive, sums, 1.0), 0.0)


def column_kernel(exp_ref, factor_ref, valid_ref, row_ref, col_ref):
    weight = row_scale(valid_ref, jnp.sum(row_ref[...], axis=0)) * factor_ref[...]
    col_ref[...] = jnp.broadcast_to(weighted_columns(exp_ref, weight)[None], col_ref.shape)


def weighted_rows(exp_ref, weight):
    sums = jnp.zeros((8, LANES), F32)
    for block, rows in blocks(exp_ref.shape[0]):
        part = jnp.zeros((rows.stop - rows.start, LANES), F32)
        for chunk in range(weight.shape[0]):
            values = exp_ref[rows, chunk * LANES : (chunk + 1) * LANES]
            part += values * weight[chunk : chunk + 1, :]
        sums += turned(part, block, False)
    return sums


def row_kernel(exp_ref, factor_ref, col_ref, row_ref):
    weight = 1.0 / jnp.sum(col_ref[...], axis=0)
    sums = weighted_rows(exp_ref, weight) * factor_ref[...]
    row_ref[...] = jnp.broadcast_to(sums[None], row_ref.shape)


def student_kernel(*refs):
    place_ref, *line_refs = refs[: ROWS + 1]
    slot_ref, protos_ref, stud_ref, row_ref, pay_ref, exp_ref = refs[ROWS + 1 :]
    arrived = in_order(place_ref[2], line_refs, pay_ref, SLOTS)
    onehot = place_onehot(slot_ref[:1, :], stud_ref.shape[0])
    stud_ref[...] = dot_nn(onehot, arrived).astype(BF16)
    tops, totals = exps_below_top(stud_ref, protos_ref, STUDENT_SCALE, None, exp_ref)
    row_ref[...] = tops + jnp.log(jnp.where(totals > 0.0, totals, 1.0))


def last_row_kernel(exp_ref, factor_ref, col_ref, stud_row_ref, row_ref):
    weight = 1.0 / jnp.sum(col_ref[...], axis=0)
    sums = weighted_rows(exp_ref, weight) * factor_ref[...]
    both = jnp.concatenate([sums, stud_row_ref[...]], axis=0)
    row_ref[...] = jnp.broadcast_to(both[None], row_ref.shape)


def gradient_kernel(
    base_ref, exp_ref, factor_ref, valid_ref, col_ref, row_ref, stud_ref, protos_ref,
    tok_ref, grad_ref, scale_ref, lse_ref, total_ref,
):
    tokens, width = stud_ref.shape
    weights = 1.0 / jnp.sum(col_ref[...], axis=0)
    sums = jnp.sum(row_ref[:, :8, :], axis=0)
    scale = row_scale(valid_ref, sums) * (factor_ref[...] * STUDENT_SCALE)
    lses = lse_over_first(row_ref[:, 8:, :]) - math.log(STUDENT_SCALE)
    lses = jnp.where(valid_ref[...] > 0.0, lses, -FAR_BELOW)
    for block, rows in blocks(tokens):
        size = rows.stop - rows.start
        scale_ref[rows, :] = column(scale, block, size)
        lse_ref[rows, :] = column(lses, block, size)
    step = 2 * LANES
    for chunk in range(protos_ref.shape[0] // step):
        scores = dot_nt(stud_ref[...], protos_ref[chunk * step : (chunk + 1) * step, :])
        for half in range(2):
            index = 2 * chunk + half
            lanes = slice(index * LANES, (index + 1) * LANES)
            part = scores[:, half * LANES : (half + 1) * LANES] * STUDENT_SCALE
            student = jnp.exp(part - lse_ref[...])
            target = exp_ref[:, lanes] * scale_ref[...] * weights[index : index + 1, :]
            grad_ref[:, lanes] = (student - target).astype(BF16)
    total_ref[:tokens, :] = dot_nn(grad_ref[...], protos_ref[...])
    total_ref[tokens:, :] = jnp.zeros((SLOTS, width), F32)
    for device in range(tok_ref.shape[0]):
        base = base_ref[0, device]
        start = pl.multiple_of(base // 8 * 8, 8)
        rows = pltpu.roll(total_ref[pl.ds(start, SLOTS + 8), :], SLOTS + 8 - base % 8, 0)
        tok_ref[device, :, :] = rows[:SLOTS, :].astype(BF16)


def proto_kernel(place_ref, grad_ref, stud_ref, near_ref, far_ref):
    share = near_ref.shape[1]
    group = place_ref[0]
    for away in range(PROTO // 2):
        x = lax.rem(group // 2 + away, PROTO // 2)
        core = lax.rem(group, 2)
        start = pl.multiple_of((2 * x + 1 - core) * share, share)
        far_ref[away, :, :] = dot_tn(grad_ref[:, pl.ds(start, share)], stud_ref[...])
        start = pl.multiple_of((2 * x + core) * share, share)
        near_ref[away, :, :] = dot_tn(grad_ref[:, pl.ds(start, share)], stud_ref[...])


def sum_kernel(parts_ref, near_ref, *refs):
    *far_refs, out_ref, proto_ref = refs
    total = jnp.sum(parts_ref[...].astype(F32), axis=0)
    out_ref[...] = jnp.broadcast_to(total[None], out_ref.shape)
    total = near_ref[0]
    for far_ref in far_refs:
        total = total + far_ref[...]
    proto_ref[...] = total


def patch_kernel(place_ref, count_ref, mask_ref, onehot_ref):
    patches = onehot_ref.shape[0]
    device = place_ref[1]
    wanted = iota((patches, CAP), 1)
    rank = (wanted % SLOTS) * PROTO + row_offset(wanted // SLOTS, device)
    at = (iota((patches, CAP), 0) == rank).astype(F32)
    mask = jnp.broadcast_to(mask_ref[...].astype(F32), (8, patches))
    chosen = (dot_nn(mask, at, HIGH)[:1] + 0.5).astype(jnp.int32)
    chosen = jnp.where(rank[:1, :] < count_ref[0], chosen, -1)
    onehot_ref[...] = (iota((patches, CAP), 0) == chosen).astype(BF16)


def spread_kernel(onehot_ref, rows_ref, out_ref):
    rest = rows_ref[...].reshape(CAP, out_ref.shape[1])
    total = None
    for _ in range(3):
        part = rest.astype(BF16)
        rest = rest - part.astype(F32)
        moved = dot_nn(onehot_ref[...], part)
        total = moved if total is None else total + moved
    out_ref[...] = total


def call(kernel, outs, inputs, scalars=0, scratch=(), cost=None):
    smem = [pl.BlockSpec(memory_space=pltpu.SMEM)] * scalars
    arrays = [pl.BlockSpec(memory_space=pltpu.VMEM)] * (len(inputs) - scalars)
    return pl.pallas_call(
        kernel,
        out_shape=[jax.ShapeDtypeStruct(shape, dtype) for shape, dtype in outs],
        in_specs=smem + arrays,
        out_specs=[pl.BlockSpec(memory_space=pltpu.VMEM)] * len(outs),
        scratch_shapes=list(scratch),
        compiler_params=pltpu.CompilerParams(vmem_limit_bytes=VMEM),
        cost_estimate=cost,
    )(*inputs)


def most_tokens(devices):
    slack = sum((PROTO - 1 - device % PROTO) for device in range(devices))
    return -(-((BAL * devices + slack) // PROTO) // 16) * 16


def exchange(parts, axis):
    return lax.all_to_all(parts, axis, 0, 0, tiled=True)


def on_device(devices, teacher_patches, student_patches, prototypes, mask_index, counts):
    patches, width = teacher_patches.shape
    share = prototypes.shape[0]
    protos_held = PROTO * share
    chunks = protos_held // LANES
    tokens = most_tokens(devices)
    line = devices // ROWS
    group = lax.axis_index("proto")
    y = lax.axis_index("y")
    device = y * line + lax.axis_index("z")
    place = jnp.stack([group, device, y]).astype(jnp.int32)

    half = PROTO // 2
    swap = [(p, p ^ 1) for p in range(PROTO)]
    routes = [[(p, (p + 2 * away) % PROTO) for p in range(PROTO)] for away in range(half)]
    (pay,) = pl.pallas_call(
        pick_kernel,
        out_shape=[
            jax.ShapeDtypeStruct((line, 2 * SLOTS, width), BF16),
        ],
        in_specs=[
            pl.BlockSpec(memory_space=pltpu.SMEM),
            pl.BlockSpec(memory_space=pltpu.VMEM),
            pl.BlockSpec(memory_space=pl.ANY),
            pl.BlockSpec(memory_space=pl.ANY),
        ],
        out_specs=[pl.BlockSpec(memory_space=pltpu.VMEM)],
        scratch_shapes=[pltpu.VMEM((2, patches, width), BF16), pltpu.SemaphoreType.DMA((2,))],
        compiler_params=pltpu.CompilerParams(vmem_limit_bytes=60 * 1024 * 1024),
    )(counts, mask_index, teacher_patches, student_patches)
    pay = exchange(pay, "z")
    lines = [pay]
    for away in range(1, ROWS):
        route = [(i, (i - away) % ROWS) for i in range(ROWS)]
        lines.append(lax.ppermute(pay, "y", route))
    pair = jnp.stack([prototypes, lax.ppermute(prototypes, "proto", swap)])
    pairs_held = [pair]
    for away in range(1, half):
        pairs_held.append(lax.ppermute(pair, "proto", routes[-away % half]))
    (protos,) = call(
        prototypes_kernel, [((protos_held, width), BF16)], (place, *pairs_held), scalars=1
    )
    (onehot,) = call(
        patch_kernel, [((patches, CAP), BF16)], (place, counts, mask_index), scalars=2
    )

    packed = ((8, LANES), F32)
    col_out = ((PROTO, chunks, LANES), F32)
    row_out = ((devices, 8, LANES), F32)
    pay_scratch = pltpu.VMEM((devices, SLOTS, width), BF16)
    pairs = tokens * protos_held
    work = pl.CostEstimate(
        flops=2 * pairs * width, bytes_accessed=8 * pairs, transcendentals=pairs
    )
    teach, slots, valid, base, col = call(
        first_kernel,
        [
            ((tokens, width), BF16),
            ((8, devices * SLOTS), F32),
            packed,
            ((8, LANES), jnp.int32),
            col_out,
        ],
        (place, *lines, protos),
        scalars=1,
        scratch=(pay_scratch,),
        cost=work,
    )
    col = exchange(col, "proto")
    stud, stud_row = call(
        student_kernel,
        [((tokens, width), BF16), packed],
        (place, *lines, slots, protos),
        scalars=1,
        scratch=(pay_scratch, pltpu.VMEM((tokens, protos_held), F32)),
        cost=work,
    )
    exps, top, row, stud_row = call(
        second_kernel,
        [((tokens, protos_held), F32), packed, row_out, packed],
        (teach, protos, col, stud_row),
        cost=work,
    )
    row = exchange(row, TOK)
    factor, col = call(third_kernel, [packed, col_out], (exps, top, valid, row))
    col = exchange(col, "proto")
    (row,) = call(row_kernel, [row_out], (exps, factor, col))
    row = exchange(row, TOK)
    (col,) = call(column_kernel, [col_out], (exps, factor, valid, row))
    col = exchange(col, "proto")
    (row,) = call(
        last_row_kernel, [((devices, 16, LANES), F32)], (exps, factor, col, stud_row)
    )
    row = exchange(row, TOK)
    grad_slots, grads = call(
        gradient_kernel,
        [((devices, SLOTS, width), BF16), ((tokens, protos_held), BF16)],
        (base, exps, factor, valid, col, row, stud, protos),
        scalars=1,
        scratch=(
            pltpu.VMEM((tokens, LANES), F32),
            pltpu.VMEM((tokens, LANES), F32),
            pltpu.VMEM((tokens + SLOTS, width), F32),
        ),
        cost=work,
    )
    near, far = call(
        proto_kernel,
        [((half, share, width), F32), ((half, share, width), F32)],
        (place, grads, stud),
        scalars=1,
        cost=work,
    )
    mine = near + lax.ppermute(far, "proto", swap)
    arrived = [lax.ppermute(mine[away], "proto", routes[away]) for away in range(1, half)]
    rows, grad_prototypes = call(
        sum_kernel,
        [((PROTO, SLOTS, width), F32), ((share, width), F32)],
        (exchange(grad_slots, TOK), mine, *arrived),
    )
    rows = exchange(rows, "proto")
    (grad_patches,) = call(spread_kernel, [((patches, width), F32)], (onehot, rows))
    return (grad_patches, grad_prototypes)


def solution(mesh):
    devices, protos = mesh.devices.shape
    shape = (ROWS, devices // ROWS, protos)
    mesh = Mesh(mesh.devices.reshape(shape), (*TOK, "proto"))
    return jax.shard_map(
        functools.partial(on_device, devices),
        mesh=mesh,
        in_specs=(
            P(TOK, None),
            P(TOK, None),
            P(("proto", *TOK), None),
            P(TOK, None),
            P(TOK),
        ),
        out_specs=(P(TOK, None), P(("proto", *TOK), None)),
        check_vma=False,
    )
```

profile of v0, /device:TPU:32, one launch (start us, length us, event | category | flops | bytes accessed | tf_op | source)
XLA Modules:
  0.0 163.1 jit_solution(13783954528191951592)
XLA Ops:
  0.6 0.1 collective-permute-start.3
  1.4 2.7 %shard_map.69 = bf16[8,64,256]{2,1,0:T(8,128)(2,1)} custom-call(s32[1]{0:T(128)S(6)} %copy.7.count_ref, s32[1,512]{1,0:T(1,128)} %mask_ref.3, bf16[512,256]{1,0:T(8,128)(2,1)} %teacher_ref.1, bf16[512,256]{1,0:T(8,128)(2,1)} %student_ref.1), custom_call_target="tpu_custom_call" | custom-call | tf_op jit(solution)/shard_map/pallas_call | solution.py:388
  4.1 8.6 %all-to-all-start = ((bf16[8,64,256]{2,1,0:T(8,128)(2,1)}), bf16[8,64,256]{2,1,0:T(8,128)(2,1)S(1)}, u32[]{:S(2)}, u32[]{:S(2)}) async-start(bf16[8,64,256]{2,1,0:T(8,128)(2,1)} %shard_map.69), calls=%async_computation | async-start | bytes 524288 | tf_op jit(solution)/shard_map/all_to_all | solution.py:370
  12.7 0.0 collective-permute-done.3
  12.7 0.9 pad_maximum_fusion.refs_0_
  13.6 2.8 %collective-permute-start.4 = (bf16[2,256,256]{2,1,0:T(8,128)(2,1)S(1)}, bf16[2,256,256]{2,1,0:T(8,128)(2,1)S(1)}, u32[]{:S(2)}, u32[]{:S(2)}) collective-permute-start(bf16[2,256,256]{2,1,0:T(8,128)(2,1)S(1)} %pad_maximum_fusion.refs_0_), channel_id=1, source_target_pairs={{0,6},{1,7},{2,0},{3,1},{4,2},{5,3},{6,4},{7,5},{8,14},{9,15},{10,... | collective-permute-start | bytes 786440 | tf_op jit(solution)/shard_map/ppermute | solution.py:411
  16.5 0.8 collective-permute-start.5
  17.3 0.9 collective-permute-start.6
  18.2 5.6 %all-to-all-done.refs_1_ = bf16[8,64,256]{2,1,0:T(8,128)(2,1)S(1)} async-done(((bf16[8,64,256]{2,1,0:T(8,128)(2,1)}), bf16[8,64,256]{2,1,0:T(8,128)(2,1)S(1)}, u32[]{:S(2)}, u32[]{:S(2)}) %all-to-all-start) | async-done | bytes 262176 | tf_op jit(solution)/shard_map/all_to_all | solution.py:370
  23.8 3.0 %collective-permute-start = (bf16[8,64,256]{2,1,0:T(8,128)(2,1)S(1)}, bf16[8,64,256]{2,1,0:T(8,128)(2,1)S(1)}, u32[]{:S(2)}, u32[]{:S(2)}) collective-permute-start(bf16[8,64,256]{2,1,0:T(8,128)(2,1)S(1)} %all-to-all-done.refs_1_), channel_id=1, source_target_pairs={{0,192},{64,0},{128,64},{192,128},{1,193},{65,1},{129,65},{193,129... | collective-permute-start | bytes 786440 | tf_op jit(solution)/shard_map/ppermute | solution.py:407
  26.8 0.6 collective-permute-start.1
  27.4 0.4 collective-permute-done.4.refs_1_
  27.8 1.6 collective-permute-start.2
  29.4 0.1 pad_add_fusion.place_ref.refs_0_
  29.5 0.0 collective-permute-done.5.refs_2_
  29.5 2.0 %collective-permute-done.6.refs_3_ = bf16[2,256,256]{2,1,0:T(8,128)(2,1)S(1)} collective-permute-done((bf16[2,256,256]{2,1,0:T(8,128)(2,1)S(1)}, bf16[2,256,256]{2,1,0:T(8,128)(2,1)S(1)}, u32[]{:S(2)}, u32[]{:S(2)}) %collective-permute-start.6) | collective-permute-done | bytes 262176 | tf_op jit(solution)/shard_map/ppermute | solution.py:411
  31.5 0.6 shard_map.70.refs_5_.refs_6_.protos_ref
  32.1 4.1 %collective-permute-done.refs_2_ = bf16[8,64,256]{2,1,0:T(8,128)(2,1)S(1)} collective-permute-done((bf16[8,64,256]{2,1,0:T(8,128)(2,1)S(1)}, bf16[8,64,256]{2,1,0:T(8,128)(2,1)S(1)}, u32[]{:S(2)}, u32[]{:S(2)}) %collective-permute-start) | collective-permute-done | bytes 262176 | tf_op jit(solution)/shard_map/ppermute | solution.py:407
  36.2 1.0 collective-permute-done.1.refs_3_
  37.2 2.7 %collective-permute-done.2.refs_4_ = bf16[8,64,256]{2,1,0:T(8,128)(2,1)S(1)} collective-permute-done((bf16[8,64,256]{2,1,0:T(8,128)(2,1)S(1)}, bf16[8,64,256]{2,1,0:T(8,128)(2,1)S(1)}, u32[]{:S(2)}, u32[]{:S(2)}) %collective-permute-start.2) | collective-permute-done | bytes 262176 | tf_op jit(solution)/shard_map/ppermute | solution.py:407
  39.9 3.7 %shard_map.71 = (bf16[528,256]{1,0:T(8,128)(2,1)S(1)}, f32[8,1024]{1,0:T(8,128)S(1)}, f32[8,128]{1,0:T(8,128)S(1)}, s32[8,128]{1,0:T(8,128)S(1)}, f32[8,16,128]{2,1,0:T(8,128)}) custom-call(s32[3]{0:T(128)S(1)} %pad_add_fusion.place_ref.refs_0_, bf16[8,64,256]{2,1,0:T(8,128)(2,1)S(1)} %all-to-all-done.refs_1_, ...), custom_call_target="tpu_custom_call" | custom-call | flops 553648128 | bytes 8650752 | tf_op jit(solution)/shard_map/pallas_call | solution.py:353
  43.6 4.3 %all-to-all-start.1 = ((f32[8,16,128]{2,1,0:T(8,128)}), f32[8,16,128]{2,1,0:T(8,128)S(1)}, u32[]{:S(2)}, u32[]{:S(2)}) async-start(f32[8,16,128]{2,1,0:T(8,128)} %get-tuple-element.23), calls=%async_computation.1 | async-start | bytes 131072 | tf_op jit(solution)/shard_map/all_to_all | solution.py:370
  47.9 3.2 %shard_map.72 = (bf16[528,256]{1,0:T(8,128)(2,1)S(1)}, f32[8,128]{1,0:T(8,128)S(1)}) custom-call(s32[3]{0:T(128)S(1)} %pad_add_fusion.place_ref.refs_0_, bf16[8,64,256]{2,1,0:T(8,128)(2,1)S(1)} %all-to-all-done.refs_1_, bf16[8,64,256]{2,1,0:T(8,128)(2,1)S(1)} %collective-permute-done.refs_2_, bf16[8,64,256]{2,1,0:T(8,128)(2,1)S(1)} %collective-permute-done.1.refs_3_, ...), custom_call_target="tpu_custom_call" | custom-call | flops 553648128 | bytes 8650752 | tf_op jit(solution)/shard_map/pallas_call | solution.py:353
  51.1 2.4 %all-to-all-done.1.col_ref = f32[8,16,128]{2,1,0:T(8,128)S(1)} async-done(((f32[8,16,128]{2,1,0:T(8,128)}), f32[8,16,128]{2,1,0:T(8,128)S(1)}, u32[]{:S(2)}, u32[]{:S(2)}) %all-to-all-start.1) | async-done | bytes 65568 | tf_op jit(solution)/shard_map/all_to_all | solution.py:370
  53.5 2.0 %shard_map.73 = (f32[528,2048]{1,0:T(8,128)S(1)}, f32[8,128]{1,0:T(8,128)S(1)}, f32[32,8,128]{2,1,0:T(8,128)S(1)}, f32[8,128]{1,0:T(8,128)S(1)}) custom-call(bf16[528,256]{1,0:T(8,128)(2,1)S(1)} %get-tuple-element.22.teach_ref, bf16[2048,256]{1,0:T(8,128)(2,1)S(1)} %shard_map.70.refs_5_.refs_6_.protos_ref, f32[8,16,128]{2,1,0:T(8,128)S(1)} %all-to-all-done.1.col_ref, ...), custom_call_target="tpu_custom_call" | custom-call | flops 553648128 | bytes 8650752 | tf_op jit(solution)/shard_map/pallas_call | solution.py:353
  55.5 16.1 %all_to_all.45.row_ref = f32[32,8,128]{2,1,0:T(8,128)S(1)} all-to-all(f32[32,8,128]{2,1,0:T(8,128)S(1)} %get-tuple-element.29), channel_id=1, replica_groups=mesh['y'=4,'z'=8,'proto'=8] {'y','z'}, dimensions={0} | all-to-all | bytes 262144 | tf_op jit(solution)/shard_map/all_to_all | solution.py:370
  71.7 0.8 shard_map.74
  72.5 8.3 %all_to_all.46.col_ref = f32[8,16,128]{2,1,0:T(8,128)S(1)} all-to-all(f32[8,16,128]{2,1,0:T(8,128)S(1)} %get-tuple-element.31), channel_id=1, replica_groups=mesh['y'=4,'z'=8,'proto'=8] {'proto'}, dimensions={0} | all-to-all | bytes 131072 | tf_op jit(solution)/shard_map/all_to_all | solution.py:370
  80.8 0.7 shard_map.75
  81.5 13.8 %all_to_all.47.row_ref = f32[32,8,128]{2,1,0:T(8,128)S(1)} all-to-all(f32[32,8,128]{2,1,0:T(8,128)S(1)} %shard_map.75), channel_id=1, replica_groups=mesh['y'=4,'z'=8,'proto'=8] {'y','z'}, dimensions={0} | all-to-all | bytes 262144 | tf_op jit(solution)/shard_map/all_to_all | solution.py:370
  95.3 0.8 shard_map.76
  96.1 8.0 %all_to_all.48.col_ref = f32[8,16,128]{2,1,0:T(8,128)S(1)} all-to-all(f32[8,16,128]{2,1,0:T(8,128)S(1)} %shard_map.76), channel_id=1, replica_groups=mesh['y'=4,'z'=8,'proto'=8] {'proto'}, dimensions={0} | all-to-all | bytes 131072 | tf_op jit(solution)/shard_map/all_to_all | solution.py:370
  104.1 0.7 shard_map.77
  104.8 16.3 %all_to_all.49.row_ref = f32[32,16,128]{2,1,0:T(8,128)S(1)} all-to-all(f32[32,16,128]{2,1,0:T(8,128)S(1)} %shard_map.77), channel_id=1, replica_groups=mesh['y'=4,'z'=8,'proto'=8] {'y','z'}, dimensions={0} | all-to-all | bytes 524288 | tf_op jit(solution)/shard_map/all_to_all | solution.py:370
  121.1 4.2 %shard_map.78 = (bf16[32,32,256]{2,1,0:T(8,128)(2,1)}, bf16[528,2048]{1,0:T(8,128)(2,1)S(1)}) custom-call(s32[8,128]{1,0:T(8,128)S(1)} %get-tuple-element.21.base_ref, f32[528,2048]{1,0:T(8,128)S(1)} %get-tuple-element.26.exp_ref, f32[8,128]{1,0:T(8,128)S(1)} %get-tuple-element.30.factor_ref, f32[8,128]{1,0:T(8,128)S(1)} %get-tuple-element.28.valid_ref, ...), custom_call_target="tpu_custom_call" | custom-call | flops 553648128 | bytes 8650752 | tf_op jit(solution)/shard_map/pallas_call | solution.py:353
  125.4 1.6 shard_map.79
  127.0 0.1 collective-permute-start.7
  127.1 0.0 copy-start
  127.1 4.6 %all-to-all-start.7 = ((bf16[32,32,256]{2,1,0:T(8,128)(2,1)}), bf16[32,32,256]{2,1,0:T(8,128)(2,1)S(1)}, u32[]{:S(2)}, u32[]{:S(2)}) async-start(bf16[32,32,256]{2,1,0:T(8,128)(2,1)} %get-tuple-element.34), calls=%async_computation.7 | async-start | bytes 1048576 | tf_op jit(solution)/shard_map/all_to_all | solution.py:370
  131.7 0.0 collective-permute-done.7
  131.7 1.4 add.7.near_ref
  133.1 0.1 slice_bitcast_fusion
  133.2 1.2 collective-permute-start.10
  134.4 0.9 collective-permute-start.8
  135.3 1.0 collective-permute-start.9
  136.3 13.9 %all-to-all-done.7.parts_ref = bf16[32,32,256]{2,1,0:T(8,128)(2,1)S(1)} async-done(((bf16[32,32,256]{2,1,0:T(8,128)(2,1)}), bf16[32,32,256]{2,1,0:T(8,128)(2,1)S(1)}, u32[]{:S(2)}, u32[]{:S(2)}) %all-to-all-start.7) | async-done | bytes 524320 | tf_op jit(solution)/shard_map/all_to_all | solution.py:370
  150.2 0.0 collective-permute-done.10.refs_2_
  150.2 0.0 collective-permute-done.8.refs_0_
  150.2 0.0 collective-permute-done.9.refs_1_
  150.2 0.9 shard_map.80
  151.1 3.4 %all-to-all-start.8 = ((f32[8,32,256]{2,1,0:T(8,128)}), f32[8,32,256]{2,1,0:T(8,128)S(1)}, u32[]{:S(2)}, u32[]{:S(2)}) async-start(f32[8,32,256]{2,1,0:T(8,128)} %get-tuple-element.38), calls=%async_computation.8 | async-start | bytes 524288 | tf_op jit(solution)/shard_map/all_to_all | solution.py:370
  154.5 0.0 copy-done
  154.5 1.0 shard_map.68.onehot_ref
  155.6 6.4 %all-to-all-done.8.rows_ref = f32[8,32,256]{2,1,0:T(8,128)S(1)} async-done(((f32[8,32,256]{2,1,0:T(8,128)}), f32[8,32,256]{2,1,0:T(8,128)S(1)}, u32[]{:S(2)}, u32[]{:S(2)}) %all-to-all-start.8) | async-done | bytes 262176 | tf_op jit(solution)/shard_map/all_to_all | solution.py:370
  162.0 1.2 shard_map.81
Async XLA Ops:
  0.6 12.1 %collective-permute-start.3 = (bf16[256,256]{1,0:T(8,128)(2,1)}, bf16[256,256]{1,0:T(8,128)(2,1)S(1)}, u32[]{:S(2)}, u32[]{:S(2)}) collective-permute-start(bf16[256,256]{1,0:T(8,128)(2,1)} %param.7), channel_id=1, source_target_pairs={{0,1},{1,0},{2,3},{3,2},{4,5},{5,4},{6,7},{7,6},{8,9},{9,8},{10,11... | collective-permute-start | bytes 393224 | tf_op jit(solution)/shard_map/ppermute | solution.py:408
  4.1 19.7 %all-to-all-start = ((bf16[8,64,256]{2,1,0:T(8,128)(2,1)}), bf16[8,64,256]{2,1,0:T(8,128)(2,1)S(1)}, u32[]{:S(2)}, u32[]{:S(2)}) async-start(bf16[8,64,256]{2,1,0:T(8,128)(2,1)} %shard_map.69), calls=%async_computation | async-start | bytes 524288 | tf_op jit(solution)/shard_map/all_to_all | solution.py:370
  13.6 14.2 %collective-permute-start.4 = (bf16[2,256,256]{2,1,0:T(8,128)(2,1)S(1)}, bf16[2,256,256]{2,1,0:T(8,128)(2,1)S(1)}, u32[]{:S(2)}, u32[]{:S(2)}) collective-permute-start(bf16[2,256,256]{2,1,0:T(8,128)(2,1)S(1)} %pad_maximum_fusion.refs_0_), channel_id=1, source_target_pairs={{0,6},{1,7},{2,0},{3,1},{4,2},{5,3},{6,4},{7,5},{8,14},{9,15},{10,... | collective-permute-start | bytes 786440 | tf_op jit(solution)/shard_map/ppermute | solution.py:411
  16.5 13.0 %collective-permute-start.5 = (bf16[2,256,256]{2,1,0:T(8,128)(2,1)S(1)}, bf16[2,256,256]{2,1,0:T(8,128)(2,1)S(1)}, u32[]{:S(2)}, u32[]{:S(2)}) collective-permute-start(bf16[2,256,256]{2,1,0:T(8,128)(2,1)S(1)} %pad_maximum_fusion.refs_0_), channel_id=1, source_target_pairs={{0,4},{1,5},{2,6},{3,7},{4,0},{5,1},{6,2},{7,3},{8,12},{9,13},{10,... | collective-permute-start | bytes 786440 | tf_op jit(solution)/shard_map/ppermute | solution.py:411
  17.3 14.2 %collective-permute-start.6 = (bf16[2,256,256]{2,1,0:T(8,128)(2,1)S(1)}, bf16[2,256,256]{2,1,0:T(8,128)(2,1)S(1)}, u32[]{:S(2)}, u32[]{:S(2)}) collective-permute-start(bf16[2,256,256]{2,1,0:T(8,128)(2,1)S(1)} %pad_maximum_fusion.refs_0_), channel_id=1, source_target_pairs={{0,2},{1,3},{2,4},{3,5},{4,6},{5,7},{6,0},{7,1},{8,10},{9,11},{10,... | collective-permute-start | bytes 786440 | tf_op jit(solution)/shard_map/ppermute | solution.py:411
  23.8 12.4 %collective-permute-start = (bf16[8,64,256]{2,1,0:T(8,128)(2,1)S(1)}, bf16[8,64,256]{2,1,0:T(8,128)(2,1)S(1)}, u32[]{:S(2)}, u32[]{:S(2)}) collective-permute-start(bf16[8,64,256]{2,1,0:T(8,128)(2,1)S(1)} %all-to-all-done.refs_1_), channel_id=1, source_target_pairs={{0,192},{64,0},{128,64},{192,128},{1,193},{65,1},{129,65},{193,129... | collective-permute-start | bytes 786440 | tf_op jit(solution)/shard_map/ppermute | solution.py:407
  26.8 10.3 %collective-permute-start.1 = (bf16[8,64,256]{2,1,0:T(8,128)(2,1)S(1)}, bf16[8,64,256]{2,1,0:T(8,128)(2,1)S(1)}, u32[]{:S(2)}, u32[]{:S(2)}) collective-permute-start(bf16[8,64,256]{2,1,0:T(8,128)(2,1)S(1)} %all-to-all-done.refs_1_), channel_id=1, source_target_pairs={{0,128},{64,192},{128,0},{192,64},{1,129},{65,193},{129,1},{193,65... | collective-permute-start | bytes 786440 | tf_op jit(solution)/shard_map/ppermute | solution.py:407
  27.8 12.1 %collective-permute-start.2 = (bf16[8,64,256]{2,1,0:T(8,128)(2,1)S(1)}, bf16[8,64,256]{2,1,0:T(8,128)(2,1)S(1)}, u32[]{:S(2)}, u32[]{:S(2)}) collective-permute-start(bf16[8,64,256]{2,1,0:T(8,128)(2,1)S(1)} %all-to-all-done.refs_1_), channel_id=1, source_target_pairs={{0,64},{64,128},{128,192},{192,0},{1,65},{65,129},{129,193},{193,1... | collective-permute-start | bytes 786440 | tf_op jit(solution)/shard_map/ppermute | solution.py:407
  43.6 9.9 %all-to-all-start.1 = ((f32[8,16,128]{2,1,0:T(8,128)}), f32[8,16,128]{2,1,0:T(8,128)S(1)}, u32[]{:S(2)}, u32[]{:S(2)}) async-start(f32[8,16,128]{2,1,0:T(8,128)} %get-tuple-element.23), calls=%async_computation.1 | async-start | bytes 131072 | tf_op jit(solution)/shard_map/all_to_all | solution.py:370
  127.0 4.7 %collective-permute-start.7 = (f32[4,256,256]{2,1,0:T(8,128)S(1)}, f32[4,256,256]{2,1,0:T(8,128)}, u32[]{:S(2)}, u32[]{:S(2)}) collective-permute-start(f32[4,256,256]{2,1,0:T(8,128)S(1)} %get-tuple-element.37), channel_id=1, source_target_pairs={{0,1},{1,0},{2,3},{3,2},{4,5},{5,4},{6,7},{7,6},{8,9},{9,8},{10,11... | collective-permute-start | bytes 3145736 | tf_op jit(solution)/shard_map/ppermute | solution.py:486
  127.1 27.4 %copy-start = (s32[1,512]{1,0:T(1,128)S(1)}, s32[1,512]{1,0:T(1,128)}, u32[]{:S(2)}) copy-start(s32[1,512]{1,0:T(1,128)} %mask_ref.3) | copy-start | bytes 6148
  127.1 23.0 %all-to-all-start.7 = ((bf16[32,32,256]{2,1,0:T(8,128)(2,1)}), bf16[32,32,256]{2,1,0:T(8,128)(2,1)S(1)}, u32[]{:S(2)}, u32[]{:S(2)}) async-start(bf16[32,32,256]{2,1,0:T(8,128)(2,1)} %get-tuple-element.34), calls=%async_computation.7 | async-start | bytes 1048576 | tf_op jit(solution)/shard_map/all_to_all | solution.py:370
  133.2 17.0 %collective-permute-start.10 = (f32[256,256]{1,0:T(8,128)S(1)}, f32[256,256]{1,0:T(8,128)S(1)}, u32[]{:S(2)}, u32[]{:S(2)}) collective-permute-start(f32[256,256]{1,0:T(8,128)S(1)} %get-tuple-element.40), channel_id=1, source_target_pairs={{0,6},{1,7},{2,0},{3,1},{4,2},{5,3},{6,4},{7,5},{8,14},{9,15},{10,... | collective-permute-start | bytes 786440 | tf_op jit(solution)/shard_map/ppermute | solution.py:487
  134.4 15.8 %collective-permute-start.8 = (f32[256,256]{1,0:T(8,128)S(1)}, f32[256,256]{1,0:T(8,128)S(1)}, u32[]{:S(2)}, u32[]{:S(2)}) collective-permute-start(f32[256,256]{1,0:T(8,128)S(1)} %get-tuple-element.42), channel_id=1, source_target_pairs={{0,2},{1,3},{2,4},{3,5},{4,6},{5,7},{6,0},{7,1},{8,10},{9,11},{10,... | collective-permute-start | bytes 786440 | tf_op jit(solution)/shard_map/ppermute | solution.py:487
  135.3 14.9 %collective-permute-start.9 = (f32[256,256]{1,0:T(8,128)S(1)}, f32[256,256]{1,0:T(8,128)S(1)}, u32[]{:S(2)}, u32[]{:S(2)}) collective-permute-start(f32[256,256]{1,0:T(8,128)S(1)} %get-tuple-element.41), channel_id=1, source_target_pairs={{0,4},{1,5},{2,6},{3,7},{4,0},{5,1},{6,2},{7,3},{8,12},{9,13},{10,... | collective-permute-start | bytes 786440 | tf_op jit(solution)/shard_map/ppermute | solution.py:487
  151.1 10.9 %all-to-all-start.8 = ((f32[8,32,256]{2,1,0:T(8,128)}), f32[8,32,256]{2,1,0:T(8,128)S(1)}, u32[]{:S(2)}, u32[]{:S(2)}) async-start(f32[8,32,256]{2,1,0:T(8,128)} %get-tuple-element.38), calls=%async_computation.8 | async-start | bytes 524288 | tf_op jit(solution)/shard_map/all_to_all | solution.py:370
where the time goes:
time: 164 us; the launch traced here: 163 us
  blocking collectives  62.6 us (38%)
  waiting for transfers between devices  38.4 us (23%)
  starting transfers between devices  33.9 us (21%)
  Pallas kernels  24.3 us (15%)
  other arithmetic  2.41 us (1%)
    all_to_all x5, blocking collectives, exchange(): return lax.all_to_all(parts, axis, 0, 0, tiled=True)  62.6 us
    all_to_all x4, waiting for transfers between devices, exchange(): return lax.all_to_all(parts, axis, 0, 0, tiled=True)  28.3 us
    pallas_call x13, Pallas kernels, call(): pl.pallas_call(kernel, out_shape=[jax.ShapeDtypeStruct(shape, dtype) for...  21.6 us
    all_to_all x4, starting transfers between devices, exchange(): return lax.all_to_all(parts, axis, 0, 0, tiled=True)  20.9 us
    ppermute x3, waiting for transfers between devices, on_device(): lines.append(lax.ppermute(pay, 'y', route))  7.76 us
    ppermute x3, starting transfers between devices, on_device(): lines.append(lax.ppermute(pay, 'y', route))  5.22 us
    ppermute x3, starting transfers between devices, on_device(): pairs_held.append(lax.ppermute(pair, 'proto', routes[-away % half]))  4.52 us
  transfers between devices with their start and end apart: 15, of which 9 were waited for; matrix products, arithmetic and copies ran while one was open for 2% of the time, Pallas kernels for 5%

commit v1 on v0

--- a/solution.py
+++ b/solution.py
@@ -110,13 +110,17 @@
 def prototypes_kernel(place_ref, *refs):
     *pair_refs, protos_ref = refs
     share = pair_refs[0].shape[1]
-    group = place_ref[0]
-    core = lax.rem(group, 2)
     for away, pair_ref in enumerate(pair_refs):
-        x = lax.rem(group // 2 + away, PROTO // 2)
+        x = lax.rem(place_ref[0] // 2 + away, PROTO // 2)
         for other in range(2):
-            start = pl.multiple_of((2 * x + (core + other) % 2) * share, share)
+            start = pl.multiple_of((other * (PROTO // 2) + x) * share, share)
             protos_ref[pl.ds(start, share), :] = pair_ref[other]
+
+
+def by_core(sums):
+    half = sums.shape[0] // 2
+    core = lax.rem(lax.axis_index("proto"), 2)
+    return jnp.where(core == 0, sums, jnp.concatenate([sums[half:], sums[:half]], axis=0))
 
 
 def in_order(y, line_refs, pay_ref, first_slot):
@@ -165,7 +169,7 @@
         top = jnp.max(scores, axis=0, keepdims=True)
         lse = top + jnp.log(jnp.sum(jnp.exp(scores - top), axis=0, keepdims=True))
         rows += [lse[:, :LANES], lse[:, LANES:]]
-    col_ref[...] = jnp.broadcast_to(jnp.concatenate(rows, axis=0)[None], col_ref.shape)
+    col_ref[...] = jnp.broadcast_to(by_core(jnp.concatenate(rows, axis=0))[None], col_ref.shape)
 
 
 def wide(packed):
@@ -198,7 +202,7 @@
 
 
 def second_kernel(teach_ref, protos_ref, col_ref, stud_row_ref, exp_ref, top_ref, row_ref, stud_out_ref):
-    col_pot = -wide(lse_over_first(col_ref[...]))
+    col_pot = -wide(by_core(lse_over_first(col_ref[...])))
     tops, totals = exps_below_top(teach_ref, protos_ref, TEACHER_SCALE, col_pot, exp_ref)
     top_ref[...] = tops
     lses = tops + jnp.log(jnp.where(totals > 0.0, totals, 1.0))
@@ -222,7 +226,7 @@
     row_pot = -lse_over_first(row_ref[...])
     factor = jnp.where(valid_ref[...] > 0.0, jnp.exp(top_ref[...] + row_pot), 0.0)
     factor_ref[...] = factor
-    col_ref[...] = jnp.broadcast_to(weighted_columns(exp_ref, factor)[None], col_ref.shape)
+    col_ref[...] = jnp.broadcast_to(by_core(weighted_columns(exp_ref, factor))[None], col_ref.shape)
 
 
 def row_scale(valid_ref, sums):
@@ -232,7 +236,7 @@
 
 def column_kernel(exp_ref, factor_ref, valid_ref, row_ref, col_ref):
     weight = row_scale(valid_ref, jnp.sum(row_ref[...], axis=0)) * factor_ref[...]
-    col_ref[...] = jnp.broadcast_to(weighted_columns(exp_ref, weight)[None], col_ref.shape)
+    col_ref[...] = jnp.broadcast_to(by_core(weighted_columns(exp_ref, weight))[None], col_ref.shape)
 
 
 def weighted_rows(exp_ref, weight):
@@ -247,7 +251,7 @@
 
 
 def row_kernel(exp_ref, factor_ref, col_ref, row_ref):
-    weight = 1.0 / jnp.sum(col_ref[...], axis=0)
+    weight = 1.0 / by_core(jnp.sum(col_ref[...], axis=0))
     sums = weighted_rows(exp_ref, weight) * factor_ref[...]
     row_ref[...] = jnp.broadcast_to(sums[None], row_ref.shape)
 
@@ -263,7 +267,7 @@
 
 
 def last_row_kernel(exp_ref, factor_ref, col_ref, stud_row_ref, row_ref):
-    weight = 1.0 / jnp.sum(col_ref[...], axis=0)
+    weight = 1.0 / by_core(jnp.sum(col_ref[...], axis=0))
     sums = weighted_rows(exp_ref, weight) * factor_ref[...]
     both = jnp.concatenate([sums, stud_row_ref[...]], axis=0)
     row_ref[...] = jnp.broadcast_to(both[None], row_ref.shape)
@@ -271,10 +275,10 @@
 
 def gradient_kernel(
     base_ref, exp_ref, factor_ref, valid_ref, col_ref, row_ref, stud_ref, protos_ref,
-    tok_ref, grad_ref, scale_ref, lse_ref, total_ref,
+    tok_ref, near_ref, far_ref, scale_ref, lse_ref, total_ref,
 ):
     tokens, width = stud_ref.shape
-    weights = 1.0 / jnp.sum(col_ref[...], axis=0)
+    weights = 1.0 / by_core(jnp.sum(col_ref[...], axis=0))
     sums = jnp.sum(row_ref[:, :8, :], axis=0)
     scale = row_scale(valid_ref, sums) * (factor_ref[...] * STUDENT_SCALE)
     lses = lse_over_first(row_ref[:, 8:, :]) - math.log(STUDENT_SCALE)
@@ -292,8 +296,13 @@
             part = scores[:, half * LANES : (half + 1) * LANES] * STUDENT_SCALE
             student = jnp.exp(part - lse_ref[...])
             target = exp_ref[:, lanes] * scale_ref[...] * weights[index : index + 1, :]
-            grad_ref[:, lanes] = (student - target).astype(BF16)
-    total_ref[:tokens, :] = dot_nn(grad_ref[...], protos_ref[...])
+            grads_ref, at = (near_ref, index) if 2 * index < weights.shape[0] else (far_ref, index - weights.shape[0] // 2)
+            grads_ref[:, at * LANES : (at + 1) * LANES] = (student - target).astype(BF16)
+    held = near_ref.shape[1]
+    total_ref[:tokens, :] = dot_nn(near_ref[...], protos_ref[:held, :]) + dot_nn(
+        far_ref[:, :held], protos_ref[held:, :]
+    )
+    far_ref[:, held:] = stud_ref[...]
     total_ref[tokens:, :] = jnp.zeros((SLOTS, width), F32)
     for device in range(tok_ref.shape[0]):
         base = base_ref[0, device]
@@ -302,16 +311,13 @@
         tok_ref[device, :, :] = rows[:SLOTS, :].astype(BF16)
 
 
-def proto_kernel(place_ref, grad_ref, stud_ref, near_ref, far_ref):
-    share = near_ref.shape[1]
-    group = place_ref[0]
+def proto_kernel(place_ref, near_ref, far_ref, stud_ref, out_ref):
+    _, share, width = out_ref.shape
+    other = far_ref[:, near_ref.shape[1] :]
     for away in range(PROTO // 2):
-        x = lax.rem(group // 2 + away, PROTO // 2)
-        core = lax.rem(group, 2)
-        start = pl.multiple_of((2 * x + 1 - core) * share, share)
-        far_ref[away, :, :] = dot_tn(grad_ref[:, pl.ds(start, share)], stud_ref[...])
-        start = pl.multiple_of((2 * x + core) * share, share)
-        near_ref[away, :, :] = dot_tn(grad_ref[:, pl.ds(start, share)], stud_ref[...])
+        start = pl.multiple_of(lax.rem(place_ref[0] // 2 + away, PROTO // 2) * share, share)
+        part = pl.ds(start, share)
+        out_ref[away, :, :] = dot_tn(near_ref[:, part], stud_ref[...]) + dot_tn(far_ref[:, part], other)
 
 
 def sum_kernel(parts_ref, near_ref, *refs):
@@ -464,9 +470,13 @@
         last_row_kernel, [((devices, 16, LANES), F32)], (exps, factor, col, stud_row)
     )
     row = exchange(row, TOK)
-    grad_slots, grads = call(
+    grad_slots, near, far = call(
         gradient_kernel,
-        [((devices, SLOTS, width), BF16), ((tokens, protos_held), BF16)],
+        [
+            ((devices, SLOTS, width), BF16),
+            ((tokens, protos_held // 2), BF16),
+            ((tokens, protos_held // 2 + width), BF16),
+        ],
         (base, exps, factor, valid, col, row, stud, protos),
         scalars=1,
         scratch=(
@@ -476,14 +486,13 @@
         ),
         cost=work,
     )
-    near, far = call(
+    (mine,) = call(
         proto_kernel,
-        [((half, share, width), F32), ((half, share, width), F32)],
-        (place, grads, stud),
+        [((half, share, width), F32)],
+        (place, near, lax.ppermute(far, "proto", swap), stud),
         scalars=1,
         cost=work,
     )
-    mine = near + lax.ppermute(far, "proto", swap)
     arrived = [lax.ppermute(mine[away], "proto", routes[away]) for away in range(1, half)]
     rows, grad_prototypes = call(
         sum_kernel,

time: 164 us -> 165 us (level)
  local copies, waits for them, and re-layouts: 0.06 us -> 3.08 us
  other arithmetic: 2.41 us -> 0.1 us
    unnamed x2 -> x10, local copies, waits for them, and re-layouts: 0.01 us -> 3.02 us
  transfers between devices with their start and end apart: 15 -> 15, of which waited for: 9 -> 9; matrix products, arithmetic and copies ran while one was open for 2% -> 0% of each run, Pallas kernels for 5% -> 6%
where the time goes in v1:
time: 165 us; the launch traced here: 164 us
  blocking collectives  62.6 us (38%)
  waiting for transfers between devices  38 us (23%)
  starting transfers between devices  33.3 us (20%)
  Pallas kernels  25 us (15%)
  local copies, waits for them, and re-layouts  3.08 us (2%)
    all_to_all x5, blocking collectives, exchange(): return lax.all_to_all(parts, axis, 0, 0, tiled=True)  62.6 us
    all_to_all x4, waiting for transfers between devices, exchange(): return lax.all_to_all(parts, axis, 0, 0, tiled=True)  26.8 us
    pallas_call x13, Pallas kernels, call(): pl.pallas_call(kernel, out_shape=[jax.ShapeDtypeStruct(shape, dtype) for...  22.3 us
    all_to_all x4, starting transfers between devices, exchange(): return lax.all_to_all(parts, axis, 0, 0, tiled=True)  20.9 us
    ppermute x3, waiting for transfers between devices, on_device(): lines.append(lax.ppermute(pay, 'y', route))  8.65 us
    ppermute x3, starting transfers between devices, on_device(): lines.append(lax.ppermute(pay, 'y', route))  4.69 us
    ppermute x3, starting transfers between devices, on_device(): pairs_held.append(lax.ppermute(pair, 'proto', routes[-away % half]))  4.52 us
  transfers between devices with their start and end apart: 15, of which 9 were waited for; matrix products, arithmetic and copies ran while one was open for 0% of the time, Pallas kernels for 6%

profile of v1, /device:TPU:32, one launch (start us, length us, event | category | flops | bytes accessed | tf_op | source)
XLA Modules:
  0.0 163.6 jit_solution(3665782371969475634)
XLA Ops:
  0.6 0.0 copy-start.4
  0.6 0.1 collective-permute-start.3
  1.4 2.7 %shard_map.69 = bf16[8,64,256]{2,1,0:T(8,128)(2,1)} custom-call(s32[1]{0:T(128)S(6)} %copy.7.count_ref, s32[1,512]{1,0:T(1,128)} %mask_ref.3, bf16[512,256]{1,0:T(8,128)(2,1)} %teacher_ref.1, bf16[512,256]{1,0:T(8,128)(2,1)} %student_ref.1), custom_call_target="tpu_custom_call" | custom-call | tf_op jit(solution)/shard_map/pallas_call | solution.py:394
  4.1 8.6 %all-to-all-start = ((bf16[8,64,256]{2,1,0:T(8,128)(2,1)}), bf16[8,64,256]{2,1,0:T(8,128)(2,1)S(1)}, u32[]{:S(2)}, u32[]{:S(2)}) async-start(bf16[8,64,256]{2,1,0:T(8,128)(2,1)} %shard_map.69), calls=%async_computation | async-start | bytes 524288 | tf_op jit(solution)/shard_map/all_to_all | solution.py:376
  12.7 0.0 collective-permute-done.3
  12.7 0.0 copy-done.4
  12.8 2.8 %collective-permute-start.4 = (bf16[2,256,256]{2,1,0:T(8,128)(2,1)S(1)}, bf16[2,256,256]{2,1,0:T(8,128)(2,1)S(1)}, u32[]{:S(2)}, u32[]{:S(2)}) collective-permute-start(bf16[2,256,256]{2,1,0:T(8,128)(2,1)S(1)} %pad_maximum_fusion.refs_0_), channel_id=1, source_target_pairs={{0,6},{1,7},{2,0},{3,1},{4,2},{5,3},{6,4},{7,5},{8,14},{9,15},{10,... | collective-permute-start | bytes 786440 | tf_op jit(solution)/shard_map/ppermute | solution.py:417
  15.6 0.8 collective-permute-start.5
  16.4 0.9 collective-permute-start.6
  17.3 6.5 %all-to-all-done.refs_1_ = bf16[8,64,256]{2,1,0:T(8,128)(2,1)S(1)} async-done(((bf16[8,64,256]{2,1,0:T(8,128)(2,1)}), bf16[8,64,256]{2,1,0:T(8,128)(2,1)S(1)}, u32[]{:S(2)}, u32[]{:S(2)}) %all-to-all-start) | async-done | bytes 262176 | tf_op jit(solution)/shard_map/all_to_all | solution.py:376
  23.8 3.0 %collective-permute-start = (bf16[8,64,256]{2,1,0:T(8,128)(2,1)S(1)}, bf16[8,64,256]{2,1,0:T(8,128)(2,1)S(1)}, u32[]{:S(2)}, u32[]{:S(2)}) collective-permute-start(bf16[8,64,256]{2,1,0:T(8,128)(2,1)S(1)} %all-to-all-done.refs_1_), channel_id=1, source_target_pairs={{0,192},{64,0},{128,64},{192,128},{1,193},{65,1},{129,65},{193,129... | collective-permute-start | bytes 786440 | tf_op jit(solution)/shard_map/ppermute | solution.py:413
  26.8 0.6 collective-permute-start.1
  27.5 0.0 collective-permute-done.4.refs_1_
  27.5 1.0 collective-permute-start.2
  28.5 0.1 pad_add_fusion.place_ref.refs_0_
  28.6 0.0 collective-permute-done.5.refs_2_
  28.6 2.0 %collective-permute-done.6.refs_3_ = bf16[2,256,256]{2,1,0:T(8,128)(2,1)S(1)} collective-permute-done((bf16[2,256,256]{2,1,0:T(8,128)(2,1)S(1)}, bf16[2,256,256]{2,1,0:T(8,128)(2,1)S(1)}, u32[]{:S(2)}, u32[]{:S(2)}) %collective-permute-start.6) | collective-permute-done | bytes 262176 | tf_op jit(solution)/shard_map/ppermute | solution.py:417
  30.6 0.6 shard_map.70.refs_5_.refs_6_.protos_ref
  31.2 5.0 %collective-permute-done.refs_2_ = bf16[8,64,256]{2,1,0:T(8,128)(2,1)S(1)} collective-permute-done((bf16[8,64,256]{2,1,0:T(8,128)(2,1)S(1)}, bf16[8,64,256]{2,1,0:T(8,128)(2,1)S(1)}, u32[]{:S(2)}, u32[]{:S(2)}) %collective-permute-start) | collective-permute-done | bytes 262176 | tf_op jit(solution)/shard_map/ppermute | solution.py:413
  36.2 1.0 collective-permute-done.1.refs_3_
  37.2 2.7 %collective-permute-done.2.refs_4_ = bf16[8,64,256]{2,1,0:T(8,128)(2,1)S(1)} collective-permute-done((bf16[8,64,256]{2,1,0:T(8,128)(2,1)S(1)}, bf16[8,64,256]{2,1,0:T(8,128)(2,1)S(1)}, u32[]{:S(2)}, u32[]{:S(2)}) %collective-permute-start.2) | collective-permute-done | bytes 262176 | tf_op jit(solution)/shard_map/ppermute | solution.py:413
  39.9 3.7 %shard_map.71 = (bf16[528,256]{1,0:T(8,128)(2,1)S(1)}, f32[8,1024]{1,0:T(8,128)S(1)}, f32[8,128]{1,0:T(8,128)S(1)}, s32[8,128]{1,0:T(8,128)S(1)}, f32[8,16,128]{2,1,0:T(8,128)}) custom-call(s32[3]{0:T(128)S(1)} %pad_add_fusion.place_ref.refs_0_, bf16[8,64,256]{2,1,0:T(8,128)(2,1)S(1)} %all-to-all-done.refs_1_, ...), custom_call_target="tpu_custom_call" | custom-call | flops 553648128 | bytes 8650752 | tf_op jit(solution)/shard_map/pallas_call | solution.py:359
  43.6 4.3 %all-to-all-start.1 = ((f32[8,16,128]{2,1,0:T(8,128)}), f32[8,16,128]{2,1,0:T(8,128)S(1)}, u32[]{:S(2)}, u32[]{:S(2)}) async-start(f32[8,16,128]{2,1,0:T(8,128)} %get-tuple-element.22), calls=%async_computation.1 | async-start | bytes 131072 | tf_op jit(solution)/shard_map/all_to_all | solution.py:376
  47.9 3.2 %shard_map.72 = (bf16[528,256]{1,0:T(8,128)(2,1)S(1)}, f32[8,128]{1,0:T(8,128)S(1)}) custom-call(s32[3]{0:T(128)S(1)} %pad_add_fusion.place_ref.refs_0_, bf16[8,64,256]{2,1,0:T(8,128)(2,1)S(1)} %all-to-all-done.refs_1_, bf16[8,64,256]{2,1,0:T(8,128)(2,1)S(1)} %collective-permute-done.refs_2_, bf16[8,64,256]{2,1,0:T(8,128)(2,1)S(1)} %collective-permute-done.1.refs_3_, ...), custom_call_target="tpu_custom_call" | custom-call | flops 553648128 | bytes 8650752 | tf_op jit(solution)/shard_map/pallas_call | solution.py:359
  51.1 2.4 %all-to-all-done.1.col_ref = f32[8,16,128]{2,1,0:T(8,128)S(1)} async-done(((f32[8,16,128]{2,1,0:T(8,128)}), f32[8,16,128]{2,1,0:T(8,128)S(1)}, u32[]{:S(2)}, u32[]{:S(2)}) %all-to-all-start.1) | async-done | bytes 65568 | tf_op jit(solution)/shard_map/all_to_all | solution.py:376
  53.5 2.0 %shard_map.73 = (f32[528,2048]{1,0:T(8,128)S(1)}, f32[8,128]{1,0:T(8,128)S(1)}, f32[32,8,128]{2,1,0:T(8,128)S(1)}, f32[8,128]{1,0:T(8,128)S(1)}) custom-call(bf16[528,256]{1,0:T(8,128)(2,1)S(1)} %get-tuple-element.21.teach_ref, bf16[2048,256]{1,0:T(8,128)(2,1)S(1)} %shard_map.70.refs_5_.refs_6_.protos_ref, f32[8,16,128]{2,1,0:T(8,128)S(1)} %all-to-all-done.1.col_ref, ...), custom_call_target="tpu_custom_call" | custom-call | flops 553648128 | bytes 8650752 | tf_op jit(solution)/shard_map/pallas_call | solution.py:359
  55.6 16.1 %all_to_all.45.row_ref = f32[32,8,128]{2,1,0:T(8,128)S(1)} all-to-all(f32[32,8,128]{2,1,0:T(8,128)S(1)} %get-tuple-element.28), channel_id=1, replica_groups=mesh['y'=4,'z'=8,'proto'=8] {'y','z'}, dimensions={0} | all-to-all | bytes 262144 | tf_op jit(solution)/shard_map/all_to_all | solution.py:376
  71.7 0.8 shard_map.74
  72.5 8.3 %all_to_all.46.col_ref = f32[8,16,128]{2,1,0:T(8,128)S(1)} all-to-all(f32[8,16,128]{2,1,0:T(8,128)S(1)} %get-tuple-element.30), channel_id=1, replica_groups=mesh['y'=4,'z'=8,'proto'=8] {'proto'}, dimensions={0} | all-to-all | bytes 131072 | tf_op jit(solution)/shard_map/all_to_all | solution.py:376
  80.8 0.7 shard_map.75
  81.5 13.8 %all_to_all.47.row_ref = f32[32,8,128]{2,1,0:T(8,128)S(1)} all-to-all(f32[32,8,128]{2,1,0:T(8,128)S(1)} %shard_map.75), channel_id=1, replica_groups=mesh['y'=4,'z'=8,'proto'=8] {'y','z'}, dimensions={0} | all-to-all | bytes 262144 | tf_op jit(solution)/shard_map/all_to_all | solution.py:376
  95.4 0.8 shard_map.76
  96.2 8.0 %all_to_all.48.col_ref = f32[8,16,128]{2,1,0:T(8,128)S(1)} all-to-all(f32[8,16,128]{2,1,0:T(8,128)S(1)} %shard_map.76), channel_id=1, replica_groups=mesh['y'=4,'z'=8,'proto'=8] {'proto'}, dimensions={0} | all-to-all | bytes 131072 | tf_op jit(solution)/shard_map/all_to_all | solution.py:376
  104.2 0.7 shard_map.77
  104.9 16.3 %all_to_all.49.row_ref = f32[32,16,128]{2,1,0:T(8,128)S(1)} all-to-all(f32[32,16,128]{2,1,0:T(8,128)S(1)} %shard_map.77), channel_id=1, replica_groups=mesh['y'=4,'z'=8,'proto'=8] {'y','z'}, dimensions={0} | all-to-all | bytes 524288 | tf_op jit(solution)/shard_map/all_to_all | solution.py:376
  121.2 5.0 %shard_map.78 = (bf16[32,32,256]{2,1,0:T(8,128)(2,1)S(1)}, bf16[528,1024]{1,0:T(8,128)(2,1)S(1)}, bf16[528,1280]{1,0:T(8,128)(2,1)}) custom-call(s32[8,128]{1,0:T(8,128)S(1)} %get-tuple-element.20.base_ref, f32[528,2048]{1,0:T(8,128)S(1)} %get-tuple-element.25.exp_ref, f32[8,128]{1,0:T(8,128)S(1)} %get-tuple-element.29.factor_ref, ...), custom_call_target="tpu_custom_call" | custom-call | flops 553648128 | bytes 8650752 | tf_op jit(solution)/shard_map/pallas_call | solution.py:359
  126.2 0.0 copy-start
  126.2 1.0 copy-done
  127.1 0.0 copy-start.2
  127.2 0.0 collective-permute-start.7
  127.2 0.8 copy-done.2
  127.9 4.6 %all-to-all-start.7 = ((bf16[32,32,256]{2,1,0:T(8,128)(2,1)}), bf16[32,32,256]{2,1,0:T(8,128)(2,1)S(1)}, u32[]{:S(2)}, u32[]{:S(2)}) async-start(bf16[32,32,256]{2,1,0:T(8,128)(2,1)} %copy-done.2), calls=%async_computation.7 | async-start | bytes 1048576 | tf_op jit(solution)/shard_map/all_to_all | solution.py:376
  132.5 0.0 collective-permute-done.7.far_ref
  132.5 0.0 copy-start.1
  132.5 1.2 copy-done.1
  133.8 1.6 shard_map.79.near_ref
  135.4 0.1 slice_bitcast_fusion
  135.4 1.2 collective-permute-start.10
  136.7 0.9 collective-permute-start.8
  137.5 0.0 copy-start.3
  137.5 1.0 collective-permute-start.9
  138.5 11.5 %all-to-all-done.7.parts_ref = bf16[32,32,256]{2,1,0:T(8,128)(2,1)S(1)} async-done(((bf16[32,32,256]{2,1,0:T(8,128)(2,1)}), bf16[32,32,256]{2,1,0:T(8,128)(2,1)S(1)}, u32[]{:S(2)}, u32[]{:S(2)}) %all-to-all-start.7) | async-done | bytes 524320 | tf_op jit(solution)/shard_map/all_to_all | solution.py:376
  150.0 0.0 collective-permute-done.10.refs_2_
  150.0 0.6 collective-permute-done.8.refs_0_
  150.6 0.0 collective-permute-done.9.refs_1_
  150.6 0.9 shard_map.80
  151.5 3.4 %all-to-all-start.8 = ((f32[8,32,256]{2,1,0:T(8,128)}), f32[8,32,256]{2,1,0:T(8,128)S(1)}, u32[]{:S(2)}, u32[]{:S(2)}) async-start(f32[8,32,256]{2,1,0:T(8,128)} %get-tuple-element.36), calls=%async_computation.8 | async-start | bytes 524288 | tf_op jit(solution)/shard_map/all_to_all | solution.py:376
  154.9 0.0 copy-done.3
  154.9 1.0 shard_map.68.onehot_ref
  156.0 6.4 %all-to-all-done.8.rows_ref = f32[8,32,256]{2,1,0:T(8,128)S(1)} async-done(((f32[8,32,256]{2,1,0:T(8,128)}), f32[8,32,256]{2,1,0:T(8,128)S(1)}, u32[]{:S(2)}, u32[]{:S(2)}) %all-to-all-start.8) | async-done | bytes 262176 | tf_op jit(solution)/shard_map/all_to_all | solution.py:376
  162.4 1.2 shard_map.81
  (1 shorter events, 0.0 us)
Async XLA Ops:
  0.6 12.1 %copy-start.4 = (bf16[256,256]{1,0:T(8,128)(2,1)S(1)}, bf16[256,256]{1,0:T(8,128)(2,1)}, u32[]{:S(2)}) copy-start(bf16[256,256]{1,0:T(8,128)(2,1)} %param.7) | copy-start | bytes 393220
  0.6 12.1 %collective-permute-start.3 = (bf16[256,256]{1,0:T(8,128)(2,1)}, bf16[256,256]{1,0:T(8,128)(2,1)S(1)}, u32[]{:S(2)}, u32[]{:S(2)}) collective-permute-start(bf16[256,256]{1,0:T(8,128)(2,1)} %param.7), channel_id=1, source_target_pairs={{0,1},{1,0},{2,3},{3,2},{4,5},{5,4},{6,7},{7,6},{8,9},{9,8},{10,11... | collective-permute-start | bytes 393224 | tf_op jit(solution)/shard_map/ppermute | solution.py:414
  4.1 19.7 %all-to-all-start = ((bf16[8,64,256]{2,1,0:T(8,128)(2,1)}), bf16[8,64,256]{2,1,0:T(8,128)(2,1)S(1)}, u32[]{:S(2)}, u32[]{:S(2)}) async-start(bf16[8,64,256]{2,1,0:T(8,128)(2,1)} %shard_map.69), calls=%async_computation | async-start | bytes 524288 | tf_op jit(solution)/shard_map/all_to_all | solution.py:376
  12.8 14.7 %collective-permute-start.4 = (bf16[2,256,256]{2,1,0:T(8,128)(2,1)S(1)}, bf16[2,256,256]{2,1,0:T(8,128)(2,1)S(1)}, u32[]{:S(2)}, u32[]{:S(2)}) collective-permute-start(bf16[2,256,256]{2,1,0:T(8,128)(2,1)S(1)} %pad_maximum_fusion.refs_0_), channel_id=1, source_target_pairs={{0,6},{1,7},{2,0},{3,1},{4,2},{5,3},{6,4},{7,5},{8,14},{9,15},{10,... | collective-permute-start | bytes 786440 | tf_op jit(solution)/shard_map/ppermute | solution.py:417
  15.6 13.0 %collective-permute-start.5 = (bf16[2,256,256]{2,1,0:T(8,128)(2,1)S(1)}, bf16[2,256,256]{2,1,0:T(8,128)(2,1)S(1)}, u32[]{:S(2)}, u32[]{:S(2)}) collective-permute-start(bf16[2,256,256]{2,1,0:T(8,128)(2,1)S(1)} %pad_maximum_fusion.refs_0_), channel_id=1, source_target_pairs={{0,4},{1,5},{2,6},{3,7},{4,0},{5,1},{6,2},{7,3},{8,12},{9,13},{10,... | collective-permute-start | bytes 786440 | tf_op jit(solution)/shard_map/ppermute | solution.py:417
  16.4 14.2 %collective-permute-start.6 = (bf16[2,256,256]{2,1,0:T(8,128)(2,1)S(1)}, bf16[2,256,256]{2,1,0:T(8,128)(2,1)S(1)}, u32[]{:S(2)}, u32[]{:S(2)}) collective-permute-start(bf16[2,256,256]{2,1,0:T(8,128)(2,1)S(1)} %pad_maximum_fusion.refs_0_), channel_id=1, source_target_pairs={{0,2},{1,3},{2,4},{3,5},{4,6},{5,7},{6,0},{7,1},{8,10},{9,11},{10,... | collective-permute-start | bytes 786440 | tf_op jit(solution)/shard_map/ppermute | solution.py:417
  23.8 12.4 %collective-permute-start = (bf16[8,64,256]{2,1,0:T(8,128)(2,1)S(1)}, bf16[8,64,256]{2,1,0:T(8,128)(2,1)S(1)}, u32[]{:S(2)}, u32[]{:S(2)}) collective-permute-start(bf16[8,64,256]{2,1,0:T(8,128)(2,1)S(1)} %all-to-all-done.refs_1_), channel_id=1, source_target_pairs={{0,192},{64,0},{128,64},{192,128},{1,193},{65,1},{129,65},{193,129... | collective-permute-start | bytes 786440 | tf_op jit(solution)/shard_map/ppermute | solution.py:413
  26.8 10.3 %collective-permute-start.1 = (bf16[8,64,256]{2,1,0:T(8,128)(2,1)S(1)}, bf16[8,64,256]{2,1,0:T(8,128)(2,1)S(1)}, u32[]{:S(2)}, u32[]{:S(2)}) collective-permute-start(bf16[8,64,256]{2,1,0:T(8,128)(2,1)S(1)} %all-to-all-done.refs_1_), channel_id=1, source_target_pairs={{0,128},{64,192},{128,0},{192,64},{1,129},{65,193},{129,1},{193,65... | collective-permute-start | bytes 786440 | tf_op jit(solution)/shard_map/ppermute | solution.py:413
  27.5 12.4 %collective-permute-start.2 = (bf16[8,64,256]{2,1,0:T(8,128)(2,1)S(1)}, bf16[8,64,256]{2,1,0:T(8,128)(2,1)S(1)}, u32[]{:S(2)}, u32[]{:S(2)}) collective-permute-start(bf16[8,64,256]{2,1,0:T(8,128)(2,1)S(1)} %all-to-all-done.refs_1_), channel_id=1, source_target_pairs={{0,64},{64,128},{128,192},{192,0},{1,65},{65,129},{129,193},{193,1... | collective-permute-start | bytes 786440 | tf_op jit(solution)/shard_map/ppermute | solution.py:413
  43.6 9.9 %all-to-all-start.1 = ((f32[8,16,128]{2,1,0:T(8,128)}), f32[8,16,128]{2,1,0:T(8,128)S(1)}, u32[]{:S(2)}, u32[]{:S(2)}) async-start(f32[8,16,128]{2,1,0:T(8,128)} %get-tuple-element.22), calls=%async_computation.1 | async-start | bytes 131072 | tf_op jit(solution)/shard_map/all_to_all | solution.py:376
  126.2 1.0 copy-start
  127.1 0.8 copy-start.2
  127.2 5.4 %collective-permute-start.7 = (bf16[528,1280]{1,0:T(8,128)(2,1)}, bf16[528,1280]{1,0:T(8,128)(2,1)S(1)}, u32[]{:S(2)}, u32[]{:S(2)}) collective-permute-start(bf16[528,1280]{1,0:T(8,128)(2,1)} %get-tuple-element.35), channel_id=1, source_target_pairs={{0,1},{1,0},{2,3},{3,2},{4,5},{5,4},{6,7},{7,6},{8,9},{9,8},{10,11... | collective-permute-start | bytes 4055048 | tf_op jit(solution)/shard_map/ppermute | solution.py:492
  127.9 22.1 %all-to-all-start.7 = ((bf16[32,32,256]{2,1,0:T(8,128)(2,1)}), bf16[32,32,256]{2,1,0:T(8,128)(2,1)S(1)}, u32[]{:S(2)}, u32[]{:S(2)}) async-start(bf16[32,32,256]{2,1,0:T(8,128)(2,1)} %copy-done.2), calls=%async_computation.7 | async-start | bytes 1048576 | tf_op jit(solution)/shard_map/all_to_all | solution.py:376
  132.5 1.2 copy-start.1
  135.4 14.6 %collective-permute-start.10 = (f32[256,256]{1,0:T(8,128)S(1)}, f32[256,256]{1,0:T(8,128)S(1)}, u32[]{:S(2)}, u32[]{:S(2)}) collective-permute-start(f32[256,256]{1,0:T(8,128)S(1)} %get-tuple-element.38), channel_id=1, source_target_pairs={{0,6},{1,7},{2,0},{3,1},{4,2},{5,3},{6,4},{7,5},{8,14},{9,15},{10,... | collective-permute-start | bytes 786440 | tf_op jit(solution)/shard_map/ppermute | solution.py:496
  136.7 13.9 %collective-permute-start.8 = (f32[256,256]{1,0:T(8,128)S(1)}, f32[256,256]{1,0:T(8,128)S(1)}, u32[]{:S(2)}, u32[]{:S(2)}) collective-permute-start(f32[256,256]{1,0:T(8,128)S(1)} %get-tuple-element.40), channel_id=1, source_target_pairs={{0,2},{1,3},{2,4},{3,5},{4,6},{5,7},{6,0},{7,1},{8,10},{9,11},{10,... | collective-permute-start | bytes 786440 | tf_op jit(solution)/shard_map/ppermute | solution.py:496
  137.5 17.4 %copy-start.3 = (s32[1,512]{1,0:T(1,128)S(1)}, s32[1,512]{1,0:T(1,128)}, u32[]{:S(2)}) copy-start(s32[1,512]{1,0:T(1,128)} %mask_ref.3) | copy-start | bytes 6148
  137.5 13.1 %collective-permute-start.9 = (f32[256,256]{1,0:T(8,128)S(1)}, f32[256,256]{1,0:T(8,128)S(1)}, u32[]{:S(2)}, u32[]{:S(2)}) collective-permute-start(f32[256,256]{1,0:T(8,128)S(1)} %get-tuple-element.39), channel_id=1, source_target_pairs={{0,4},{1,5},{2,6},{3,7},{4,0},{5,1},{6,2},{7,3},{8,12},{9,13},{10,... | collective-permute-start | bytes 786440 | tf_op jit(solution)/shard_map/ppermute | solution.py:496
  151.5 10.9 %all-to-all-start.8 = ((f32[8,32,256]{2,1,0:T(8,128)}), f32[8,32,256]{2,1,0:T(8,128)S(1)}, u32[]{:S(2)}, u32[]{:S(2)}) async-start(f32[8,32,256]{2,1,0:T(8,128)} %get-tuple-element.36), calls=%async_computation.8 | async-start | bytes 524288 | tf_op jit(solution)/shard_map/all_to_all | solution.py:376

commit v2 on v0

--- a/solution.py
+++ b/solution.py
@@ -14,6 +14,7 @@
 SLOTS = CAP // PROTO
 ROWS = 4
 TOK = ("y", "z")
+USED = 5
 LANES = 128
 TEACHER_SCALE = 1.0 / 0.07
 STUDENT_SCALE = 1.0 / 0.1
@@ -246,10 +247,12 @@
     return sums
 
 
-def row_kernel(exp_ref, factor_ref, col_ref, row_ref):
+def row_kernel(first, exp_ref, factor_ref, col_ref, stud_row_ref, row_ref):
     weight = 1.0 / jnp.sum(col_ref[...], axis=0)
     sums = weighted_rows(exp_ref, weight) * factor_ref[...]
-    row_ref[...] = jnp.broadcast_to(sums[None], row_ref.shape)
+    free = 8 - USED
+    both = jnp.concatenate([sums[:USED], stud_row_ref[first : first + free, :]], axis=0)
+    row_ref[...] = jnp.broadcast_to(both[None], row_ref.shape)
 
 
 def student_kernel(*refs):
@@ -262,22 +265,17 @@
     row_ref[...] = tops + jnp.log(jnp.where(totals > 0.0, totals, 1.0))
 
 
-def last_row_kernel(exp_ref, factor_ref, col_ref, stud_row_ref, row_ref):
-    weight = 1.0 / jnp.sum(col_ref[...], axis=0)
-    sums = weighted_rows(exp_ref, weight) * factor_ref[...]
-    both = jnp.concatenate([sums, stud_row_ref[...]], axis=0)
-    row_ref[...] = jnp.broadcast_to(both[None], row_ref.shape)
-
-
 def gradient_kernel(
-    base_ref, exp_ref, factor_ref, valid_ref, col_ref, row_ref, stud_ref, protos_ref,
-    tok_ref, grad_ref, scale_ref, lse_ref, total_ref,
+    base_ref, exp_ref, factor_ref, valid_ref, col_ref, early_ref, row_ref, stud_ref, protos_ref,
+    tok_ref, grad_ref, score_ref, scale_ref, lse_ref, total_ref,
 ):
     tokens, width = stud_ref.shape
     weights = 1.0 / jnp.sum(col_ref[...], axis=0)
-    sums = jnp.sum(row_ref[:, :8, :], axis=0)
+    sums = jnp.sum(row_ref[...], axis=0)
     scale = row_scale(valid_ref, sums) * (factor_ref[...] * STUDENT_SCALE)
-    lses = lse_over_first(row_ref[:, 8:, :]) - math.log(STUDENT_SCALE)
+    early, late = lse_over_first(early_ref[...]), lse_over_first(row_ref[...])
+    lses = jnp.concatenate([early[USED:], late[USED:], jnp.zeros((2, LANES), F32)], axis=0)
+    lses = lses - math.log(STUDENT_SCALE)
     lses = jnp.where(valid_ref[...] > 0.0, lses, -FAR_BELOW)
     for block, rows in blocks(tokens):
         size = rows.stop - rows.start
@@ -285,14 +283,16 @@
         lse_ref[rows, :] = column(lses, block, size)
     step = 2 * LANES
     for chunk in range(protos_ref.shape[0] // step):
-        scores = dot_nt(stud_ref[...], protos_ref[chunk * step : (chunk + 1) * step, :])
+        slot = chunk % 2
+        score_ref[slot] = dot_nt(stud_ref[...], protos_ref[chunk * step : (chunk + 1) * step, :])
         for half in range(2):
             index = 2 * chunk + half
             lanes = slice(index * LANES, (index + 1) * LANES)
-            part = scores[:, half * LANES : (half + 1) * LANES] * STUDENT_SCALE
-            student = jnp.exp(part - lse_ref[...])
-            target = exp_ref[:, lanes] * scale_ref[...] * weights[index : index + 1, :]
-            grad_ref[:, lanes] = (student - target).astype(BF16)
+            for _, rows in blocks(tokens):
+                part = score_ref[slot, rows, half * LANES : (half + 1) * LANES] * STUDENT_SCALE
+                student = jnp.exp(part - lse_ref[rows, :])
+                target = exp_ref[rows, lanes] * scale_ref[rows, :] * weights[index : index + 1, :]
+                grad_ref[rows, lanes] = (student - target).astype(BF16)
     total_ref[:tokens, :] = dot_nn(grad_ref[...], protos_ref[...])
     total_ref[tokens:, :] = jnp.zeros((SLOTS, width), F32)
     for device in range(tok_ref.shape[0]):
@@ -456,20 +456,22 @@
     row = exchange(row, TOK)
     factor, col = call(third_kernel, [packed, col_out], (exps, top, valid, row))
     col = exchange(col, "proto")
-    (row,) = call(row_kernel, [row_out], (exps, factor, col))
+    (row,) = call(functools.partial(row_kernel, 0), [row_out], (exps, factor, col, stud_row))
     row = exchange(row, TOK)
+    early = row
     (col,) = call(column_kernel, [col_out], (exps, factor, valid, row))
     col = exchange(col, "proto")
     (row,) = call(
-        last_row_kernel, [((devices, 16, LANES), F32)], (exps, factor, col, stud_row)
+        functools.partial(row_kernel, 8 - USED), [row_out], (exps, factor, col, stud_row)
     )
     row = exchange(row, TOK)
     grad_slots, grads = call(
         gradient_kernel,
         [((devices, SLOTS, width), BF16), ((tokens, protos_held), BF16)],
-        (base, exps, factor, valid, col, row, stud, protos),
+        (base, exps, factor, valid, col, early, row, stud, protos),
         scalars=1,
         scratch=(
+            pltpu.VMEM((2, tokens, 2 * LANES), F32),
             pltpu.VMEM((tokens, LANES), F32),
             pltpu.VMEM((tokens, LANES), F32),
             pltpu.VMEM((tokens + SLOTS, width), F32),

time: 164 us -> 162 us (0.988)
  blocking collectives: 62.6 us -> 60.1 us
    all_to_all x5, blocking collectives: 62.6 us -> 60.1 us  [exchange(): return lax.all_to_all(parts, axis, 0, 0, tiled=True)]
where the time goes in v2:
time: 162 us; the launch traced here: 161 us
  blocking collectives  60.1 us (37%)
  waiting for transfers between devices  38.6 us (24%)
  starting transfers between devices  33.7 us (21%)
  Pallas kernels  24.3 us (15%)
  other arithmetic  2.41 us (1%)
    all_to_all x5, blocking collectives, exchange(): return lax.all_to_all(parts, axis, 0, 0, tiled=True)  60.1 us
    all_to_all x4, waiting for transfers between devices, exchange(): return lax.all_to_all(parts, axis, 0, 0, tiled=True)  28.4 us
    pallas_call x13, Pallas kernels, call(): pl.pallas_call(kernel, out_shape=[jax.ShapeDtypeStruct(shape, dtype) for...  21.6 us
    all_to_all x4, starting transfers between devices, exchange(): return lax.all_to_all(parts, axis, 0, 0, tiled=True)  20.6 us
    ppermute x3, waiting for transfers between devices, on_device(): lines.append(lax.ppermute(pay, 'y', route))  7.76 us
    ppermute x3, starting transfers between devices, on_device(): lines.append(lax.ppermute(pay, 'y', route))  5.22 us
    ppermute x3, starting transfers between devices, on_device(): pairs_held.append(lax.ppermute(pair, 'proto', routes[-away % half]))  4.52 us
  transfers between devices with their start and end apart: 15, of which 9 were waited for; matrix products, arithmetic and copies ran while one was open for 2% of the time, Pallas kernels for 5%

profile of v2, /device:TPU:32, one launch (start us, length us, event | category | flops | bytes accessed | tf_op | source)
XLA Modules:
  0.0 160.6 jit_solution(1190572014903185998)
XLA Ops:
  0.6 0.1 collective-permute-start.3
  1.4 2.7 %shard_map.69 = bf16[8,64,256]{2,1,0:T(8,128)(2,1)} custom-call(s32[1]{0:T(128)S(6)} %copy.7.count_ref, s32[1,512]{1,0:T(1,128)} %mask_ref.3, bf16[512,256]{1,0:T(8,128)(2,1)} %teacher_ref.1, bf16[512,256]{1,0:T(8,128)(2,1)} %student_ref.1), custom_call_target="tpu_custom_call" | custom-call | tf_op jit(solution)/shard_map/pallas_call | solution.py:388
  4.1 8.6 %all-to-all-start = ((bf16[8,64,256]{2,1,0:T(8,128)(2,1)}), bf16[8,64,256]{2,1,0:T(8,128)(2,1)S(1)}, u32[]{:S(2)}, u32[]{:S(2)}) async-start(bf16[8,64,256]{2,1,0:T(8,128)(2,1)} %shard_map.69), calls=%async_computation | async-start | bytes 524288 | tf_op jit(solution)/shard_map/all_to_all | solution.py:370
  12.7 0.0 collective-permute-done.3
  12.7 0.9 pad_maximum_fusion.refs_0_
  13.6 2.8 %collective-permute-start.4 = (bf16[2,256,256]{2,1,0:T(8,128)(2,1)S(1)}, bf16[2,256,256]{2,1,0:T(8,128)(2,1)S(1)}, u32[]{:S(2)}, u32[]{:S(2)}) collective-permute-start(bf16[2,256,256]{2,1,0:T(8,128)(2,1)S(1)} %pad_maximum_fusion.refs_0_), channel_id=1, source_target_pairs={{0,6},{1,7},{2,0},{3,1},{4,2},{5,3},{6,4},{7,5},{8,14},{9,15},{10,... | collective-permute-start | bytes 786440 | tf_op jit(solution)/shard_map/ppermute | solution.py:411
  16.5 0.8 collective-permute-start.5
  17.3 0.9 collective-permute-start.6
  18.2 5.6 %all-to-all-done.refs_1_ = bf16[8,64,256]{2,1,0:T(8,128)(2,1)S(1)} async-done(((bf16[8,64,256]{2,1,0:T(8,128)(2,1)}), bf16[8,64,256]{2,1,0:T(8,128)(2,1)S(1)}, u32[]{:S(2)}, u32[]{:S(2)}) %all-to-all-start) | async-done | bytes 262176 | tf_op jit(solution)/shard_map/all_to_all | solution.py:370
  23.8 3.0 %collective-permute-start = (bf16[8,64,256]{2,1,0:T(8,128)(2,1)S(1)}, bf16[8,64,256]{2,1,0:T(8,128)(2,1)S(1)}, u32[]{:S(2)}, u32[]{:S(2)}) collective-permute-start(bf16[8,64,256]{2,1,0:T(8,128)(2,1)S(1)} %all-to-all-done.refs_1_), channel_id=1, source_target_pairs={{0,192},{64,0},{128,64},{192,128},{1,193},{65,1},{129,65},{193,129... | collective-permute-start | bytes 786440 | tf_op jit(solution)/shard_map/ppermute | solution.py:407
  26.8 0.6 collective-permute-start.1
  27.4 0.4 collective-permute-done.4.refs_1_
  27.8 1.6 collective-permute-start.2
  29.4 0.1 pad_add_fusion.place_ref.refs_0_
  29.5 0.0 collective-permute-done.5.refs_2_
  29.5 2.0 %collective-permute-done.6.refs_3_ = bf16[2,256,256]{2,1,0:T(8,128)(2,1)S(1)} collective-permute-done((bf16[2,256,256]{2,1,0:T(8,128)(2,1)S(1)}, bf16[2,256,256]{2,1,0:T(8,128)(2,1)S(1)}, u32[]{:S(2)}, u32[]{:S(2)}) %collective-permute-start.6) | collective-permute-done | bytes 262176 | tf_op jit(solution)/shard_map/ppermute | solution.py:411
  31.5 0.6 shard_map.70.refs_5_.refs_6_.protos_ref
  32.1 4.1 %collective-permute-done.refs_2_ = bf16[8,64,256]{2,1,0:T(8,128)(2,1)S(1)} collective-permute-done((bf16[8,64,256]{2,1,0:T(8,128)(2,1)S(1)}, bf16[8,64,256]{2,1,0:T(8,128)(2,1)S(1)}, u32[]{:S(2)}, u32[]{:S(2)}) %collective-permute-start) | collective-permute-done | bytes 262176 | tf_op jit(solution)/shard_map/ppermute | solution.py:407
  36.2 1.0 collective-permute-done.1.refs_3_
  37.2 2.7 %collective-permute-done.2.refs_4_ = bf16[8,64,256]{2,1,0:T(8,128)(2,1)S(1)} collective-permute-done((bf16[8,64,256]{2,1,0:T(8,128)(2,1)S(1)}, bf16[8,64,256]{2,1,0:T(8,128)(2,1)S(1)}, u32[]{:S(2)}, u32[]{:S(2)}) %collective-permute-start.2) | collective-permute-done | bytes 262176 | tf_op jit(solution)/shard_map/ppermute | solution.py:407
  39.9 3.7 %shard_map.71 = (bf16[528,256]{1,0:T(8,128)(2,1)S(1)}, f32[8,1024]{1,0:T(8,128)S(1)}, f32[8,128]{1,0:T(8,128)S(1)}, s32[8,128]{1,0:T(8,128)S(1)}, f32[8,16,128]{2,1,0:T(8,128)}) custom-call(s32[3]{0:T(128)S(1)} %pad_add_fusion.place_ref.refs_0_, bf16[8,64,256]{2,1,0:T(8,128)(2,1)S(1)} %all-to-all-done.refs_1_, ...), custom_call_target="tpu_custom_call" | custom-call | flops 553648128 | bytes 8650752 | tf_op jit(solution)/shard_map/pallas_call | solution.py:353
  43.6 4.3 %all-to-all-start.1 = ((f32[8,16,128]{2,1,0:T(8,128)}), f32[8,16,128]{2,1,0:T(8,128)S(1)}, u32[]{:S(2)}, u32[]{:S(2)}) async-start(f32[8,16,128]{2,1,0:T(8,128)} %get-tuple-element.23), calls=%async_computation.1 | async-start | bytes 131072 | tf_op jit(solution)/shard_map/all_to_all | solution.py:370
  47.9 3.2 %shard_map.72 = (bf16[528,256]{1,0:T(8,128)(2,1)S(1)}, f32[8,128]{1,0:T(8,128)S(1)}) custom-call(s32[3]{0:T(128)S(1)} %pad_add_fusion.place_ref.refs_0_, bf16[8,64,256]{2,1,0:T(8,128)(2,1)S(1)} %all-to-all-done.refs_1_, bf16[8,64,256]{2,1,0:T(8,128)(2,1)S(1)} %collective-permute-done.refs_2_, bf16[8,64,256]{2,1,0:T(8,128)(2,1)S(1)} %collective-permute-done.1.refs_3_, ...), custom_call_target="tpu_custom_call" | custom-call | flops 553648128 | bytes 8650752 | tf_op jit(solution)/shard_map/pallas_call | solution.py:353
  51.1 2.4 %all-to-all-done.1.col_ref = f32[8,16,128]{2,1,0:T(8,128)S(1)} async-done(((f32[8,16,128]{2,1,0:T(8,128)}), f32[8,16,128]{2,1,0:T(8,128)S(1)}, u32[]{:S(2)}, u32[]{:S(2)}) %all-to-all-start.1) | async-done | bytes 65568 | tf_op jit(solution)/shard_map/all_to_all | solution.py:370
  53.5 2.0 %shard_map.73 = (f32[528,2048]{1,0:T(8,128)S(1)}, f32[8,128]{1,0:T(8,128)S(1)}, f32[32,8,128]{2,1,0:T(8,128)S(1)}, f32[8,128]{1,0:T(8,128)S(1)}) custom-call(bf16[528,256]{1,0:T(8,128)(2,1)S(1)} %get-tuple-element.22.teach_ref, bf16[2048,256]{1,0:T(8,128)(2,1)S(1)} %shard_map.70.refs_5_.refs_6_.protos_ref, f32[8,16,128]{2,1,0:T(8,128)S(1)} %all-to-all-done.1.col_ref, ...), custom_call_target="tpu_custom_call" | custom-call | flops 553648128 | bytes 8650752 | tf_op jit(solution)/shard_map/pallas_call | solution.py:353
  55.5 16.1 %all_to_all.45.row_ref = f32[32,8,128]{2,1,0:T(8,128)S(1)} all-to-all(f32[32,8,128]{2,1,0:T(8,128)S(1)} %get-tuple-element.29), channel_id=1, replica_groups=mesh['y'=4,'z'=8,'proto'=8] {'y','z'}, dimensions={0} | all-to-all | bytes 262144 | tf_op jit(solution)/shard_map/all_to_all | solution.py:370
  71.7 0.8 shard_map.74
  72.5 8.3 %all_to_all.46.col_ref = f32[8,16,128]{2,1,0:T(8,128)S(1)} all-to-all(f32[8,16,128]{2,1,0:T(8,128)S(1)} %get-tuple-element.31), channel_id=1, replica_groups=mesh['y'=4,'z'=8,'proto'=8] {'proto'}, dimensions={0} | all-to-all | bytes 131072 | tf_op jit(solution)/shard_map/all_to_all | solution.py:370
  80.8 0.7 shard_map.75
  81.5 13.8 %all_to_all.47.row_ref.early_ref = f32[32,8,128]{2,1,0:T(8,128)S(1)} all-to-all(f32[32,8,128]{2,1,0:T(8,128)S(1)} %shard_map.75), channel_id=1, replica_groups=mesh['y'=4,'z'=8,'proto'=8] {'y','z'}, dimensions={0} | all-to-all | bytes 262144 | tf_op jit(solution)/shard_map/all_to_all | solution.py:370
  95.3 0.8 shard_map.76
  96.1 8.0 %all_to_all.48.col_ref = f32[8,16,128]{2,1,0:T(8,128)S(1)} all-to-all(f32[8,16,128]{2,1,0:T(8,128)S(1)} %shard_map.76), channel_id=1, replica_groups=mesh['y'=4,'z'=8,'proto'=8] {'proto'}, dimensions={0} | all-to-all | bytes 131072 | tf_op jit(solution)/shard_map/all_to_all | solution.py:370
  104.1 0.7 shard_map.77
  104.8 13.9 %all_to_all.49.row_ref = f32[32,8,128]{2,1,0:T(8,128)S(1)} all-to-all(f32[32,8,128]{2,1,0:T(8,128)S(1)} %shard_map.77), channel_id=1, replica_groups=mesh['y'=4,'z'=8,'proto'=8] {'y','z'}, dimensions={0} | all-to-all | bytes 262144 | tf_op jit(solution)/shard_map/all_to_all | solution.py:370
  118.7 4.3 %shard_map.78 = (bf16[32,32,256]{2,1,0:T(8,128)(2,1)}, bf16[528,2048]{1,0:T(8,128)(2,1)S(1)}) custom-call(s32[8,128]{1,0:T(8,128)S(1)} %get-tuple-element.21.base_ref, f32[528,2048]{1,0:T(8,128)S(1)} %get-tuple-element.26.exp_ref, f32[8,128]{1,0:T(8,128)S(1)} %get-tuple-element.30.factor_ref, f32[8,128]{1,0:T(8,128)S(1)} %get-tuple-element.28.valid_ref, ...), custom_call_target="tpu_custom_call" | custom-call | flops 553648128 | bytes 8650752 | tf_op jit(solution)/shard_map/pallas_call | solution.py:353
  122.9 1.6 %shard_map.79 = (f32[4,256,256]{2,1,0:T(8,128)S(1)}, f32[4,256,256]{2,1,0:T(8,128)S(1)}) custom-call(s32[3]{0:T(128)S(1)} %pad_add_fusion.place_ref.refs_0_, bf16[528,2048]{1,0:T(8,128)(2,1)S(1)} %get-tuple-element.35.grad_ref, bf16[528,256]{1,0:T(8,128)(2,1)S(1)} %get-tuple-element.33.stud_ref), custom_call_target="tpu_custom_call" | custom-call | flops 553648128 | bytes 8650752 | tf_op jit(solution)/shard_map/pallas_call | solution.py:353
  124.6 0.1 collective-permute-start.7
  124.7 0.0 copy-start
  124.7 4.3 %all-to-all-start.7 = ((bf16[32,32,256]{2,1,0:T(8,128)(2,1)}), bf16[32,32,256]{2,1,0:T(8,128)(2,1)S(1)}, u32[]{:S(2)}, u32[]{:S(2)}) async-start(bf16[32,32,256]{2,1,0:T(8,128)(2,1)} %get-tuple-element.34), calls=%async_computation.7 | async-start | bytes 1048576 | tf_op jit(solution)/shard_map/all_to_all | solution.py:370
  129.0 0.0 collective-permute-done.7
  129.0 1.4 add.7.near_ref
  130.4 0.1 slice_bitcast_fusion
  130.5 1.2 collective-permute-start.10
  131.7 0.9 collective-permute-start.8
  132.6 1.0 collective-permute-start.9
  133.6 14.0 %all-to-all-done.7.parts_ref = bf16[32,32,256]{2,1,0:T(8,128)(2,1)S(1)} async-done(((bf16[32,32,256]{2,1,0:T(8,128)(2,1)}), bf16[32,32,256]{2,1,0:T(8,128)(2,1)S(1)}, u32[]{:S(2)}, u32[]{:S(2)}) %all-to-all-start.7) | async-done | bytes 524320 | tf_op jit(solution)/shard_map/all_to_all | solution.py:370
  147.6 0.0 collective-permute-done.10.refs_2_
  147.7 0.0 collective-permute-done.8.refs_0_
  147.7 0.0 collective-permute-done.9.refs_1_
  147.7 0.9 shard_map.80
  148.6 3.4 %all-to-all-start.8 = ((f32[8,32,256]{2,1,0:T(8,128)}), f32[8,32,256]{2,1,0:T(8,128)S(1)}, u32[]{:S(2)}, u32[]{:S(2)}) async-start(f32[8,32,256]{2,1,0:T(8,128)} %get-tuple-element.38), calls=%async_computation.8 | async-start | bytes 524288 | tf_op jit(solution)/shard_map/all_to_all | solution.py:370
  152.0 0.0 copy-done
  152.0 1.0 shard_map.68.onehot_ref
  153.1 6.4 %all-to-all-done.8.rows_ref = f32[8,32,256]{2,1,0:T(8,128)S(1)} async-done(((f32[8,32,256]{2,1,0:T(8,128)}), f32[8,32,256]{2,1,0:T(8,128)S(1)}, u32[]{:S(2)}, u32[]{:S(2)}) %all-to-all-start.8) | async-done | bytes 262176 | tf_op jit(solution)/shard_map/all_to_all | solution.py:370
  159.5 1.2 shard_map.81
Async XLA Ops:
  0.6 12.1 %collective-permute-start.3 = (bf16[256,256]{1,0:T(8,128)(2,1)}, bf16[256,256]{1,0:T(8,128)(2,1)S(1)}, u32[]{:S(2)}, u32[]{:S(2)}) collective-permute-start(bf16[256,256]{1,0:T(8,128)(2,1)} %param.7), channel_id=1, source_target_pairs={{0,1},{1,0},{2,3},{3,2},{4,5},{5,4},{6,7},{7,6},{8,9},{9,8},{10,11... | collective-permute-start | bytes 393224 | tf_op jit(solution)/shard_map/ppermute | solution.py:408
  4.1 19.7 %all-to-all-start = ((bf16[8,64,256]{2,1,0:T(8,128)(2,1)}), bf16[8,64,256]{2,1,0:T(8,128)(2,1)S(1)}, u32[]{:S(2)}, u32[]{:S(2)}) async-start(bf16[8,64,256]{2,1,0:T(8,128)(2,1)} %shard_map.69), calls=%async_computation | async-start | bytes 524288 | tf_op jit(solution)/shard_map/all_to_all | solution.py:370
  13.6 14.2 %collective-permute-start.4 = (bf16[2,256,256]{2,1,0:T(8,128)(2,1)S(1)}, bf16[2,256,256]{2,1,0:T(8,128)(2,1)S(1)}, u32[]{:S(2)}, u32[]{:S(2)}) collective-permute-start(bf16[2,256,256]{2,1,0:T(8,128)(2,1)S(1)} %pad_maximum_fusion.refs_0_), channel_id=1, source_target_pairs={{0,6},{1,7},{2,0},{3,1},{4,2},{5,3},{6,4},{7,5},{8,14},{9,15},{10,... | collective-permute-start | bytes 786440 | tf_op jit(solution)/shard_map/ppermute | solution.py:411
  16.5 13.0 %collective-permute-start.5 = (bf16[2,256,256]{2,1,0:T(8,128)(2,1)S(1)}, bf16[2,256,256]{2,1,0:T(8,128)(2,1)S(1)}, u32[]{:S(2)}, u32[]{:S(2)}) collective-permute-start(bf16[2,256,256]{2,1,0:T(8,128)(2,1)S(1)} %pad_maximum_fusion.refs_0_), channel_id=1, source_target_pairs={{0,4},{1,5},{2,6},{3,7},{4,0},{5,1},{6,2},{7,3},{8,12},{9,13},{10,... | collective-permute-start | bytes 786440 | tf_op jit(solution)/shard_map/ppermute | solution.py:411
  17.3 14.2 %collective-permute-start.6 = (bf16[2,256,256]{2,1,0:T(8,128)(2,1)S(1)}, bf16[2,256,256]{2,1,0:T(8,128)(2,1)S(1)}, u32[]{:S(2)}, u32[]{:S(2)}) collective-permute-start(bf16[2,256,256]{2,1,0:T(8,128)(2,1)S(1)} %pad_maximum_fusion.refs_0_), channel_id=1, source_target_pairs={{0,2},{1,3},{2,4},{3,5},{4,6},{5,7},{6,0},{7,1},{8,10},{9,11},{10,... | collective-permute-start | bytes 786440 | tf_op jit(solution)/shard_map/ppermute | solution.py:411
  23.8 12.4 %collective-permute-start = (bf16[8,64,256]{2,1,0:T(8,128)(2,1)S(1)}, bf16[8,64,256]{2,1,0:T(8,128)(2,1)S(1)}, u32[]{:S(2)}, u32[]{:S(2)}) collective-permute-start(bf16[8,64,256]{2,1,0:T(8,128)(2,1)S(1)} %all-to-all-done.refs_1_), channel_id=1, source_target_pairs={{0,192},{64,0},{128,64},{192,128},{1,193},{65,1},{129,65},{193,129... | collective-permute-start | bytes 786440 | tf_op jit(solution)/shard_map/ppermute | solution.py:407
  26.8 10.3 %collective-permute-start.1 = (bf16[8,64,256]{2,1,0:T(8,128)(2,1)S(1)}, bf16[8,64,256]{2,1,0:T(8,128)(2,1)S(1)}, u32[]{:S(2)}, u32[]{:S(2)}) collective-permute-start(bf16[8,64,256]{2,1,0:T(8,128)(2,1)S(1)} %all-to-all-done.refs_1_), channel_id=1, source_target_pairs={{0,128},{64,192},{128,0},{192,64},{1,129},{65,193},{129,1},{193,65... | collective-permute-start | bytes 786440 | tf_op jit(solution)/shard_map/ppermute | solution.py:407
  27.8 12.1 %collective-permute-start.2 = (bf16[8,64,256]{2,1,0:T(8,128)(2,1)S(1)}, bf16[8,64,256]{2,1,0:T(8,128)(2,1)S(1)}, u32[]{:S(2)}, u32[]{:S(2)}) collective-permute-start(bf16[8,64,256]{2,1,0:T(8,128)(2,1)S(1)} %all-to-all-done.refs_1_), channel_id=1, source_target_pairs={{0,64},{64,128},{128,192},{192,0},{1,65},{65,129},{129,193},{193,1... | collective-permute-start | bytes 786440 | tf_op jit(solution)/shard_map/ppermute | solution.py:407
  43.6 9.9 %all-to-all-start.1 = ((f32[8,16,128]{2,1,0:T(8,128)}), f32[8,16,128]{2,1,0:T(8,128)S(1)}, u32[]{:S(2)}, u32[]{:S(2)}) async-start(f32[8,16,128]{2,1,0:T(8,128)} %get-tuple-element.23), calls=%async_computation.1 | async-start | bytes 131072 | tf_op jit(solution)/shard_map/all_to_all | solution.py:370
  124.6 4.5 %collective-permute-start.7 = (f32[4,256,256]{2,1,0:T(8,128)S(1)}, f32[4,256,256]{2,1,0:T(8,128)}, u32[]{:S(2)}, u32[]{:S(2)}) collective-permute-start(f32[4,256,256]{2,1,0:T(8,128)S(1)} %get-tuple-element.37), channel_id=1, source_target_pairs={{0,1},{1,0},{2,3},{3,2},{4,5},{5,4},{6,7},{7,6},{8,9},{9,8},{10,11... | collective-permute-start | bytes 3145736 | tf_op jit(solution)/shard_map/ppermute | solution.py:488
  124.7 27.3 %copy-start = (s32[1,512]{1,0:T(1,128)S(1)}, s32[1,512]{1,0:T(1,128)}, u32[]{:S(2)}) copy-start(s32[1,512]{1,0:T(1,128)} %mask_ref.3) | copy-start | bytes 6148
  124.7 23.0 %all-to-all-start.7 = ((bf16[32,32,256]{2,1,0:T(8,128)(2,1)}), bf16[32,32,256]{2,1,0:T(8,128)(2,1)S(1)}, u32[]{:S(2)}, u32[]{:S(2)}) async-start(bf16[32,32,256]{2,1,0:T(8,128)(2,1)} %get-tuple-element.34), calls=%async_computation.7 | async-start | bytes 1048576 | tf_op jit(solution)/shard_map/all_to_all | solution.py:370
  130.5 17.1 %collective-permute-start.10 = (f32[256,256]{1,0:T(8,128)S(1)}, f32[256,256]{1,0:T(8,128)S(1)}, u32[]{:S(2)}, u32[]{:S(2)}) collective-permute-start(f32[256,256]{1,0:T(8,128)S(1)} %get-tuple-element.40), channel_id=1, source_target_pairs={{0,6},{1,7},{2,0},{3,1},{4,2},{5,3},{6,4},{7,5},{8,14},{9,15},{10,... | collective-permute-start | bytes 786440 | tf_op jit(solution)/shard_map/ppermute | solution.py:489
  131.7 15.9 %collective-permute-start.8 = (f32[256,256]{1,0:T(8,128)S(1)}, f32[256,256]{1,0:T(8,128)S(1)}, u32[]{:S(2)}, u32[]{:S(2)}) collective-permute-start(f32[256,256]{1,0:T(8,128)S(1)} %get-tuple-element.42), channel_id=1, source_target_pairs={{0,2},{1,3},{2,4},{3,5},{4,6},{5,7},{6,0},{7,1},{8,10},{9,11},{10,... | collective-permute-start | bytes 786440 | tf_op jit(solution)/shard_map/ppermute | solution.py:489
  132.6 15.1 %collective-permute-start.9 = (f32[256,256]{1,0:T(8,128)S(1)}, f32[256,256]{1,0:T(8,128)S(1)}, u32[]{:S(2)}, u32[]{:S(2)}) collective-permute-start(f32[256,256]{1,0:T(8,128)S(1)} %get-tuple-element.41), channel_id=1, source_target_pairs={{0,4},{1,5},{2,6},{3,7},{4,0},{5,1},{6,2},{7,3},{8,12},{9,13},{10,... | collective-permute-start | bytes 786440 | tf_op jit(solution)/shard_map/ppermute | solution.py:489
  148.6 10.9 %all-to-all-start.8 = ((f32[8,32,256]{2,1,0:T(8,128)}), f32[8,32,256]{2,1,0:T(8,128)S(1)}, u32[]{:S(2)}, u32[]{:S(2)}) async-start(f32[8,32,256]{2,1,0:T(8,128)} %get-tuple-element.38), calls=%async_computation.8 | async-start | bytes 524288 | tf_op jit(solution)/shard_map/all_to_all | solution.py:370

commit v3 on v2

--- a/solution.py
+++ b/solution.py
@@ -314,30 +314,32 @@
         near_ref[away, :, :] = dot_tn(grad_ref[:, pl.ds(start, share)], stud_ref[...])
 
 
-def sum_kernel(parts_ref, near_ref, *refs):
-    *far_refs, out_ref, proto_ref = refs
-    total = jnp.sum(parts_ref[...].astype(F32), axis=0)
-    out_ref[...] = jnp.broadcast_to(total[None], out_ref.shape)
-    total = near_ref[0]
-    for far_ref in far_refs:
-        total = total + far_ref[...]
-    proto_ref[...] = total
-
-
-def patch_kernel(place_ref, count_ref, mask_ref, onehot_ref):
+def sum_kernel(parts_ref, out_ref):
+    out_ref[...] = jnp.sum(parts_ref[...].astype(F32), axis=0)
+
+
+def patch_kernel(place_ref, count_ref, mask_ref, near_ref, *refs):
+    *far_refs, onehot_ref, proto_ref = refs
     patches = onehot_ref.shape[0]
-    device = place_ref[1]
+    group, device = place_ref[0], place_ref[1]
     wanted = iota((patches, CAP), 1)
-    rank = (wanted % SLOTS) * PROTO + row_offset(wanted // SLOTS, device)
+    block = wanted // SLOTS
+    source = (group // 2 + block // 2) % (PROTO // 2) * 2 + (group + block) % 2
+    rank = (wanted % SLOTS) * PROTO + row_offset(source, device)
     at = (iota((patches, CAP), 0) == rank).astype(F32)
     mask = jnp.broadcast_to(mask_ref[...].astype(F32), (8, patches))
     chosen = (dot_nn(mask, at, HIGH)[:1] + 0.5).astype(jnp.int32)
     chosen = jnp.where(rank[:1, :] < count_ref[0], chosen, -1)
     onehot_ref[...] = (iota((patches, CAP), 0) == chosen).astype(BF16)
-
-
-def spread_kernel(onehot_ref, rows_ref, out_ref):
-    rest = rows_ref[...].reshape(CAP, out_ref.shape[1])
+    total = near_ref[0]
+    for far_ref in far_refs:
+        total = total + far_ref[...]
+    proto_ref[...] = total
+
+
+def spread_kernel(onehot_ref, *refs):
+    *row_refs, out_ref = refs
+    rest = jnp.concatenate([ref[i] for ref in row_refs for i in range(2)], axis=0)
     total = None
     for _ in range(3):
         part = rest.astype(BF16)
@@ -412,10 +414,6 @@
     (protos,) = call(
         prototypes_kernel, [((protos_held, width), BF16)], (place, *pairs_held), scalars=1
     )
-    (onehot,) = call(
-        patch_kernel, [((patches, CAP), BF16)], (place, counts, mask_index), scalars=2
-    )
-
     packed = ((8, LANES), F32)
     col_out = ((PROTO, chunks, LANES), F32)
     row_out = ((devices, 8, LANES), F32)
@@ -487,13 +485,18 @@
     )
     mine = near + lax.ppermute(far, "proto", swap)
     arrived = [lax.ppermute(mine[away], "proto", routes[away]) for away in range(1, half)]
-    rows, grad_prototypes = call(
-        sum_kernel,
-        [((PROTO, SLOTS, width), F32), ((share, width), F32)],
-        (exchange(grad_slots, TOK), mine, *arrived),
-    )
-    rows = exchange(rows, "proto")
-    (grad_patches,) = call(spread_kernel, [((patches, width), F32)], (onehot, rows))
+    (rows,) = call(sum_kernel, [((SLOTS, width), F32)], (exchange(grad_slots, TOK),))
+    rows = jnp.stack([rows, lax.ppermute(rows, "proto", swap)])
+    all_rows = [rows]
+    for away in range(1, half):
+        all_rows.append(lax.ppermute(rows, "proto", routes[-away % half]))
+    onehot, grad_prototypes = call(
+        patch_kernel,
+        [((patches, CAP), BF16), ((share, width), F32)],
+        (place, counts, mask_index, mine, *arrived),
+        scalars=2,
+    )
+    (grad_patches,) = call(spread_kernel, [((patches, width), F32)], (onehot, *all_rows))
     return (grad_patches, grad_prototypes)
 
 

time: 162 us -> 157 us (0.969)
  waiting for transfers between devices: 38.6 us -> 31.9 us
  starting transfers between devices: 33.7 us -> 35.4 us
    all_to_all x4 -> x3, waiting for transfers between devices: 28.4 us -> 21.1 us  [exchange(): return lax.all_to_all(parts, axis, 0, 0, tiled=True)]
    ppermute x0 -> x4, starting transfers between devices: none -> 3.72 us  [the longest x3 3.63 us: on_device(): all_rows.append(lax.ppermute(rows, 'proto', routes[-away % half]))]
    all_to_all x4 -> x3, starting transfers between devices: 20.6 us -> 17.2 us  [exchange(): return lax.all_to_all(parts, axis, 0, 0, tiled=True)]
    ppermute x0 -> x4, waiting for transfers between devices: none -> 3.07 us  [the longest x3 1.88 us: on_device(): all_rows.append(lax.ppermute(rows, 'proto', routes[-away % half]))]
    ppermute x3, waiting for transfers between devices: 2.38 us -> 0.01 us  [on_device(): pairs_held.append(lax.ppermute(pair, 'proto', routes[-away % half]))]
  transfers between devices with their start and end apart: 15 -> 18, of which waited for: 9 -> 8; matrix products, arithmetic and copies ran while one was open for 2% -> 2% of each run, Pallas kernels for 5% -> 5%
where the time goes in v3:
time: 157 us; the launch traced here: 156 us
  blocking collectives  60.9 us (39%)
  starting transfers between devices  35.4 us (23%)
  waiting for transfers between devices  31.9 us (20%)
  Pallas kernels  24.3 us (15%)
  other arithmetic  2.42 us (2%)
    all_to_all x5, blocking collectives, exchange(): return lax.all_to_all(parts, axis, 0, 0, tiled=True)  60.9 us
    pallas_call x13, Pallas kernels, call(): pl.pallas_call(kernel, out_shape=[jax.ShapeDtypeStruct(shape, dtype) for...  21.5 us
    all_to_all x3, waiting for transfers between devices, exchange(): return lax.all_to_all(parts, axis, 0, 0, tiled=True)  21.1 us
    all_to_all x3, starting transfers between devices, exchange(): return lax.all_to_all(parts, axis, 0, 0, tiled=True)  17.2 us
    ppermute x3, waiting for transfers between devices, on_device(): lines.append(lax.ppermute(pay, 'y', route))  7.74 us
    ppermute x3, starting transfers between devices, on_device(): lines.append(lax.ppermute(pay, 'y', route))  5.83 us
    ppermute x3, starting transfers between devices, on_device(): pairs_held.append(lax.ppermute(pair, 'proto', routes[-away % half]))  5.73 us
    ppermute x3, starting transfers between devices, on_device(): all_rows.append(lax.ppermute(rows, 'proto', routes[-away % half]))  3.63 us
  transfers between devices with their start and end apart: 18, of which 8 were waited for; matrix products, arithmetic and copies ran while one was open for 2% of the time, Pallas kernels for 5%

profile of v3, /device:TPU:32, one launch (start us, length us, event | category | flops | bytes accessed | tf_op | source)
XLA Modules:
  0.0 156.4 jit_solution(5892564508961847506)
XLA Ops:
  0.6 0.1 collective-permute-start.3
  1.4 2.7 %shard_map.68 = bf16[8,64,256]{2,1,0:T(8,128)(2,1)} custom-call(s32[1]{0:T(128)S(6)} %copy.7.count_ref, s32[1,512]{1,0:T(1,128)} %mask_ref.3, bf16[512,256]{1,0:T(8,128)(2,1)} %teacher_ref.1, bf16[512,256]{1,0:T(8,128)(2,1)} %student_ref.1), custom_call_target="tpu_custom_call" | custom-call | tf_op jit(solution)/shard_map/pallas_call | solution.py:390
  4.1 8.6 %all-to-all-start = ((bf16[8,64,256]{2,1,0:T(8,128)(2,1)}), bf16[8,64,256]{2,1,0:T(8,128)(2,1)S(1)}, u32[]{:S(2)}, u32[]{:S(2)}) async-start(bf16[8,64,256]{2,1,0:T(8,128)(2,1)} %shard_map.68), calls=%async_computation | async-start | bytes 524288 | tf_op jit(solution)/shard_map/all_to_all | solution.py:372
  12.7 0.0 collective-permute-done.3
  12.7 0.9 pad_maximum_fusion.refs_0_
  13.6 1.6 %collective-permute-start.6 = (bf16[2,256,256]{2,1,0:T(8,128)(2,1)S(1)}, bf16[2,256,256]{2,1,0:T(8,128)(2,1)S(1)}, u32[]{:S(2)}, u32[]{:S(2)}) collective-permute-start(bf16[2,256,256]{2,1,0:T(8,128)(2,1)S(1)} %pad_maximum_fusion.refs_0_), channel_id=1, source_target_pairs={{0,2},{1,3},{2,4},{3,5},{4,6},{5,7},{6,0},{7,1},{8,10},{9,11},{10,... | collective-permute-start | bytes 786440 | tf_op jit(solution)/shard_map/ppermute | solution.py:413
  15.2 2.7 %collective-permute-start.5 = (bf16[2,256,256]{2,1,0:T(8,128)(2,1)S(1)}, bf16[2,256,256]{2,1,0:T(8,128)(2,1)S(1)}, u32[]{:S(2)}, u32[]{:S(2)}) collective-permute-start(bf16[2,256,256]{2,1,0:T(8,128)(2,1)S(1)} %pad_maximum_fusion.refs_0_), channel_id=1, source_target_pairs={{0,4},{1,5},{2,6},{3,7},{4,0},{5,1},{6,2},{7,3},{8,12},{9,13},{10,... | collective-permute-start | bytes 786440 | tf_op jit(solution)/shard_map/ppermute | solution.py:413
  17.9 1.4 collective-permute-start.4
  19.4 4.4 %all-to-all-done.refs_1_ = bf16[8,64,256]{2,1,0:T(8,128)(2,1)S(1)} async-done(((bf16[8,64,256]{2,1,0:T(8,128)(2,1)}), bf16[8,64,256]{2,1,0:T(8,128)(2,1)S(1)}, u32[]{:S(2)}, u32[]{:S(2)}) %all-to-all-start) | async-done | bytes 262176 | tf_op jit(solution)/shard_map/all_to_all | solution.py:372
  23.8 1.6 %collective-permute-start.2 = (bf16[8,64,256]{2,1,0:T(8,128)(2,1)S(1)}, bf16[8,64,256]{2,1,0:T(8,128)(2,1)S(1)}, u32[]{:S(2)}, u32[]{:S(2)}) collective-permute-start(bf16[8,64,256]{2,1,0:T(8,128)(2,1)S(1)} %all-to-all-done.refs_1_), channel_id=1, source_target_pairs={{0,64},{64,128},{128,192},{192,0},{1,65},{65,129},{129,193},{193,1... | collective-permute-start | bytes 786440 | tf_op jit(solution)/shard_map/ppermute | solution.py:409
  25.4 2.9 %collective-permute-start.1 = (bf16[8,64,256]{2,1,0:T(8,128)(2,1)S(1)}, bf16[8,64,256]{2,1,0:T(8,128)(2,1)S(1)}, u32[]{:S(2)}, u32[]{:S(2)}) collective-permute-start(bf16[8,64,256]{2,1,0:T(8,128)(2,1)S(1)} %all-to-all-done.refs_1_), channel_id=1, source_target_pairs={{0,128},{64,192},{128,0},{192,64},{1,129},{65,193},{129,1},{193,65... | collective-permute-start | bytes 786440 | tf_op jit(solution)/shard_map/ppermute | solution.py:409
  28.3 0.0 collective-permute-done.6.refs_3_
  28.3 1.3 collective-permute-start
  29.6 0.1 pad_add_fusion.place_ref.refs_0_
  29.7 0.0 collective-permute-done.5.refs_2_
  29.7 0.0 collective-permute-done.4.refs_1_
  29.7 0.6 shard_map.69.refs_5_.refs_6_.protos_ref
  30.3 3.0 %collective-permute-done.2.refs_4_ = bf16[8,64,256]{2,1,0:T(8,128)(2,1)S(1)} collective-permute-done((bf16[8,64,256]{2,1,0:T(8,128)(2,1)S(1)}, bf16[8,64,256]{2,1,0:T(8,128)(2,1)S(1)}, u32[]{:S(2)}, u32[]{:S(2)}) %collective-permute-start.2) | collective-permute-done | bytes 262176 | tf_op jit(solution)/shard_map/ppermute | solution.py:409
  33.3 4.8 %collective-permute-done.1.refs_3_ = bf16[8,64,256]{2,1,0:T(8,128)(2,1)S(1)} collective-permute-done((bf16[8,64,256]{2,1,0:T(8,128)(2,1)S(1)}, bf16[8,64,256]{2,1,0:T(8,128)(2,1)S(1)}, u32[]{:S(2)}, u32[]{:S(2)}) %collective-permute-start.1) | collective-permute-done | bytes 262176 | tf_op jit(solution)/shard_map/ppermute | solution.py:409
  38.1 0.0 collective-permute-done.refs_2_
  38.1 3.7 %shard_map.70 = (bf16[528,256]{1,0:T(8,128)(2,1)S(1)}, f32[8,1024]{1,0:T(8,128)S(1)}, f32[8,128]{1,0:T(8,128)S(1)}, s32[8,128]{1,0:T(8,128)S(1)}, f32[8,16,128]{2,1,0:T(8,128)}) custom-call(s32[3]{0:T(128)S(1)} %pad_add_fusion.place_ref.refs_0_, bf16[8,64,256]{2,1,0:T(8,128)(2,1)S(1)} %all-to-all-done.refs_1_, ...), custom_call_target="tpu_custom_call" | custom-call | flops 553648128 | bytes 8650752 | tf_op jit(solution)/shard_map/pallas_call | solution.py:355
  41.8 4.3 %all-to-all-start.1 = ((f32[8,16,128]{2,1,0:T(8,128)}), f32[8,16,128]{2,1,0:T(8,128)S(1)}, u32[]{:S(2)}, u32[]{:S(2)}) async-start(f32[8,16,128]{2,1,0:T(8,128)} %get-tuple-element.23), calls=%async_computation.1 | async-start | bytes 131072 | tf_op jit(solution)/shard_map/all_to_all | solution.py:372
  46.1 3.2 %shard_map.71 = (bf16[528,256]{1,0:T(8,128)(2,1)S(1)}, f32[8,128]{1,0:T(8,128)S(1)}) custom-call(s32[3]{0:T(128)S(1)} %pad_add_fusion.place_ref.refs_0_, bf16[8,64,256]{2,1,0:T(8,128)(2,1)S(1)} %all-to-all-done.refs_1_, bf16[8,64,256]{2,1,0:T(8,128)(2,1)S(1)} %collective-permute-done.refs_2_, bf16[8,64,256]{2,1,0:T(8,128)(2,1)S(1)} %collective-permute-done.1.refs_3_, ...), custom_call_target="tpu_custom_call" | custom-call | flops 553648128 | bytes 8650752 | tf_op jit(solution)/shard_map/pallas_call | solution.py:355
  49.3 2.4 %all-to-all-done.1.col_ref = f32[8,16,128]{2,1,0:T(8,128)S(1)} async-done(((f32[8,16,128]{2,1,0:T(8,128)}), f32[8,16,128]{2,1,0:T(8,128)S(1)}, u32[]{:S(2)}, u32[]{:S(2)}) %all-to-all-start.1) | async-done | bytes 65568 | tf_op jit(solution)/shard_map/all_to_all | solution.py:372
  51.7 2.0 %shard_map.72 = (f32[528,2048]{1,0:T(8,128)S(1)}, f32[8,128]{1,0:T(8,128)S(1)}, f32[32,8,128]{2,1,0:T(8,128)S(1)}, f32[8,128]{1,0:T(8,128)S(1)}) custom-call(bf16[528,256]{1,0:T(8,128)(2,1)S(1)} %get-tuple-element.22.teach_ref, bf16[2048,256]{1,0:T(8,128)(2,1)S(1)} %shard_map.69.refs_5_.refs_6_.protos_ref, f32[8,16,128]{2,1,0:T(8,128)S(1)} %all-to-all-done.1.col_ref, ...), custom_call_target="tpu_custom_call" | custom-call | flops 553648128 | bytes 8650752 | tf_op jit(solution)/shard_map/pallas_call | solution.py:355
  53.7 17.0 %all_to_all.40.row_ref = f32[32,8,128]{2,1,0:T(8,128)S(1)} all-to-all(f32[32,8,128]{2,1,0:T(8,128)S(1)} %get-tuple-element.29), channel_id=1, replica_groups=mesh['y'=4,'z'=8,'proto'=8] {'y','z'}, dimensions={0} | all-to-all | bytes 262144 | tf_op jit(solution)/shard_map/all_to_all | solution.py:372
  70.8 0.8 shard_map.73
  71.6 8.1 %all_to_all.41.col_ref = f32[8,16,128]{2,1,0:T(8,128)S(1)} all-to-all(f32[8,16,128]{2,1,0:T(8,128)S(1)} %get-tuple-element.31), channel_id=1, replica_groups=mesh['y'=4,'z'=8,'proto'=8] {'proto'}, dimensions={0} | all-to-all | bytes 131072 | tf_op jit(solution)/shard_map/all_to_all | solution.py:372
  79.7 0.7 shard_map.74
  80.5 13.9 %all_to_all.42.row_ref.early_ref = f32[32,8,128]{2,1,0:T(8,128)S(1)} all-to-all(f32[32,8,128]{2,1,0:T(8,128)S(1)} %shard_map.74), channel_id=1, replica_groups=mesh['y'=4,'z'=8,'proto'=8] {'y','z'}, dimensions={0} | all-to-all | bytes 262144 | tf_op jit(solution)/shard_map/all_to_all | solution.py:372
  94.3 0.8 shard_map.75
  95.1 8.0 %all_to_all.43.col_ref = f32[8,16,128]{2,1,0:T(8,128)S(1)} all-to-all(f32[8,16,128]{2,1,0:T(8,128)S(1)} %shard_map.75), channel_id=1, replica_groups=mesh['y'=4,'z'=8,'proto'=8] {'proto'}, dimensions={0} | all-to-all | bytes 131072 | tf_op jit(solution)/shard_map/all_to_all | solution.py:372
  103.1 0.7 shard_map.76
  103.8 13.9 %all_to_all.44.row_ref = f32[32,8,128]{2,1,0:T(8,128)S(1)} all-to-all(f32[32,8,128]{2,1,0:T(8,128)S(1)} %shard_map.76), channel_id=1, replica_groups=mesh['y'=4,'z'=8,'proto'=8] {'y','z'}, dimensions={0} | all-to-all | bytes 262144 | tf_op jit(solution)/shard_map/all_to_all | solution.py:372
  117.7 4.3 %shard_map.77 = (bf16[32,32,256]{2,1,0:T(8,128)(2,1)}, bf16[528,2048]{1,0:T(8,128)(2,1)S(1)}) custom-call(s32[8,128]{1,0:T(8,128)S(1)} %get-tuple-element.21.base_ref, f32[528,2048]{1,0:T(8,128)S(1)} %get-tuple-element.26.exp_ref, f32[8,128]{1,0:T(8,128)S(1)} %get-tuple-element.30.factor_ref, f32[8,128]{1,0:T(8,128)S(1)} %get-tuple-element.28.valid_ref, ...), custom_call_target="tpu_custom_call" | custom-call | flops 553648128 | bytes 8650752 | tf_op jit(solution)/shard_map/pallas_call | solution.py:355
  121.9 0.0 copy-start
  121.9 1.6 %shard_map.78 = (f32[4,256,256]{2,1,0:T(8,128)S(1)}, f32[4,256,256]{2,1,0:T(8,128)S(1)}) custom-call(s32[3]{0:T(128)S(1)} %pad_add_fusion.place_ref.refs_0_, bf16[528,2048]{1,0:T(8,128)(2,1)S(1)} %get-tuple-element.34.grad_ref, bf16[528,256]{1,0:T(8,128)(2,1)S(1)} %get-tuple-element.33.stud_ref), custom_call_target="tpu_custom_call" | custom-call | flops 553648128 | bytes 8650752 | tf_op jit(solution)/shard_map/pallas_call | solution.py:355
  123.6 0.1 collective-permute-start.7
  123.7 4.3 %all-to-all-start.7 = ((bf16[32,32,256]{2,1,0:T(8,128)(2,1)}), bf16[32,32,256]{2,1,0:T(8,128)(2,1)S(1)}, u32[]{:S(2)}, u32[]{:S(2)}) async-start(bf16[32,32,256]{2,1,0:T(8,128)(2,1)} %get-tuple-element.38), calls=%async_computation.7 | async-start | bytes 1048576 | tf_op jit(solution)/shard_map/all_to_all | solution.py:372
  128.0 0.0 collective-permute-done.7
  128.0 1.4 add.7.near_ref
  129.4 0.1 slice_bitcast_fusion
  129.5 1.2 collective-permute-start.10
  130.7 1.5 collective-permute-start.9
  132.2 0.0 collective-permute-start.8
  132.2 14.3 %all-to-all-done.7.parts_ref = bf16[32,32,256]{2,1,0:T(8,128)(2,1)S(1)} async-done(((bf16[32,32,256]{2,1,0:T(8,128)(2,1)}), bf16[32,32,256]{2,1,0:T(8,128)(2,1)S(1)}, u32[]{:S(2)}, u32[]{:S(2)}) %all-to-all-start.7) | async-done | bytes 524320 | tf_op jit(solution)/shard_map/all_to_all | solution.py:372
  146.5 0.1 shard_map.80
  146.6 0.1 collective-permute-start.11
  146.7 1.2 collective-permute-done.11
  147.9 0.6 collective-permute-start.14
  148.4 2.1 %collective-permute-start.13 = (f32[2,32,256]{2,1,0:T(8,128)S(1)}, f32[2,32,256]{2,1,0:T(8,128)S(1)}, u32[]{:S(2)}, u32[]{:S(2)}) collective-permute-start(f32[2,32,256]{2,1,0:T(8,128)S(1)} %pad_maximum_fusion.1.refs_0_), channel_id=1, source_target_pairs={{0,4},{1,5},{2,6},{3,7},{4,0},{5,1},{6,2},{7,3},{8,12},{9,13},{10,... | collective-permute-start | bytes 196616 | tf_op jit(solution)/shard_map/ppermute | solution.py:492
  150.5 0.0 collective-permute-done.10.refs_2_
  150.5 1.0 collective-permute-start.12
  151.5 0.0 collective-permute-done.9.refs_1_
  151.5 0.0 collective-permute-done.8.refs_0_
  151.5 0.0 copy-done
  151.5 1.8 %shard_map.79 = (bf16[512,256]{1,0:T(8,128)(2,1)S(1)}, f32[256,256]{1,0:T(8,128)}) custom-call(s32[3]{0:T(128)S(1)} %pad_add_fusion.place_ref.refs_0_, s32[1]{0:T(128)S(6)} %copy.7.count_ref, s32[1,512]{1,0:T(1,128)S(1)} %copy-done, f32[4,256,256]{2,1,0:T(8,128)S(1)} %add.7.near_ref, f32[256,256]{1,0:T(8,128)S(1)} %collective-permute-done.8.refs_0_, ...), custom_call_target="tpu_custom_call" | custom-call | tf_op jit(solution)/shard_map/pallas_call | solution.py:355
  153.3 1.3 collective-permute-done.14.refs_3_
  154.6 0.0 collective-permute-done.13.refs_2_
  154.7 0.6 collective-permute-done.12.refs_1_
  155.2 1.2 shard_map.81
  (1 shorter events, 0.0 us)
Async XLA Ops:
  0.6 12.1 %collective-permute-start.3 = (bf16[256,256]{1,0:T(8,128)(2,1)}, bf16[256,256]{1,0:T(8,128)(2,1)S(1)}, u32[]{:S(2)}, u32[]{:S(2)}) collective-permute-start(bf16[256,256]{1,0:T(8,128)(2,1)} %param.7), channel_id=1, source_target_pairs={{0,1},{1,0},{2,3},{3,2},{4,5},{5,4},{6,7},{7,6},{8,9},{9,8},{10,11... | collective-permute-start | bytes 393224 | tf_op jit(solution)/shard_map/ppermute | solution.py:410
  4.1 19.7 %all-to-all-start = ((bf16[8,64,256]{2,1,0:T(8,128)(2,1)}), bf16[8,64,256]{2,1,0:T(8,128)(2,1)S(1)}, u32[]{:S(2)}, u32[]{:S(2)}) async-start(bf16[8,64,256]{2,1,0:T(8,128)(2,1)} %shard_map.68), calls=%async_computation | async-start | bytes 524288 | tf_op jit(solution)/shard_map/all_to_all | solution.py:372
  13.6 14.6 %collective-permute-start.6 = (bf16[2,256,256]{2,1,0:T(8,128)(2,1)S(1)}, bf16[2,256,256]{2,1,0:T(8,128)(2,1)S(1)}, u32[]{:S(2)}, u32[]{:S(2)}) collective-permute-start(bf16[2,256,256]{2,1,0:T(8,128)(2,1)S(1)} %pad_maximum_fusion.refs_0_), channel_id=1, source_target_pairs={{0,2},{1,3},{2,4},{3,5},{4,6},{5,7},{6,0},{7,1},{8,10},{9,11},{10,... | collective-permute-start | bytes 786440 | tf_op jit(solution)/shard_map/ppermute | solution.py:413
  15.2 14.5 %collective-permute-start.5 = (bf16[2,256,256]{2,1,0:T(8,128)(2,1)S(1)}, bf16[2,256,256]{2,1,0:T(8,128)(2,1)S(1)}, u32[]{:S(2)}, u32[]{:S(2)}) collective-permute-start(bf16[2,256,256]{2,1,0:T(8,128)(2,1)S(1)} %pad_maximum_fusion.refs_0_), channel_id=1, source_target_pairs={{0,4},{1,5},{2,6},{3,7},{4,0},{5,1},{6,2},{7,3},{8,12},{9,13},{10,... | collective-permute-start | bytes 786440 | tf_op jit(solution)/shard_map/ppermute | solution.py:413
  17.9 11.8 %collective-permute-start.4 = (bf16[2,256,256]{2,1,0:T(8,128)(2,1)S(1)}, bf16[2,256,256]{2,1,0:T(8,128)(2,1)S(1)}, u32[]{:S(2)}, u32[]{:S(2)}) collective-permute-start(bf16[2,256,256]{2,1,0:T(8,128)(2,1)S(1)} %pad_maximum_fusion.refs_0_), channel_id=1, source_target_pairs={{0,6},{1,7},{2,0},{3,1},{4,2},{5,3},{6,4},{7,5},{8,14},{9,15},{10,... | collective-permute-start | bytes 786440 | tf_op jit(solution)/shard_map/ppermute | solution.py:413
  23.8 9.5 %collective-permute-start.2 = (bf16[8,64,256]{2,1,0:T(8,128)(2,1)S(1)}, bf16[8,64,256]{2,1,0:T(8,128)(2,1)S(1)}, u32[]{:S(2)}, u32[]{:S(2)}) collective-permute-start(bf16[8,64,256]{2,1,0:T(8,128)(2,1)S(1)} %all-to-all-done.refs_1_), channel_id=1, source_target_pairs={{0,64},{64,128},{128,192},{192,0},{1,65},{65,129},{129,193},{193,1... | collective-permute-start | bytes 786440 | tf_op jit(solution)/shard_map/ppermute | solution.py:409
  25.4 12.7 %collective-permute-start.1 = (bf16[8,64,256]{2,1,0:T(8,128)(2,1)S(1)}, bf16[8,64,256]{2,1,0:T(8,128)(2,1)S(1)}, u32[]{:S(2)}, u32[]{:S(2)}) collective-permute-start(bf16[8,64,256]{2,1,0:T(8,128)(2,1)S(1)} %all-to-all-done.refs_1_), channel_id=1, source_target_pairs={{0,128},{64,192},{128,0},{192,64},{1,129},{65,193},{129,1},{193,65... | collective-permute-start | bytes 786440 | tf_op jit(solution)/shard_map/ppermute | solution.py:409
  28.3 9.8 %collective-permute-start = (bf16[8,64,256]{2,1,0:T(8,128)(2,1)S(1)}, bf16[8,64,256]{2,1,0:T(8,128)(2,1)S(1)}, u32[]{:S(2)}, u32[]{:S(2)}) collective-permute-start(bf16[8,64,256]{2,1,0:T(8,128)(2,1)S(1)} %all-to-all-done.refs_1_), channel_id=1, source_target_pairs={{0,192},{64,0},{128,64},{192,128},{1,193},{65,1},{129,65},{193,129... | collective-permute-start | bytes 786440 | tf_op jit(solution)/shard_map/ppermute | solution.py:409
  41.8 9.9 %all-to-all-start.1 = ((f32[8,16,128]{2,1,0:T(8,128)}), f32[8,16,128]{2,1,0:T(8,128)S(1)}, u32[]{:S(2)}, u32[]{:S(2)}) async-start(f32[8,16,128]{2,1,0:T(8,128)} %get-tuple-element.23), calls=%async_computation.1 | async-start | bytes 131072 | tf_op jit(solution)/shard_map/all_to_all | solution.py:372
  121.9 29.6 %copy-start = (s32[1,512]{1,0:T(1,128)S(1)}, s32[1,512]{1,0:T(1,128)}, u32[]{:S(2)}) copy-start(s32[1,512]{1,0:T(1,128)} %mask_ref.3) | copy-start | bytes 6148
  123.6 4.4 %collective-permute-start.7 = (f32[4,256,256]{2,1,0:T(8,128)S(1)}, f32[4,256,256]{2,1,0:T(8,128)}, u32[]{:S(2)}, u32[]{:S(2)}) collective-permute-start(f32[4,256,256]{2,1,0:T(8,128)S(1)} %get-tuple-element.36), channel_id=1, source_target_pairs={{0,1},{1,0},{2,3},{3,2},{4,5},{5,4},{6,7},{7,6},{8,9},{9,8},{10,11... | collective-permute-start | bytes 3145736 | tf_op jit(solution)/shard_map/ppermute | solution.py:486
  123.7 22.8 %all-to-all-start.7 = ((bf16[32,32,256]{2,1,0:T(8,128)(2,1)}), bf16[32,32,256]{2,1,0:T(8,128)(2,1)S(1)}, u32[]{:S(2)}, u32[]{:S(2)}) async-start(bf16[32,32,256]{2,1,0:T(8,128)(2,1)} %get-tuple-element.38), calls=%async_computation.7 | async-start | bytes 1048576 | tf_op jit(solution)/shard_map/all_to_all | solution.py:372
  129.5 21.0 %collective-permute-start.10 = (f32[256,256]{1,0:T(8,128)S(1)}, f32[256,256]{1,0:T(8,128)S(1)}, u32[]{:S(2)}, u32[]{:S(2)}) collective-permute-start(f32[256,256]{1,0:T(8,128)S(1)} %get-tuple-element.40), channel_id=1, source_target_pairs={{0,6},{1,7},{2,0},{3,1},{4,2},{5,3},{6,4},{7,5},{8,14},{9,15},{10,... | collective-permute-start | bytes 786440 | tf_op jit(solution)/shard_map/ppermute | solution.py:487
  130.7 20.8 %collective-permute-start.9 = (f32[256,256]{1,0:T(8,128)S(1)}, f32[256,256]{1,0:T(8,128)S(1)}, u32[]{:S(2)}, u32[]{:S(2)}) collective-permute-start(f32[256,256]{1,0:T(8,128)S(1)} %get-tuple-element.41), channel_id=1, source_target_pairs={{0,4},{1,5},{2,6},{3,7},{4,0},{5,1},{6,2},{7,3},{8,12},{9,13},{10,... | collective-permute-start | bytes 786440 | tf_op jit(solution)/shard_map/ppermute | solution.py:487
  132.2 19.3 %collective-permute-start.8 = (f32[256,256]{1,0:T(8,128)S(1)}, f32[256,256]{1,0:T(8,128)S(1)}, u32[]{:S(2)}, u32[]{:S(2)}) collective-permute-start(f32[256,256]{1,0:T(8,128)S(1)} %get-tuple-element.42), channel_id=1, source_target_pairs={{0,2},{1,3},{2,4},{3,5},{4,6},{5,7},{6,0},{7,1},{8,10},{9,11},{10,... | collective-permute-start | bytes 786440 | tf_op jit(solution)/shard_map/ppermute | solution.py:487
  146.6 1.3 collective-permute-start.11
  147.9 6.8 %collective-permute-start.14 = (f32[2,32,256]{2,1,0:T(8,128)S(1)}, f32[2,32,256]{2,1,0:T(8,128)S(1)}, u32[]{:S(2)}, u32[]{:S(2)}) collective-permute-start(f32[2,32,256]{2,1,0:T(8,128)S(1)} %pad_maximum_fusion.1.refs_0_), channel_id=1, source_target_pairs={{0,2},{1,3},{2,4},{3,5},{4,6},{5,7},{6,0},{7,1},{8,10},{9,11},{10,... | collective-permute-start | bytes 196616 | tf_op jit(solution)/shard_map/ppermute | solution.py:492
  148.4 6.2 %collective-permute-start.13 = (f32[2,32,256]{2,1,0:T(8,128)S(1)}, f32[2,32,256]{2,1,0:T(8,128)S(1)}, u32[]{:S(2)}, u32[]{:S(2)}) collective-permute-start(f32[2,32,256]{2,1,0:T(8,128)S(1)} %pad_maximum_fusion.1.refs_0_), channel_id=1, source_target_pairs={{0,4},{1,5},{2,6},{3,7},{4,0},{5,1},{6,2},{7,3},{8,12},{9,13},{10,... | collective-permute-start | bytes 196616 | tf_op jit(solution)/shard_map/ppermute | solution.py:492
  150.5 4.7 %collective-permute-start.12 = (f32[2,32,256]{2,1,0:T(8,128)S(1)}, f32[2,32,256]{2,1,0:T(8,128)S(1)}, u32[]{:S(2)}, u32[]{:S(2)}) collective-permute-start(f32[2,32,256]{2,1,0:T(8,128)S(1)} %pad_maximum_fusion.1.refs_0_), channel_id=1, source_target_pairs={{0,6},{1,7},{2,0},{3,1},{4,2},{5,3},{6,4},{7,5},{8,14},{9,15},{10,... | collective-permute-start | bytes 196616 | tf_op jit(solution)/shard_map/ppermute | solution.py:492

commit v4 on v3

--- a/solution.py
+++ b/solution.py
@@ -49,19 +49,31 @@
     return [(at // LANES, slice(at, min(at + LANES, tokens))) for at in range(0, tokens, LANES)]
 
 
-def turned(rows, block, first_lane_only):
-    at = iota((8, LANES), 0) == block
+def turned(parts, first_lane_only):
+    count = len(parts)
+    short = LANES - parts[-1].shape[0]
+    if short:
+        parts = parts + [jnp.zeros((short, LANES), F32)]
+    at = jnp.ones((8, LANES), F32)
     if first_lane_only:
-        at = at & (iota((8, LANES), 1) == 0)
-    short = LANES - rows.shape[0]
-    if short:
-        rows = jnp.concatenate([rows, jnp.zeros((short, LANES), F32)], axis=0)
-    return dot_nt(at.astype(F32), rows, HIGH)
-
-
-def column(packed, block, size):
-    at = (iota((8, LANES), 0) == block).astype(F32)
-    return dot_tn(packed, at, HIGH)[:size]
+        at = (iota((8, LANES), 1) == 0).astype(F32)
+    values = dot_nt(at, jnp.concatenate(parts, axis=0), HIGH)
+    rows = [values[:1, block * LANES : (block + 1) * LANES] for block in range(count)]
+    return jnp.concatenate(rows + [jnp.zeros((8 - count, LANES), F32)], axis=0)
+
+
+def in_parts(packed):
+    parts = []
+    for _ in range(3):
+        part = packed.astype(BF16).astype(F32)
+        packed = packed - part
+        parts.append(part)
+    return jnp.concatenate(parts + [jnp.zeros((8, LANES), F32)], axis=0).astype(BF16)
+
+
+def column(parts, block, size):
+    at = (iota((32, LANES), 0) % 8 == block).astype(F32).astype(BF16)
+    return dot_tn(parts, at)[:size]
 
 
 def lse_over_first(values):
@@ -180,8 +192,7 @@
         if shift is not None:
             scores = scores + shift[:, start : start + step]
         out_ref[:, start : start + step] = scores
-    tops = jnp.zeros((8, LANES), F32)
-    totals = jnp.zeros((8, LANES), F32)
+    tops, totals = [], []
     starts = range(0, protos_ref.shape[0], LANES)
     for block, rows in blocks(left_ref.shape[0]):
         top = out_ref[rows, :LANES]
@@ -193,9 +204,9 @@
             exps = jnp.exp(out_ref[rows, start : start + LANES] - top)
             out_ref[rows, start : start + LANES] = exps
             sums += exps
-        tops += turned(top, block, True)
-        totals += turned(sums, block, False)
-    return tops, totals
+        tops.append(top)
+        totals.append(sums)
+    return turned(tops, True), turned(totals, False)
 
 
 def second_kernel(teach_ref, protos_ref, col_ref, stud_row_ref, exp_ref, top_ref, row_ref, stud_out_ref):
@@ -210,6 +221,7 @@
 def weighted_columns(exp_ref, weight):
     chunks = exp_ref.shape[1] // LANES
     sums = [jnp.zeros((8, LANES), F32) for _ in range(chunks)]
+    weight = in_parts(weight)
     for block, rows in blocks(exp_ref.shape[0]):
         size = rows.stop - rows.start
         factor = column(weight, block, size)
@@ -237,14 +249,14 @@
 
 
 def weighted_rows(exp_ref, weight):
-    sums = jnp.zeros((8, LANES), F32)
+    sums = []
     for block, rows in blocks(exp_ref.shape[0]):
         part = jnp.zeros((rows.stop - rows.start, LANES), F32)
         for chunk in range(weight.shape[0]):
             values = exp_ref[rows, chunk * LANES : (chunk + 1) * LANES]
             part += values * weight[chunk : chunk + 1, :]
-        sums += turned(part, block, False)
-    return sums
+        sums.append(part)
+    return turned(sums, False)
 
 
 def row_kernel(first, exp_ref, factor_ref, col_ref, stud_row_ref, row_ref):
@@ -277,6 +289,7 @@
     lses = jnp.concatenate([early[USED:], late[USED:], jnp.zeros((2, LANES), F32)], axis=0)
     lses = lses - math.log(STUDENT_SCALE)
     lses = jnp.where(valid_ref[...] > 0.0, lses, -FAR_BELOW)
+    scale, lses = in_parts(scale), in_parts(lses)
     for block, rows in blocks(tokens):
         size = rows.stop - rows.start
         scale_ref[rows, :] = column(scale, block, size)

time: 157 us -> 156 us (level)
  no operation moved by 1% of the time
where the time goes in v4:
time: 156 us; the launch traced here: 155 us
  blocking collectives  60.9 us (39%)
  starting transfers between devices  35.4 us (23%)
  waiting for transfers between devices  32 us (21%)
  Pallas kernels  23.3 us (15%)
  other arithmetic  2.42 us (2%)
    all_to_all x5, blocking collectives, exchange(): return lax.all_to_all(parts, axis, 0, 0, tiled=True)  60.9 us
    all_to_all x3, waiting for transfers between devices, exchange(): return lax.all_to_all(parts, axis, 0, 0, tiled=True)  21.1 us
    pallas_call x13, Pallas kernels, call(): pl.pallas_call(kernel, out_shape=[jax.ShapeDtypeStruct(shape, dtype) for...  20.5 us
    all_to_all x3, starting transfers between devices, exchange(): return lax.all_to_all(parts, axis, 0, 0, tiled=True)  17.2 us
    ppermute x3, waiting for transfers between devices, on_device(): lines.append(lax.ppermute(pay, 'y', route))  7.74 us
    ppermute x3, starting transfers between devices, on_device(): lines.append(lax.ppermute(pay, 'y', route))  5.83 us
    ppermute x3, starting transfers between devices, on_device(): pairs_held.append(lax.ppermute(pair, 'proto', routes[-away % half]))  5.73 us
    ppermute x3, starting transfers between devices, on_device(): all_rows.append(lax.ppermute(rows, 'proto', routes[-away % half]))  3.63 us
  transfers between devices with their start and end apart: 18, of which 8 were waited for; matrix products, arithmetic and copies ran while one was open for 2% of the time, Pallas kernels for 5%

profile of v4, /device:TPU:32, one launch (start us, length us, event | category | flops | bytes accessed | tf_op | source)
XLA Modules:
  0.0 155.4 jit_solution(1746257727578358025)
XLA Ops:
  0.6 0.1 collective-permute-start.3
  1.4 2.7 %shard_map.68 = bf16[8,64,256]{2,1,0:T(8,128)(2,1)} custom-call(s32[1]{0:T(128)S(6)} %copy.7.count_ref, s32[1,512]{1,0:T(1,128)} %mask_ref.3, bf16[512,256]{1,0:T(8,128)(2,1)} %teacher_ref.1, bf16[512,256]{1,0:T(8,128)(2,1)} %student_ref.1), custom_call_target="tpu_custom_call" | custom-call | tf_op jit(solution)/shard_map/pallas_call | solution.py:403
  4.1 8.6 %all-to-all-start = ((bf16[8,64,256]{2,1,0:T(8,128)(2,1)}), bf16[8,64,256]{2,1,0:T(8,128)(2,1)S(1)}, u32[]{:S(2)}, u32[]{:S(2)}) async-start(bf16[8,64,256]{2,1,0:T(8,128)(2,1)} %shard_map.68), calls=%async_computation | async-start | bytes 524288 | tf_op jit(solution)/shard_map/all_to_all | solution.py:385
  12.7 0.0 collective-permute-done.3
  12.7 0.9 pad_maximum_fusion.refs_0_
  13.6 1.6 %collective-permute-start.6 = (bf16[2,256,256]{2,1,0:T(8,128)(2,1)S(1)}, bf16[2,256,256]{2,1,0:T(8,128)(2,1)S(1)}, u32[]{:S(2)}, u32[]{:S(2)}) collective-permute-start(bf16[2,256,256]{2,1,0:T(8,128)(2,1)S(1)} %pad_maximum_fusion.refs_0_), channel_id=1, source_target_pairs={{0,2},{1,3},{2,4},{3,5},{4,6},{5,7},{6,0},{7,1},{8,10},{9,11},{10,... | collective-permute-start | bytes 786440 | tf_op jit(solution)/shard_map/ppermute | solution.py:426
  15.2 2.7 %collective-permute-start.5 = (bf16[2,256,256]{2,1,0:T(8,128)(2,1)S(1)}, bf16[2,256,256]{2,1,0:T(8,128)(2,1)S(1)}, u32[]{:S(2)}, u32[]{:S(2)}) collective-permute-start(bf16[2,256,256]{2,1,0:T(8,128)(2,1)S(1)} %pad_maximum_fusion.refs_0_), channel_id=1, source_target_pairs={{0,4},{1,5},{2,6},{3,7},{4,0},{5,1},{6,2},{7,3},{8,12},{9,13},{10,... | collective-permute-start | bytes 786440 | tf_op jit(solution)/shard_map/ppermute | solution.py:426
  17.9 1.4 collective-permute-start.4
  19.4 4.4 %all-to-all-done.refs_1_ = bf16[8,64,256]{2,1,0:T(8,128)(2,1)S(1)} async-done(((bf16[8,64,256]{2,1,0:T(8,128)(2,1)}), bf16[8,64,256]{2,1,0:T(8,128)(2,1)S(1)}, u32[]{:S(2)}, u32[]{:S(2)}) %all-to-all-start) | async-done | bytes 262176 | tf_op jit(solution)/shard_map/all_to_all | solution.py:385
  23.8 1.6 %collective-permute-start.2 = (bf16[8,64,256]{2,1,0:T(8,128)(2,1)S(1)}, bf16[8,64,256]{2,1,0:T(8,128)(2,1)S(1)}, u32[]{:S(2)}, u32[]{:S(2)}) collective-permute-start(bf16[8,64,256]{2,1,0:T(8,128)(2,1)S(1)} %all-to-all-done.refs_1_), channel_id=1, source_target_pairs={{0,64},{64,128},{128,192},{192,0},{1,65},{65,129},{129,193},{193,1... | collective-permute-start | bytes 786440 | tf_op jit(solution)/shard_map/ppermute | solution.py:422
  25.4 2.9 %collective-permute-start.1 = (bf16[8,64,256]{2,1,0:T(8,128)(2,1)S(1)}, bf16[8,64,256]{2,1,0:T(8,128)(2,1)S(1)}, u32[]{:S(2)}, u32[]{:S(2)}) collective-permute-start(bf16[8,64,256]{2,1,0:T(8,128)(2,1)S(1)} %all-to-all-done.refs_1_), channel_id=1, source_target_pairs={{0,128},{64,192},{128,0},{192,64},{1,129},{65,193},{129,1},{193,65... | collective-permute-start | bytes 786440 | tf_op jit(solution)/shard_map/ppermute | solution.py:422
  28.3 0.0 collective-permute-done.6.refs_3_
  28.3 1.3 collective-permute-start
  29.6 0.1 pad_add_fusion.place_ref.refs_0_
  29.7 0.0 collective-permute-done.5.refs_2_
  29.7 0.0 collective-permute-done.4.refs_1_
  29.7 0.6 shard_map.69.refs_5_.refs_6_.protos_ref
  30.3 3.0 %collective-permute-done.2.refs_4_ = bf16[8,64,256]{2,1,0:T(8,128)(2,1)S(1)} collective-permute-done((bf16[8,64,256]{2,1,0:T(8,128)(2,1)S(1)}, bf16[8,64,256]{2,1,0:T(8,128)(2,1)S(1)}, u32[]{:S(2)}, u32[]{:S(2)}) %collective-permute-start.2) | collective-permute-done | bytes 262176 | tf_op jit(solution)/shard_map/ppermute | solution.py:422
  33.3 4.8 %collective-permute-done.1.refs_3_ = bf16[8,64,256]{2,1,0:T(8,128)(2,1)S(1)} collective-permute-done((bf16[8,64,256]{2,1,0:T(8,128)(2,1)S(1)}, bf16[8,64,256]{2,1,0:T(8,128)(2,1)S(1)}, u32[]{:S(2)}, u32[]{:S(2)}) %collective-permute-start.1) | collective-permute-done | bytes 262176 | tf_op jit(solution)/shard_map/ppermute | solution.py:422
  38.1 0.0 collective-permute-done.refs_2_
  38.1 3.7 %shard_map.70 = (bf16[528,256]{1,0:T(8,128)(2,1)S(1)}, f32[8,1024]{1,0:T(8,128)S(1)}, f32[8,128]{1,0:T(8,128)S(1)}, s32[8,128]{1,0:T(8,128)S(1)}, f32[8,16,128]{2,1,0:T(8,128)}) custom-call(s32[3]{0:T(128)S(1)} %pad_add_fusion.place_ref.refs_0_, bf16[8,64,256]{2,1,0:T(8,128)(2,1)S(1)} %all-to-all-done.refs_1_, ...), custom_call_target="tpu_custom_call" | custom-call | flops 553648128 | bytes 8650752 | tf_op jit(solution)/shard_map/pallas_call | solution.py:368
  41.8 4.3 %all-to-all-start.1 = ((f32[8,16,128]{2,1,0:T(8,128)}), f32[8,16,128]{2,1,0:T(8,128)S(1)}, u32[]{:S(2)}, u32[]{:S(2)}) async-start(f32[8,16,128]{2,1,0:T(8,128)} %get-tuple-element.23), calls=%async_computation.1 | async-start | bytes 131072 | tf_op jit(solution)/shard_map/all_to_all | solution.py:385
  46.1 3.2 %shard_map.71 = (bf16[528,256]{1,0:T(8,128)(2,1)S(1)}, f32[8,128]{1,0:T(8,128)S(1)}) custom-call(s32[3]{0:T(128)S(1)} %pad_add_fusion.place_ref.refs_0_, bf16[8,64,256]{2,1,0:T(8,128)(2,1)S(1)} %all-to-all-done.refs_1_, bf16[8,64,256]{2,1,0:T(8,128)(2,1)S(1)} %collective-permute-done.refs_2_, bf16[8,64,256]{2,1,0:T(8,128)(2,1)S(1)} %collective-permute-done.1.refs_3_, ...), custom_call_target="tpu_custom_call" | custom-call | flops 553648128 | bytes 8650752 | tf_op jit(solution)/shard_map/pallas_call | solution.py:368
  49.3 2.4 %all-to-all-done.1.col_ref = f32[8,16,128]{2,1,0:T(8,128)S(1)} async-done(((f32[8,16,128]{2,1,0:T(8,128)}), f32[8,16,128]{2,1,0:T(8,128)S(1)}, u32[]{:S(2)}, u32[]{:S(2)}) %all-to-all-start.1) | async-done | bytes 65568 | tf_op jit(solution)/shard_map/all_to_all | solution.py:385
  51.7 1.9 %shard_map.72 = (f32[528,2048]{1,0:T(8,128)S(1)}, f32[8,128]{1,0:T(8,128)S(1)}, f32[32,8,128]{2,1,0:T(8,128)S(1)}, f32[8,128]{1,0:T(8,128)S(1)}) custom-call(bf16[528,256]{1,0:T(8,128)(2,1)S(1)} %get-tuple-element.22.teach_ref, bf16[2048,256]{1,0:T(8,128)(2,1)S(1)} %shard_map.69.refs_5_.refs_6_.protos_ref, f32[8,16,128]{2,1,0:T(8,128)S(1)} %all-to-all-done.1.col_ref, ...), custom_call_target="tpu_custom_call" | custom-call | flops 553648128 | bytes 8650752 | tf_op jit(solution)/shard_map/pallas_call | solution.py:368
  53.6 17.0 %all_to_all.40.row_ref = f32[32,8,128]{2,1,0:T(8,128)S(1)} all-to-all(f32[32,8,128]{2,1,0:T(8,128)S(1)} %get-tuple-element.29), channel_id=1, replica_groups=mesh['y'=4,'z'=8,'proto'=8] {'y','z'}, dimensions={0} | all-to-all | bytes 262144 | tf_op jit(solution)/shard_map/all_to_all | solution.py:385
  70.6 0.7 shard_map.73
  71.3 8.1 %all_to_all.41.col_ref = f32[8,16,128]{2,1,0:T(8,128)S(1)} all-to-all(f32[8,16,128]{2,1,0:T(8,128)S(1)} %get-tuple-element.31), channel_id=1, replica_groups=mesh['y'=4,'z'=8,'proto'=8] {'proto'}, dimensions={0} | all-to-all | bytes 131072 | tf_op jit(solution)/shard_map/all_to_all | solution.py:385
  79.4 0.6 shard_map.74
  80.0 13.9 %all_to_all.42.row_ref.early_ref = f32[32,8,128]{2,1,0:T(8,128)S(1)} all-to-all(f32[32,8,128]{2,1,0:T(8,128)S(1)} %shard_map.74), channel_id=1, replica_groups=mesh['y'=4,'z'=8,'proto'=8] {'y','z'}, dimensions={0} | all-to-all | bytes 262144 | tf_op jit(solution)/shard_map/all_to_all | solution.py:385
  93.9 0.6 shard_map.75
  94.5 8.0 %all_to_all.43.col_ref = f32[8,16,128]{2,1,0:T(8,128)S(1)} all-to-all(f32[8,16,128]{2,1,0:T(8,128)S(1)} %shard_map.75), channel_id=1, replica_groups=mesh['y'=4,'z'=8,'proto'=8] {'proto'}, dimensions={0} | all-to-all | bytes 131072 | tf_op jit(solution)/shard_map/all_to_all | solution.py:385
  102.5 0.6 shard_map.76
  103.2 13.9 %all_to_all.44.row_ref = f32[32,8,128]{2,1,0:T(8,128)S(1)} all-to-all(f32[32,8,128]{2,1,0:T(8,128)S(1)} %shard_map.76), channel_id=1, replica_groups=mesh['y'=4,'z'=8,'proto'=8] {'y','z'}, dimensions={0} | all-to-all | bytes 262144 | tf_op jit(solution)/shard_map/all_to_all | solution.py:385
  117.0 3.9 %shard_map.77 = (bf16[32,32,256]{2,1,0:T(8,128)(2,1)}, bf16[528,2048]{1,0:T(8,128)(2,1)S(1)}) custom-call(s32[8,128]{1,0:T(8,128)S(1)} %get-tuple-element.21.base_ref, f32[528,2048]{1,0:T(8,128)S(1)} %get-tuple-element.26.exp_ref, f32[8,128]{1,0:T(8,128)S(1)} %get-tuple-element.30.factor_ref, f32[8,128]{1,0:T(8,128)S(1)} %get-tuple-element.28.valid_ref, ...), custom_call_target="tpu_custom_call" | custom-call | flops 553648128 | bytes 8650752 | tf_op jit(solution)/shard_map/pallas_call | solution.py:368
  120.9 0.0 copy-start
  121.0 1.6 %shard_map.78 = (f32[4,256,256]{2,1,0:T(8,128)S(1)}, f32[4,256,256]{2,1,0:T(8,128)S(1)}) custom-call(s32[3]{0:T(128)S(1)} %pad_add_fusion.place_ref.refs_0_, bf16[528,2048]{1,0:T(8,128)(2,1)S(1)} %get-tuple-element.34.grad_ref, bf16[528,256]{1,0:T(8,128)(2,1)S(1)} %get-tuple-element.33.stud_ref), custom_call_target="tpu_custom_call" | custom-call | flops 553648128 | bytes 8650752 | tf_op jit(solution)/shard_map/pallas_call | solution.py:368
  122.6 0.1 collective-permute-start.7
  122.7 4.3 %all-to-all-start.7 = ((bf16[32,32,256]{2,1,0:T(8,128)(2,1)}), bf16[32,32,256]{2,1,0:T(8,128)(2,1)S(1)}, u32[]{:S(2)}, u32[]{:S(2)}) async-start(bf16[32,32,256]{2,1,0:T(8,128)(2,1)} %get-tuple-element.38), calls=%async_computation.7 | async-start | bytes 1048576 | tf_op jit(solution)/shard_map/all_to_all | solution.py:385
  127.0 0.0 collective-permute-done.7
  127.0 1.4 add.7.near_ref
  128.4 0.1 slice_bitcast_fusion
  128.5 1.2 collective-permute-start.10
  129.7 1.5 collective-permute-start.9
  131.2 0.0 collective-permute-start.8
  131.2 14.3 %all-to-all-done.7.parts_ref = bf16[32,32,256]{2,1,0:T(8,128)(2,1)S(1)} async-done(((bf16[32,32,256]{2,1,0:T(8,128)(2,1)}), bf16[32,32,256]{2,1,0:T(8,128)(2,1)S(1)}, u32[]{:S(2)}, u32[]{:S(2)}) %all-to-all-start.7) | async-done | bytes 524320 | tf_op jit(solution)/shard_map/all_to_all | solution.py:385
  145.5 0.1 shard_map.80
  145.6 0.1 collective-permute-start.11
  145.7 1.2 collective-permute-done.11
  146.9 0.6 collective-permute-start.14
  147.4 2.1 %collective-permute-start.13 = (f32[2,32,256]{2,1,0:T(8,128)S(1)}, f32[2,32,256]{2,1,0:T(8,128)S(1)}, u32[]{:S(2)}, u32[]{:S(2)}) collective-permute-start(f32[2,32,256]{2,1,0:T(8,128)S(1)} %pad_maximum_fusion.1.refs_0_), channel_id=1, source_target_pairs={{0,4},{1,5},{2,6},{3,7},{4,0},{5,1},{6,2},{7,3},{8,12},{9,13},{10,... | collective-permute-start | bytes 196616 | tf_op jit(solution)/shard_map/ppermute | solution.py:505
  149.5 0.0 collective-permute-done.10.refs_2_
  149.5 1.0 collective-permute-start.12
  150.5 0.0 collective-permute-done.9.refs_1_
  150.5 0.0 collective-permute-done.8.refs_0_
  150.5 0.0 copy-done
  150.5 1.8 %shard_map.79 = (bf16[512,256]{1,0:T(8,128)(2,1)S(1)}, f32[256,256]{1,0:T(8,128)}) custom-call(s32[3]{0:T(128)S(1)} %pad_add_fusion.place_ref.refs_0_, s32[1]{0:T(128)S(6)} %copy.7.count_ref, s32[1,512]{1,0:T(1,128)S(1)} %copy-done, f32[4,256,256]{2,1,0:T(8,128)S(1)} %add.7.near_ref, f32[256,256]{1,0:T(8,128)S(1)} %collective-permute-done.8.refs_0_, ...), custom_call_target="tpu_custom_call" | custom-call | tf_op jit(solution)/shard_map/pallas_call | solution.py:368
  152.4 1.3 collective-permute-done.14.refs_3_
  153.7 0.0 collective-permute-done.13.refs_2_
  153.7 0.6 collective-permute-done.12.refs_1_
  154.2 1.2 shard_map.81
  (1 shorter events, 0.0 us)
Async XLA Ops:
  0.6 12.1 %collective-permute-start.3 = (bf16[256,256]{1,0:T(8,128)(2,1)}, bf16[256,256]{1,0:T(8,128)(2,1)S(1)}, u32[]{:S(2)}, u32[]{:S(2)}) collective-permute-start(bf16[256,256]{1,0:T(8,128)(2,1)} %param.7), channel_id=1, source_target_pairs={{0,1},{1,0},{2,3},{3,2},{4,5},{5,4},{6,7},{7,6},{8,9},{9,8},{10,11... | collective-permute-start | bytes 393224 | tf_op jit(solution)/shard_map/ppermute | solution.py:423
  4.1 19.7 %all-to-all-start = ((bf16[8,64,256]{2,1,0:T(8,128)(2,1)}), bf16[8,64,256]{2,1,0:T(8,128)(2,1)S(1)}, u32[]{:S(2)}, u32[]{:S(2)}) async-start(bf16[8,64,256]{2,1,0:T(8,128)(2,1)} %shard_map.68), calls=%async_computation | async-start | bytes 524288 | tf_op jit(solution)/shard_map/all_to_all | solution.py:385
  13.6 14.6 %collective-permute-start.6 = (bf16[2,256,256]{2,1,0:T(8,128)(2,1)S(1)}, bf16[2,256,256]{2,1,0:T(8,128)(2,1)S(1)}, u32[]{:S(2)}, u32[]{:S(2)}) collective-permute-start(bf16[2,256,256]{2,1,0:T(8,128)(2,1)S(1)} %pad_maximum_fusion.refs_0_), channel_id=1, source_target_pairs={{0,2},{1,3},{2,4},{3,5},{4,6},{5,7},{6,0},{7,1},{8,10},{9,11},{10,... | collective-permute-start | bytes 786440 | tf_op jit(solution)/shard_map/ppermute | solution.py:426
  15.2 14.5 %collective-permute-start.5 = (bf16[2,256,256]{2,1,0:T(8,128)(2,1)S(1)}, bf16[2,256,256]{2,1,0:T(8,128)(2,1)S(1)}, u32[]{:S(2)}, u32[]{:S(2)}) collective-permute-start(bf16[2,256,256]{2,1,0:T(8,128)(2,1)S(1)} %pad_maximum_fusion.refs_0_), channel_id=1, source_target_pairs={{0,4},{1,5},{2,6},{3,7},{4,0},{5,1},{6,2},{7,3},{8,12},{9,13},{10,... | collective-permute-start | bytes 786440 | tf_op jit(solution)/shard_map/ppermute | solution.py:426
  17.9 11.8 %collective-permute-start.4 = (bf16[2,256,256]{2,1,0:T(8,128)(2,1)S(1)}, bf16[2,256,256]{2,1,0:T(8,128)(2,1)S(1)}, u32[]{:S(2)}, u32[]{:S(2)}) collective-permute-start(bf16[2,256,256]{2,1,0:T(8,128)(2,1)S(1)} %pad_maximum_fusion.refs_0_), channel_id=1, source_target_pairs={{0,6},{1,7},{2,0},{3,1},{4,2},{5,3},{6,4},{7,5},{8,14},{9,15},{10,... | collective-permute-start | bytes 786440 | tf_op jit(solution)/shard_map/ppermute | solution.py:426
  23.8 9.5 %collective-permute-start.2 = (bf16[8,64,256]{2,1,0:T(8,128)(2,1)S(1)}, bf16[8,64,256]{2,1,0:T(8,128)(2,1)S(1)}, u32[]{:S(2)}, u32[]{:S(2)}) collective-permute-start(bf16[8,64,256]{2,1,0:T(8,128)(2,1)S(1)} %all-to-all-done.refs_1_), channel_id=1, source_target_pairs={{0,64},{64,128},{128,192},{192,0},{1,65},{65,129},{129,193},{193,1... | collective-permute-start | bytes 786440 | tf_op jit(solution)/shard_map/ppermute | solution.py:422
  25.4 12.7 %collective-permute-start.1 = (bf16[8,64,256]{2,1,0:T(8,128)(2,1)S(1)}, bf16[8,64,256]{2,1,0:T(8,128)(2,1)S(1)}, u32[]{:S(2)}, u32[]{:S(2)}) collective-permute-start(bf16[8,64,256]{2,1,0:T(8,128)(2,1)S(1)} %all-to-all-done.refs_1_), channel_id=1, source_target_pairs={{0,128},{64,192},{128,0},{192,64},{1,129},{65,193},{129,1},{193,65... | collective-permute-start | bytes 786440 | tf_op jit(solution)/shard_map/ppermute | solution.py:422
  28.3 9.8 %collective-permute-start = (bf16[8,64,256]{2,1,0:T(8,128)(2,1)S(1)}, bf16[8,64,256]{2,1,0:T(8,128)(2,1)S(1)}, u32[]{:S(2)}, u32[]{:S(2)}) collective-permute-start(bf16[8,64,256]{2,1,0:T(8,128)(2,1)S(1)} %all-to-all-done.refs_1_), channel_id=1, source_target_pairs={{0,192},{64,0},{128,64},{192,128},{1,193},{65,1},{129,65},{193,129... | collective-permute-start | bytes 786440 | tf_op jit(solution)/shard_map/ppermute | solution.py:422
  41.8 9.9 %all-to-all-start.1 = ((f32[8,16,128]{2,1,0:T(8,128)}), f32[8,16,128]{2,1,0:T(8,128)S(1)}, u32[]{:S(2)}, u32[]{:S(2)}) async-start(f32[8,16,128]{2,1,0:T(8,128)} %get-tuple-element.23), calls=%async_computation.1 | async-start | bytes 131072 | tf_op jit(solution)/shard_map/all_to_all | solution.py:385
  120.9 29.6 %copy-start = (s32[1,512]{1,0:T(1,128)S(1)}, s32[1,512]{1,0:T(1,128)}, u32[]{:S(2)}) copy-start(s32[1,512]{1,0:T(1,128)} %mask_ref.3) | copy-start | bytes 6148
  122.6 4.4 %collective-permute-start.7 = (f32[4,256,256]{2,1,0:T(8,128)S(1)}, f32[4,256,256]{2,1,0:T(8,128)}, u32[]{:S(2)}, u32[]{:S(2)}) collective-permute-start(f32[4,256,256]{2,1,0:T(8,128)S(1)} %get-tuple-element.36), channel_id=1, source_target_pairs={{0,1},{1,0},{2,3},{3,2},{4,5},{5,4},{6,7},{7,6},{8,9},{9,8},{10,11... | collective-permute-start | bytes 3145736 | tf_op jit(solution)/shard_map/ppermute | solution.py:499
  122.7 22.8 %all-to-all-start.7 = ((bf16[32,32,256]{2,1,0:T(8,128)(2,1)}), bf16[32,32,256]{2,1,0:T(8,128)(2,1)S(1)}, u32[]{:S(2)}, u32[]{:S(2)}) async-start(bf16[32,32,256]{2,1,0:T(8,128)(2,1)} %get-tuple-element.38), calls=%async_computation.7 | async-start | bytes 1048576 | tf_op jit(solution)/shard_map/all_to_all | solution.py:385
  128.5 21.0 %collective-permute-start.10 = (f32[256,256]{1,0:T(8,128)S(1)}, f32[256,256]{1,0:T(8,128)S(1)}, u32[]{:S(2)}, u32[]{:S(2)}) collective-permute-start(f32[256,256]{1,0:T(8,128)S(1)} %get-tuple-element.40), channel_id=1, source_target_pairs={{0,6},{1,7},{2,0},{3,1},{4,2},{5,3},{6,4},{7,5},{8,14},{9,15},{10,... | collective-permute-start | bytes 786440 | tf_op jit(solution)/shard_map/ppermute | solution.py:500
  129.7 20.8 %collective-permute-start.9 = (f32[256,256]{1,0:T(8,128)S(1)}, f32[256,256]{1,0:T(8,128)S(1)}, u32[]{:S(2)}, u32[]{:S(2)}) collective-permute-start(f32[256,256]{1,0:T(8,128)S(1)} %get-tuple-element.41), channel_id=1, source_target_pairs={{0,4},{1,5},{2,6},{3,7},{4,0},{5,1},{6,2},{7,3},{8,12},{9,13},{10,... | collective-permute-start | bytes 786440 | tf_op jit(solution)/shard_map/ppermute | solution.py:500
  131.2 19.3 %collective-permute-start.8 = (f32[256,256]{1,0:T(8,128)S(1)}, f32[256,256]{1,0:T(8,128)S(1)}, u32[]{:S(2)}, u32[]{:S(2)}) collective-permute-start(f32[256,256]{1,0:T(8,128)S(1)} %get-tuple-element.42), channel_id=1, source_target_pairs={{0,2},{1,3},{2,4},{3,5},{4,6},{5,7},{6,0},{7,1},{8,10},{9,11},{10,... | collective-permute-start | bytes 786440 | tf_op jit(solution)/shard_map/ppermute | solution.py:500
  145.6 1.3 collective-permute-start.11
  146.9 6.8 %collective-permute-start.14 = (f32[2,32,256]{2,1,0:T(8,128)S(1)}, f32[2,32,256]{2,1,0:T(8,128)S(1)}, u32[]{:S(2)}, u32[]{:S(2)}) collective-permute-start(f32[2,32,256]{2,1,0:T(8,128)S(1)} %pad_maximum_fusion.1.refs_0_), channel_id=1, source_target_pairs={{0,2},{1,3},{2,4},{3,5},{4,6},{5,7},{6,0},{7,1},{8,10},{9,11},{10,... | collective-permute-start | bytes 196616 | tf_op jit(solution)/shard_map/ppermute | solution.py:505
  147.4 6.2 %collective-permute-start.13 = (f32[2,32,256]{2,1,0:T(8,128)S(1)}, f32[2,32,256]{2,1,0:T(8,128)S(1)}, u32[]{:S(2)}, u32[]{:S(2)}) collective-permute-start(f32[2,32,256]{2,1,0:T(8,128)S(1)} %pad_maximum_fusion.1.refs_0_), channel_id=1, source_target_pairs={{0,4},{1,5},{2,6},{3,7},{4,0},{5,1},{6,2},{7,3},{8,12},{9,13},{10,... | collective-permute-start | bytes 196616 | tf_op jit(solution)/shard_map/ppermute | solution.py:505
  149.5 4.7 %collective-permute-start.12 = (f32[2,32,256]{2,1,0:T(8,128)S(1)}, f32[2,32,256]{2,1,0:T(8,128)S(1)}, u32[]{:S(2)}, u32[]{:S(2)}) collective-permute-start(f32[2,32,256]{2,1,0:T(8,128)S(1)} %pad_maximum_fusion.1.refs_0_), channel_id=1, source_target_pairs={{0,6},{1,7},{2,0},{3,1},{4,2},{5,3},{6,4},{7,5},{8,14},{9,15},{10,... | collective-permute-start | bytes 196616 | tf_op jit(solution)/shard_map/ppermute | solution.py:505

commit v5 on v4

--- a/solution.py
+++ b/solution.py
@@ -278,8 +278,8 @@
 
 
 def gradient_kernel(
-    base_ref, exp_ref, factor_ref, valid_ref, col_ref, early_ref, row_ref, stud_ref, protos_ref,
-    tok_ref, grad_ref, score_ref, scale_ref, lse_ref, total_ref,
+    place_ref, base_ref, exp_ref, factor_ref, valid_ref, col_ref, early_ref, row_ref, stud_ref, protos_ref,
+    tok_ref, near_ref, far_ref, grad_ref, part_ref, weight_ref, score_ref, scale_ref, lse_ref, total_ref,
 ):
     tokens, width = stud_ref.shape
     weights = 1.0 / jnp.sum(col_ref[...], axis=0)
@@ -295,17 +295,41 @@
         scale_ref[rows, :] = column(scale, block, size)
         lse_ref[rows, :] = column(lses, block, size)
     step = 2 * LANES
-    for chunk in range(protos_ref.shape[0] // step):
-        slot = chunk % 2
-        score_ref[slot] = dot_nt(stud_ref[...], protos_ref[chunk * step : (chunk + 1) * step, :])
+    group = place_ref[0]
+    for owner in range(PROTO):
+        weight_ref[owner, :, :] = weights[2 * owner : 2 * owner + 2, :]
+    starts = []
+    for away in range(PROTO):
+        x = lax.rem(group // 2 + away, PROTO // 2)
+        core = lax.rem(group + (1 if away < PROTO // 2 else 0), 2)
+        starts.append(pl.multiple_of((2 * x + core) * step, step))
+
+    def score(away):
+        score_ref[away % 2] = dot_nt(stud_ref[...], protos_ref[pl.ds(starts[away], step), :])
+
+    def product(away):
+        out_ref = far_ref if away < PROTO // 2 else near_ref
+        out_ref[away % (PROTO // 2), :, :] = dot_tn(part_ref[away % 2], stud_ref[...])
+
+    score(0)
+    for away in range(PROTO):
+        if away + 1 < PROTO:
+            score(away + 1)
+        if away:
+            product(away - 1)
+        slot = away % 2
+        weight = weight_ref[lax.div(starts[away], step)]
         for half in range(2):
-            index = 2 * chunk + half
-            lanes = slice(index * LANES, (index + 1) * LANES)
+            lanes = pl.ds(starts[away] + half * LANES, LANES)
+            here = slice(half * LANES, (half + 1) * LANES)
             for _, rows in blocks(tokens):
-                part = score_ref[slot, rows, half * LANES : (half + 1) * LANES] * STUDENT_SCALE
+                part = score_ref[slot, rows, here] * STUDENT_SCALE
                 student = jnp.exp(part - lse_ref[rows, :])
-                target = exp_ref[rows, lanes] * scale_ref[rows, :] * weights[index : index + 1, :]
-                grad_ref[rows, lanes] = (student - target).astype(BF16)
+                target = exp_ref[rows, lanes] * scale_ref[rows, :] * weight[half : half + 1, :]
+                grads = (student - target).astype(BF16)
+                part_ref[slot, rows, here] = grads
+                grad_ref[rows, lanes] = grads
+    product(PROTO - 1)
     total_ref[:tokens, :] = dot_nn(grad_ref[...], protos_ref[...])
     total_ref[tokens:, :] = jnp.zeros((SLOTS, width), F32)
     for device in range(tok_ref.shape[0]):
@@ -313,18 +337,6 @@
         start = pl.multiple_of(base // 8 * 8, 8)
         rows = pltpu.roll(total_ref[pl.ds(start, SLOTS + 8), :], SLOTS + 8 - base % 8, 0)
         tok_ref[device, :, :] = rows[:SLOTS, :].astype(BF16)
-
-
-def proto_kernel(place_ref, grad_ref, stud_ref, near_ref, far_ref):
-    share = near_ref.shape[1]
-    group = place_ref[0]
-    for away in range(PROTO // 2):
-        x = lax.rem(group // 2 + away, PROTO // 2)
-        core = lax.rem(group, 2)
-        start = pl.multiple_of((2 * x + 1 - core) * share, share)
-        far_ref[away, :, :] = dot_tn(grad_ref[:, pl.ds(start, share)], stud_ref[...])
-        start = pl.multiple_of((2 * x + core) * share, share)
-        near_ref[away, :, :] = dot_tn(grad_ref[:, pl.ds(start, share)], stud_ref[...])
 
 
 def sum_kernel(parts_ref, out_ref):
@@ -353,13 +365,15 @@
 def spread_kernel(onehot_ref, *refs):
     *row_refs, out_ref = refs
     rest = jnp.concatenate([ref[i] for ref in row_refs for i in range(2)], axis=0)
-    total = None
+    parts = []
     for _ in range(3):
         part = rest.astype(BF16)
         rest = rest - part.astype(F32)
-        moved = dot_nn(onehot_ref[...], part)
-        total = moved if total is None else total + moved
-    out_ref[...] = total
+        parts.append(part)
+    onehot = onehot_ref[...]
+    out_ref[...] = dot_nn(
+        jnp.concatenate([onehot] * 3, axis=1), jnp.concatenate(parts, axis=0)
+    )
 
 
 def call(kernel, outs, inputs, scalars=0, scratch=(), cost=None):
@@ -476,24 +490,24 @@
         functools.partial(row_kernel, 8 - USED), [row_out], (exps, factor, col, stud_row)
     )
     row = exchange(row, TOK)
-    grad_slots, grads = call(
+    grad_slots, near, far = call(
         gradient_kernel,
-        [((devices, SLOTS, width), BF16), ((tokens, protos_held), BF16)],
-        (base, exps, factor, valid, col, early, row, stud, protos),
-        scalars=1,
+        [
+            ((devices, SLOTS, width), BF16),
+            ((half, share, width), F32),
+            ((half, share, width), F32),
+        ],
+        (place, base, exps, factor, valid, col, early, row, stud, protos),
+        scalars=2,
         scratch=(
+            pltpu.VMEM((tokens, protos_held), BF16),
+            pltpu.VMEM((2, tokens, 2 * LANES), BF16),
+            pltpu.VMEM((PROTO, 2, LANES), F32),
             pltpu.VMEM((2, tokens, 2 * LANES), F32),
             pltpu.VMEM((tokens, LANES), F32),
             pltpu.VMEM((tokens, LANES), F32),
             pltpu.VMEM((tokens + SLOTS, width), F32),
         ),
-        cost=work,
-    )
-    near, far = call(
-        proto_kernel,
-        [((half, share, width), F32), ((half, share, width), F32)],
-        (place, grads, stud),
-        scalars=1,
         cost=work,
     )
     mine = near + lax.ppermute(far, "proto", swap)

time: 156 us -> 156 us (level)
    pallas_call x13 -> x12, Pallas kernels: 20.5 us -> 20.4 us  [call(): pl.pallas_call(kernel, out_shape=[jax.ShapeDtypeStruct(shape, dtype) for...]
where the time goes in v5:
time: 156 us; the launch traced here: 155 us
  blocking collectives  60.9 us (39%)
  starting transfers between devices  35.4 us (23%)
  waiting for transfers between devices  31.1 us (20%)
  Pallas kernels  23.1 us (15%)
  other arithmetic  2.37 us (2%)
    all_to_all x5, blocking collectives, exchange(): return lax.all_to_all(parts, axis, 0, 0, tiled=True)  60.9 us
    pallas_call x12, Pallas kernels, call(): pl.pallas_call(kernel, out_shape=[jax.ShapeDtypeStruct(shape, dtype) for...  20.4 us
    all_to_all x3, waiting for transfers between devices, exchange(): return lax.all_to_all(parts, axis, 0, 0, tiled=True)  20.3 us
    all_to_all x3, starting transfers between devices, exchange(): return lax.all_to_all(parts, axis, 0, 0, tiled=True)  17.4 us
    ppermute x3, waiting for transfers between devices, on_device(): lines.append(lax.ppermute(pay, 'y', route))  7.74 us
    ppermute x3, starting transfers between devices, on_device(): lines.append(lax.ppermute(pay, 'y', route))  5.83 us
    ppermute x3, starting transfers between devices, on_device(): pairs_held.append(lax.ppermute(pair, 'proto', routes[-away % half]))  5.73 us
    ppermute x3, starting transfers between devices, on_device(): all_rows.append(lax.ppermute(rows, 'proto', routes[-away % half]))  3.62 us
  transfers between devices with their start and end apart: 18, of which 8 were waited for; matrix products, arithmetic and copies ran while one was open for 2% of the time, Pallas kernels for 5%

profile of v5, /device:TPU:32, one launch (start us, length us, event | category | flops | bytes accessed | tf_op | source)
XLA Modules:
  0.0 155.4 jit_solution(13790944291598257954)
XLA Ops:
  0.6 0.1 collective-permute-start.3
  1.4 2.7 %shard_map.68 = bf16[8,64,256]{2,1,0:T(8,128)(2,1)} custom-call(s32[1]{0:T(128)S(6)} %copy.7.count_ref, s32[1,512]{1,0:T(1,128)} %mask_ref.3, bf16[512,256]{1,0:T(8,128)(2,1)} %teacher_ref.1, bf16[512,256]{1,0:T(8,128)(2,1)} %student_ref.1), custom_call_target="tpu_custom_call" | custom-call | tf_op jit(solution)/shard_map/pallas_call | solution.py:417
  4.1 8.6 %all-to-all-start = ((bf16[8,64,256]{2,1,0:T(8,128)(2,1)}), bf16[8,64,256]{2,1,0:T(8,128)(2,1)S(1)}, u32[]{:S(2)}, u32[]{:S(2)}) async-start(bf16[8,64,256]{2,1,0:T(8,128)(2,1)} %shard_map.68), calls=%async_computation | async-start | bytes 524288 | tf_op jit(solution)/shard_map/all_to_all | solution.py:399
  12.7 0.0 collective-permute-done.3
  12.7 0.9 pad_maximum_fusion.refs_0_
  13.6 1.6 %collective-permute-start.6 = (bf16[2,256,256]{2,1,0:T(8,128)(2,1)S(1)}, bf16[2,256,256]{2,1,0:T(8,128)(2,1)S(1)}, u32[]{:S(2)}, u32[]{:S(2)}) collective-permute-start(bf16[2,256,256]{2,1,0:T(8,128)(2,1)S(1)} %pad_maximum_fusion.refs_0_), channel_id=1, source_target_pairs={{0,2},{1,3},{2,4},{3,5},{4,6},{5,7},{6,0},{7,1},{8,10},{9,11},{10,... | collective-permute-start | bytes 786440 | tf_op jit(solution)/shard_map/ppermute | solution.py:440
  15.2 2.7 %collective-permute-start.5 = (bf16[2,256,256]{2,1,0:T(8,128)(2,1)S(1)}, bf16[2,256,256]{2,1,0:T(8,128)(2,1)S(1)}, u32[]{:S(2)}, u32[]{:S(2)}) collective-permute-start(bf16[2,256,256]{2,1,0:T(8,128)(2,1)S(1)} %pad_maximum_fusion.refs_0_), channel_id=1, source_target_pairs={{0,4},{1,5},{2,6},{3,7},{4,0},{5,1},{6,2},{7,3},{8,12},{9,13},{10,... | collective-permute-start | bytes 786440 | tf_op jit(solution)/shard_map/ppermute | solution.py:440
  17.9 1.4 collective-permute-start.4
  19.4 4.4 %all-to-all-done.refs_1_ = bf16[8,64,256]{2,1,0:T(8,128)(2,1)S(1)} async-done(((bf16[8,64,256]{2,1,0:T(8,128)(2,1)}), bf16[8,64,256]{2,1,0:T(8,128)(2,1)S(1)}, u32[]{:S(2)}, u32[]{:S(2)}) %all-to-all-start) | async-done | bytes 262176 | tf_op jit(solution)/shard_map/all_to_all | solution.py:399
  23.8 1.6 %collective-permute-start.2 = (bf16[8,64,256]{2,1,0:T(8,128)(2,1)S(1)}, bf16[8,64,256]{2,1,0:T(8,128)(2,1)S(1)}, u32[]{:S(2)}, u32[]{:S(2)}) collective-permute-start(bf16[8,64,256]{2,1,0:T(8,128)(2,1)S(1)} %all-to-all-done.refs_1_), channel_id=1, source_target_pairs={{0,64},{64,128},{128,192},{192,0},{1,65},{65,129},{129,193},{193,1... | collective-permute-start | bytes 786440 | tf_op jit(solution)/shard_map/ppermute | solution.py:436
  25.4 2.9 %collective-permute-start.1 = (bf16[8,64,256]{2,1,0:T(8,128)(2,1)S(1)}, bf16[8,64,256]{2,1,0:T(8,128)(2,1)S(1)}, u32[]{:S(2)}, u32[]{:S(2)}) collective-permute-start(bf16[8,64,256]{2,1,0:T(8,128)(2,1)S(1)} %all-to-all-done.refs_1_), channel_id=1, source_target_pairs={{0,128},{64,192},{128,0},{192,64},{1,129},{65,193},{129,1},{193,65... | collective-permute-start | bytes 786440 | tf_op jit(solution)/shard_map/ppermute | solution.py:436
  28.3 0.0 collective-permute-done.6.refs_3_
  28.3 1.3 collective-permute-start
  29.6 0.1 pad_add_fusion.place_ref.refs_0_
  29.7 0.0 collective-permute-done.5.refs_2_
  29.7 0.0 collective-permute-done.4.refs_1_
  29.7 0.6 shard_map.69.refs_5_.refs_6_.protos_ref
  30.3 3.0 %collective-permute-done.2.refs_4_ = bf16[8,64,256]{2,1,0:T(8,128)(2,1)S(1)} collective-permute-done((bf16[8,64,256]{2,1,0:T(8,128)(2,1)S(1)}, bf16[8,64,256]{2,1,0:T(8,128)(2,1)S(1)}, u32[]{:S(2)}, u32[]{:S(2)}) %collective-permute-start.2) | collective-permute-done | bytes 262176 | tf_op jit(solution)/shard_map/ppermute | solution.py:436
  33.3 4.8 %collective-permute-done.1.refs_3_ = bf16[8,64,256]{2,1,0:T(8,128)(2,1)S(1)} collective-permute-done((bf16[8,64,256]{2,1,0:T(8,128)(2,1)S(1)}, bf16[8,64,256]{2,1,0:T(8,128)(2,1)S(1)}, u32[]{:S(2)}, u32[]{:S(2)}) %collective-permute-start.1) | collective-permute-done | bytes 262176 | tf_op jit(solution)/shard_map/ppermute | solution.py:436
  38.1 0.0 collective-permute-done.refs_2_
  38.1 3.7 %shard_map.70 = (bf16[528,256]{1,0:T(8,128)(2,1)S(1)}, f32[8,1024]{1,0:T(8,128)S(1)}, f32[8,128]{1,0:T(8,128)S(1)}, s32[8,128]{1,0:T(8,128)S(1)}, f32[8,16,128]{2,1,0:T(8,128)}) custom-call(s32[3]{0:T(128)S(1)} %pad_add_fusion.place_ref.refs_0_, bf16[8,64,256]{2,1,0:T(8,128)(2,1)S(1)} %all-to-all-done.refs_1_, ...), custom_call_target="tpu_custom_call" | custom-call | flops 553648128 | bytes 8650752 | tf_op jit(solution)/shard_map/pallas_call | solution.py:382
  41.8 4.3 %all-to-all-start.1 = ((f32[8,16,128]{2,1,0:T(8,128)}), f32[8,16,128]{2,1,0:T(8,128)S(1)}, u32[]{:S(2)}, u32[]{:S(2)}) async-start(f32[8,16,128]{2,1,0:T(8,128)} %get-tuple-element.22), calls=%async_computation.1 | async-start | bytes 131072 | tf_op jit(solution)/shard_map/all_to_all | solution.py:399
  46.1 3.2 %shard_map.71 = (bf16[528,256]{1,0:T(8,128)(2,1)S(1)}, f32[8,128]{1,0:T(8,128)S(1)}) custom-call(s32[3]{0:T(128)S(1)} %pad_add_fusion.place_ref.refs_0_, bf16[8,64,256]{2,1,0:T(8,128)(2,1)S(1)} %all-to-all-done.refs_1_, bf16[8,64,256]{2,1,0:T(8,128)(2,1)S(1)} %collective-permute-done.refs_2_, bf16[8,64,256]{2,1,0:T(8,128)(2,1)S(1)} %collective-permute-done.1.refs_3_, ...), custom_call_target="tpu_custom_call" | custom-call | flops 553648128 | bytes 8650752 | tf_op jit(solution)/shard_map/pallas_call | solution.py:382
  49.3 2.4 %all-to-all-done.1.col_ref = f32[8,16,128]{2,1,0:T(8,128)S(1)} async-done(((f32[8,16,128]{2,1,0:T(8,128)}), f32[8,16,128]{2,1,0:T(8,128)S(1)}, u32[]{:S(2)}, u32[]{:S(2)}) %all-to-all-start.1) | async-done | bytes 65568 | tf_op jit(solution)/shard_map/all_to_all | solution.py:399
  51.7 1.8 %shard_map.72 = (f32[528,2048]{1,0:T(8,128)S(1)}, f32[8,128]{1,0:T(8,128)S(1)}, f32[32,8,128]{2,1,0:T(8,128)S(1)}, f32[8,128]{1,0:T(8,128)S(1)}) custom-call(bf16[528,256]{1,0:T(8,128)(2,1)S(1)} %get-tuple-element.21.teach_ref, bf16[2048,256]{1,0:T(8,128)(2,1)S(1)} %shard_map.69.refs_5_.refs_6_.protos_ref, f32[8,16,128]{2,1,0:T(8,128)S(1)} %all-to-all-done.1.col_ref, ...), custom_call_target="tpu_custom_call" | custom-call | flops 553648128 | bytes 8650752 | tf_op jit(solution)/shard_map/pallas_call | solution.py:382
  53.5 17.0 %all_to_all.40.row_ref = f32[32,8,128]{2,1,0:T(8,128)S(1)} all-to-all(f32[32,8,128]{2,1,0:T(8,128)S(1)} %get-tuple-element.28), channel_id=1, replica_groups=mesh['y'=4,'z'=8,'proto'=8] {'y','z'}, dimensions={0} | all-to-all | bytes 262144 | tf_op jit(solution)/shard_map/all_to_all | solution.py:399
  70.6 0.6 shard_map.73
  71.2 8.1 %all_to_all.41.col_ref = f32[8,16,128]{2,1,0:T(8,128)S(1)} all-to-all(f32[8,16,128]{2,1,0:T(8,128)S(1)} %get-tuple-element.30), channel_id=1, replica_groups=mesh['y'=4,'z'=8,'proto'=8] {'proto'}, dimensions={0} | all-to-all | bytes 131072 | tf_op jit(solution)/shard_map/all_to_all | solution.py:399
  79.3 0.6 shard_map.74
  79.9 13.9 %all_to_all.42.row_ref.early_ref = f32[32,8,128]{2,1,0:T(8,128)S(1)} all-to-all(f32[32,8,128]{2,1,0:T(8,128)S(1)} %shard_map.74), channel_id=1, replica_groups=mesh['y'=4,'z'=8,'proto'=8] {'y','z'}, dimensions={0} | all-to-all | bytes 262144 | tf_op jit(solution)/shard_map/all_to_all | solution.py:399
  93.8 0.6 shard_map.75
  94.4 8.0 %all_to_all.43.col_ref = f32[8,16,128]{2,1,0:T(8,128)S(1)} all-to-all(f32[8,16,128]{2,1,0:T(8,128)S(1)} %shard_map.75), channel_id=1, replica_groups=mesh['y'=4,'z'=8,'proto'=8] {'proto'}, dimensions={0} | all-to-all | bytes 131072 | tf_op jit(solution)/shard_map/all_to_all | solution.py:399
  102.4 0.6 shard_map.76
  103.0 13.9 %all_to_all.44.row_ref = f32[32,8,128]{2,1,0:T(8,128)S(1)} all-to-all(f32[32,8,128]{2,1,0:T(8,128)S(1)} %shard_map.76), channel_id=1, replica_groups=mesh['y'=4,'z'=8,'proto'=8] {'y','z'}, dimensions={0} | all-to-all | bytes 262144 | tf_op jit(solution)/shard_map/all_to_all | solution.py:399
  116.9 5.5 %shard_map.77 = (bf16[32,32,256]{2,1,0:T(8,128)(2,1)}, f32[4,256,256]{2,1,0:T(8,128)S(1)}, f32[4,256,256]{2,1,0:T(8,128)}) custom-call(s32[3]{0:T(128)S(1)} %pad_add_fusion.place_ref.refs_0_, s32[8,128]{1,0:T(8,128)S(1)} %get-tuple-element.20.base_ref, f32[528,2048]{1,0:T(8,128)S(1)} %get-tuple-element.25.exp_ref, ...), custom_call_target="tpu_custom_call" | custom-call | flops 553648128 | bytes 8650752 | tf_op jit(solution)/shard_map/pallas_call | solution.py:382
  122.4 0.0 copy-start
  122.4 0.0 collective-permute-start.7
  122.4 4.5 %all-to-all-start.7 = ((bf16[32,32,256]{2,1,0:T(8,128)(2,1)}), bf16[32,32,256]{2,1,0:T(8,128)(2,1)S(1)}, u32[]{:S(2)}, u32[]{:S(2)}) async-start(bf16[32,32,256]{2,1,0:T(8,128)(2,1)} %get-tuple-element.36), calls=%async_computation.7 | async-start | bytes 1048576 | tf_op jit(solution)/shard_map/all_to_all | solution.py:399
  126.9 0.0 collective-permute-done.7
  126.9 0.0 copy-start.1
  126.9 1.0 copy-done.1
  127.9 1.4 add.7.near_ref
  129.2 0.1 slice_bitcast_fusion
  129.3 1.2 collective-permute-start.10
  130.5 1.5 collective-permute-start.9
  132.0 0.0 collective-permute-start.8
  132.0 13.4 %all-to-all-done.7.parts_ref = bf16[32,32,256]{2,1,0:T(8,128)(2,1)S(1)} async-done(((bf16[32,32,256]{2,1,0:T(8,128)(2,1)}), bf16[32,32,256]{2,1,0:T(8,128)(2,1)S(1)}, u32[]{:S(2)}, u32[]{:S(2)}) %all-to-all-start.7) | async-done | bytes 524320 | tf_op jit(solution)/shard_map/all_to_all | solution.py:399
  145.4 0.1 shard_map.79
  145.5 0.1 collective-permute-start.11
  145.6 1.2 collective-permute-done.11
  146.8 0.6 collective-permute-start.14
  147.4 2.0 %collective-permute-start.13 = (f32[2,32,256]{2,1,0:T(8,128)S(1)}, f32[2,32,256]{2,1,0:T(8,128)S(1)}, u32[]{:S(2)}, u32[]{:S(2)}) collective-permute-start(f32[2,32,256]{2,1,0:T(8,128)S(1)} %pad_maximum_fusion.1.refs_0_), channel_id=1, source_target_pairs={{0,4},{1,5},{2,6},{3,7},{4,0},{5,1},{6,2},{7,3},{8,12},{9,13},{10,... | collective-permute-start | bytes 196616 | tf_op jit(solution)/shard_map/ppermute | solution.py:519
  149.4 0.0 collective-permute-done.10.refs_2_
  149.4 1.0 collective-permute-start.12
  150.5 0.0 collective-permute-done.9.refs_1_
  150.5 0.0 collective-permute-done.8.refs_0_
  150.5 0.0 copy-done
  150.5 1.8 %shard_map.78 = (bf16[512,256]{1,0:T(8,128)(2,1)S(1)}, f32[256,256]{1,0:T(8,128)}) custom-call(s32[3]{0:T(128)S(1)} %pad_add_fusion.place_ref.refs_0_, s32[1]{0:T(128)S(6)} %copy.7.count_ref, s32[1,512]{1,0:T(1,128)S(1)} %copy-done, f32[4,256,256]{2,1,0:T(8,128)S(1)} %add.7.near_ref, f32[256,256]{1,0:T(8,128)S(1)} %collective-permute-done.8.refs_0_, ...), custom_call_target="tpu_custom_call" | custom-call | tf_op jit(solution)/shard_map/pallas_call | solution.py:382
  152.3 1.3 collective-permute-done.14.refs_3_
  153.6 0.0 collective-permute-done.13.refs_2_
  153.6 0.6 collective-permute-done.12.refs_1_
  154.2 1.2 shard_map.80
  (1 shorter events, 0.0 us)
Async XLA Ops:
  0.6 12.1 %collective-permute-start.3 = (bf16[256,256]{1,0:T(8,128)(2,1)}, bf16[256,256]{1,0:T(8,128)(2,1)S(1)}, u32[]{:S(2)}, u32[]{:S(2)}) collective-permute-start(bf16[256,256]{1,0:T(8,128)(2,1)} %param.7), channel_id=1, source_target_pairs={{0,1},{1,0},{2,3},{3,2},{4,5},{5,4},{6,7},{7,6},{8,9},{9,8},{10,11... | collective-permute-start | bytes 393224 | tf_op jit(solution)/shard_map/ppermute | solution.py:437
  4.1 19.7 %all-to-all-start = ((bf16[8,64,256]{2,1,0:T(8,128)(2,1)}), bf16[8,64,256]{2,1,0:T(8,128)(2,1)S(1)}, u32[]{:S(2)}, u32[]{:S(2)}) async-start(bf16[8,64,256]{2,1,0:T(8,128)(2,1)} %shard_map.68), calls=%async_computation | async-start | bytes 524288 | tf_op jit(solution)/shard_map/all_to_all | solution.py:399
  13.6 14.6 %collective-permute-start.6 = (bf16[2,256,256]{2,1,0:T(8,128)(2,1)S(1)}, bf16[2,256,256]{2,1,0:T(8,128)(2,1)S(1)}, u32[]{:S(2)}, u32[]{:S(2)}) collective-permute-start(bf16[2,256,256]{2,1,0:T(8,128)(2,1)S(1)} %pad_maximum_fusion.refs_0_), channel_id=1, source_target_pairs={{0,2},{1,3},{2,4},{3,5},{4,6},{5,7},{6,0},{7,1},{8,10},{9,11},{10,... | collective-permute-start | bytes 786440 | tf_op jit(solution)/shard_map/ppermute | solution.py:440
  15.2 14.5 %collective-permute-start.5 = (bf16[2,256,256]{2,1,0:T(8,128)(2,1)S(1)}, bf16[2,256,256]{2,1,0:T(8,128)(2,1)S(1)}, u32[]{:S(2)}, u32[]{:S(2)}) collective-permute-start(bf16[2,256,256]{2,1,0:T(8,128)(2,1)S(1)} %pad_maximum_fusion.refs_0_), channel_id=1, source_target_pairs={{0,4},{1,5},{2,6},{3,7},{4,0},{5,1},{6,2},{7,3},{8,12},{9,13},{10,... | collective-permute-start | bytes 786440 | tf_op jit(solution)/shard_map/ppermute | solution.py:440
  17.9 11.8 %collective-permute-start.4 = (bf16[2,256,256]{2,1,0:T(8,128)(2,1)S(1)}, bf16[2,256,256]{2,1,0:T(8,128)(2,1)S(1)}, u32[]{:S(2)}, u32[]{:S(2)}) collective-permute-start(bf16[2,256,256]{2,1,0:T(8,128)(2,1)S(1)} %pad_maximum_fusion.refs_0_), channel_id=1, source_target_pairs={{0,6},{1,7},{2,0},{3,1},{4,2},{5,3},{6,4},{7,5},{8,14},{9,15},{10,... | collective-permute-start | bytes 786440 | tf_op jit(solution)/shard_map/ppermute | solution.py:440
  23.8 9.5 %collective-permute-start.2 = (bf16[8,64,256]{2,1,0:T(8,128)(2,1)S(1)}, bf16[8,64,256]{2,1,0:T(8,128)(2,1)S(1)}, u32[]{:S(2)}, u32[]{:S(2)}) collective-permute-start(bf16[8,64,256]{2,1,0:T(8,128)(2,1)S(1)} %all-to-all-done.refs_1_), channel_id=1, source_target_pairs={{0,64},{64,128},{128,192},{192,0},{1,65},{65,129},{129,193},{193,1... | collective-permute-start | bytes 786440 | tf_op jit(solution)/shard_map/ppermute | solution.py:436
  25.4 12.7 %collective-permute-start.1 = (bf16[8,64,256]{2,1,0:T(8,128)(2,1)S(1)}, bf16[8,64,256]{2,1,0:T(8,128)(2,1)S(1)}, u32[]{:S(2)}, u32[]{:S(2)}) collective-permute-start(bf16[8,64,256]{2,1,0:T(8,128)(2,1)S(1)} %all-to-all-done.refs_1_), channel_id=1, source_target_pairs={{0,128},{64,192},{128,0},{192,64},{1,129},{65,193},{129,1},{193,65... | collective-permute-start | bytes 786440 | tf_op jit(solution)/shard_map/ppermute | solution.py:436
  28.3 9.8 %collective-permute-start = (bf16[8,64,256]{2,1,0:T(8,128)(2,1)S(1)}, bf16[8,64,256]{2,1,0:T(8,128)(2,1)S(1)}, u32[]{:S(2)}, u32[]{:S(2)}) collective-permute-start(bf16[8,64,256]{2,1,0:T(8,128)(2,1)S(1)} %all-to-all-done.refs_1_), channel_id=1, source_target_pairs={{0,192},{64,0},{128,64},{192,128},{1,193},{65,1},{129,65},{193,129... | collective-permute-start | bytes 786440 | tf_op jit(solution)/shard_map/ppermute | solution.py:436
  41.8 9.9 %all-to-all-start.1 = ((f32[8,16,128]{2,1,0:T(8,128)}), f32[8,16,128]{2,1,0:T(8,128)S(1)}, u32[]{:S(2)}, u32[]{:S(2)}) async-start(f32[8,16,128]{2,1,0:T(8,128)} %get-tuple-element.22), calls=%async_computation.1 | async-start | bytes 131072 | tf_op jit(solution)/shard_map/all_to_all | solution.py:399
  122.4 28.1 %copy-start = (s32[1,512]{1,0:T(1,128)S(1)}, s32[1,512]{1,0:T(1,128)}, u32[]{:S(2)}) copy-start(s32[1,512]{1,0:T(1,128)} %mask_ref.3) | copy-start | bytes 6148
  122.4 4.5 %collective-permute-start.7 = (f32[4,256,256]{2,1,0:T(8,128)}, f32[4,256,256]{2,1,0:T(8,128)S(1)}, u32[]{:S(2)}, u32[]{:S(2)}) collective-permute-start(f32[4,256,256]{2,1,0:T(8,128)} %get-tuple-element.34), channel_id=1, source_target_pairs={{0,1},{1,0},{2,3},{3,2},{4,5},{5,4},{6,7},{7,6},{8,9},{9,8},{10,11... | collective-permute-start | bytes 3145736 | tf_op jit(solution)/shard_map/ppermute | solution.py:513
  122.4 23.1 %all-to-all-start.7 = ((bf16[32,32,256]{2,1,0:T(8,128)(2,1)}), bf16[32,32,256]{2,1,0:T(8,128)(2,1)S(1)}, u32[]{:S(2)}, u32[]{:S(2)}) async-start(bf16[32,32,256]{2,1,0:T(8,128)(2,1)} %get-tuple-element.36), calls=%async_computation.7 | async-start | bytes 1048576 | tf_op jit(solution)/shard_map/all_to_all | solution.py:399
  126.9 1.0 copy-start.1
  129.3 20.1 %collective-permute-start.10 = (f32[256,256]{1,0:T(8,128)S(1)}, f32[256,256]{1,0:T(8,128)S(1)}, u32[]{:S(2)}, u32[]{:S(2)}) collective-permute-start(f32[256,256]{1,0:T(8,128)S(1)} %get-tuple-element.38), channel_id=1, source_target_pairs={{0,6},{1,7},{2,0},{3,1},{4,2},{5,3},{6,4},{7,5},{8,14},{9,15},{10,... | collective-permute-start | bytes 786440 | tf_op jit(solution)/shard_map/ppermute | solution.py:514
  130.5 19.9 %collective-permute-start.9 = (f32[256,256]{1,0:T(8,128)S(1)}, f32[256,256]{1,0:T(8,128)S(1)}, u32[]{:S(2)}, u32[]{:S(2)}) collective-permute-start(f32[256,256]{1,0:T(8,128)S(1)} %get-tuple-element.39), channel_id=1, source_target_pairs={{0,4},{1,5},{2,6},{3,7},{4,0},{5,1},{6,2},{7,3},{8,12},{9,13},{10,... | collective-permute-start | bytes 786440 | tf_op jit(solution)/shard_map/ppermute | solution.py:514
  132.0 18.4 %collective-permute-start.8 = (f32[256,256]{1,0:T(8,128)S(1)}, f32[256,256]{1,0:T(8,128)S(1)}, u32[]{:S(2)}, u32[]{:S(2)}) collective-permute-start(f32[256,256]{1,0:T(8,128)S(1)} %get-tuple-element.40), channel_id=1, source_target_pairs={{0,2},{1,3},{2,4},{3,5},{4,6},{5,7},{6,0},{7,1},{8,10},{9,11},{10,... | collective-permute-start | bytes 786440 | tf_op jit(solution)/shard_map/ppermute | solution.py:514
  145.5 1.3 collective-permute-start.11
  146.8 6.8 %collective-permute-start.14 = (f32[2,32,256]{2,1,0:T(8,128)S(1)}, f32[2,32,256]{2,1,0:T(8,128)S(1)}, u32[]{:S(2)}, u32[]{:S(2)}) collective-permute-start(f32[2,32,256]{2,1,0:T(8,128)S(1)} %pad_maximum_fusion.1.refs_0_), channel_id=1, source_target_pairs={{0,2},{1,3},{2,4},{3,5},{4,6},{5,7},{6,0},{7,1},{8,10},{9,11},{10,... | collective-permute-start | bytes 196616 | tf_op jit(solution)/shard_map/ppermute | solution.py:519
  147.4 6.2 %collective-permute-start.13 = (f32[2,32,256]{2,1,0:T(8,128)S(1)}, f32[2,32,256]{2,1,0:T(8,128)S(1)}, u32[]{:S(2)}, u32[]{:S(2)}) collective-permute-start(f32[2,32,256]{2,1,0:T(8,128)S(1)} %pad_maximum_fusion.1.refs_0_), channel_id=1, source_target_pairs={{0,4},{1,5},{2,6},{3,7},{4,0},{5,1},{6,2},{7,3},{8,12},{9,13},{10,... | collective-permute-start | bytes 196616 | tf_op jit(solution)/shard_map/ppermute | solution.py:519
  149.4 4.7 %collective-permute-start.12 = (f32[2,32,256]{2,1,0:T(8,128)S(1)}, f32[2,32,256]{2,1,0:T(8,128)S(1)}, u32[]{:S(2)}, u32[]{:S(2)}) collective-permute-start(f32[2,32,256]{2,1,0:T(8,128)S(1)} %pad_maximum_fusion.1.refs_0_), channel_id=1, source_target_pairs={{0,6},{1,7},{2,0},{3,1},{4,2},{5,3},{6,4},{7,5},{8,14},{9,15},{10,... | collective-permute-start | bytes 196616 | tf_op jit(solution)/shard_map/ppermute | solution.py:519

commit v6 on v4

--- a/solution.py
+++ b/solution.py
@@ -120,16 +120,23 @@
     return (iota((tokens, place.shape[1]), 0).astype(F32) == place).astype(BF16)
 
 
-def prototypes_kernel(place_ref, *refs):
-    *pair_refs, protos_ref = refs
-    share = pair_refs[0].shape[1]
+def prototypes_kernel(place_ref, here_ref, next_ref, last_ref, own_ref, other_ref, protos_ref):
+    share = own_ref.shape[0]
     group = place_ref[0]
     core = lax.rem(group, 2)
-    for away, pair_ref in enumerate(pair_refs):
-        x = lax.rem(group // 2 + away, PROTO // 2)
-        for other in range(2):
-            start = pl.multiple_of((2 * x + (core + other) % 2) * share, share)
-            protos_ref[pl.ds(start, share), :] = pair_ref[other]
+    step = 1 - 2 * core
+
+    def put(values, away, other):
+        x = lax.rem(group // 2 + away + PROTO // 2, PROTO // 2)
+        start = pl.multiple_of((2 * x + lax.rem(core + other, 2)) * share, share)
+        protos_ref[pl.ds(start, share), :] = values
+
+    for other in range(2):
+        put(here_ref[other], 0, other)
+        put(next_ref[other], step, other)
+        put(last_ref[other], -step, 1 - other)
+    put(own_ref[...], 2, 0)
+    put(other_ref[...], 2, 1)
 
 
 def in_order(y, line_refs, pay_ref, first_slot):
@@ -421,12 +428,23 @@
         route = [(i, (i - away) % ROWS) for i in range(ROWS)]
         lines.append(lax.ppermute(pay, "y", route))
     pair = jnp.stack([prototypes, lax.ppermute(prototypes, "proto", swap)])
-    pairs_held = [pair]
-    for away in range(1, half):
-        pairs_held.append(lax.ppermute(pair, "proto", routes[-away % half]))
+    apart = [(p, (p + (2 if p % 2 else -2)) % PROTO) for p in range(PROTO)]
+    beside = lax.ppermute(pair, "proto", apart)
+    opposite = lax.ppermute(prototypes, "proto", routes[2])
     (protos,) = call(
-        prototypes_kernel, [((protos_held, width), BF16)], (place, *pairs_held), scalars=1
-    )
+        prototypes_kernel,
+        [((protos_held, width), BF16)],
+        (
+            place,
+            pair,
+            beside,
+            lax.ppermute(beside, "proto", swap),
+            opposite,
+            lax.ppermute(opposite, "proto", swap),
+        ),
+        scalars=1,
+    )
+
     packed = ((8, LANES), F32)
     col_out = ((PROTO, chunks, LANES), F32)
     row_out = ((devices, 8, LANES), F32)

time: 156 us -> 160 us (1.026)
  waiting for transfers between devices: 32 us -> 35.8 us
  blocking collectives: 60.9 us -> 62.8 us
    ppermute x3 -> x4, waiting for transfers between devices: 0.01 us -> 7.04 us  [the longest x1 5.77 us: on_device(): beside = lax.ppermute(pair, 'proto', apart)]
    all_to_all x3, waiting for transfers between devices: 21.1 us -> 17.5 us  [exchange(): return lax.all_to_all(parts, axis, 0, 0, tiled=True)]
    ppermute x3 -> x4, starting transfers between devices: 5.73 us -> 3.64 us  [the longest x1 2.84 us: on_device(): beside = lax.ppermute(pair, 'proto', apart)]
    all_to_all x5, blocking collectives: 60.9 us -> 62.8 us  [exchange(): return lax.all_to_all(parts, axis, 0, 0, tiled=True)]
  transfers between devices with their start and end apart: 18 -> 19, of which waited for: 8 -> 10; matrix products, arithmetic and copies ran while one was open for 2% -> 2% of each run, Pallas kernels for 5% -> 5%
where the time goes in v6:
time: 160 us; the launch traced here: 159 us
  blocking collectives  62.8 us (39%)
  waiting for transfers between devices  35.8 us (22%)
  starting transfers between devices  33.9 us (21%)
  Pallas kernels  23 us (14%)
  other arithmetic  2.38 us (1%)
    all_to_all x5, blocking collectives, exchange(): return lax.all_to_all(parts, axis, 0, 0, tiled=True)  62.8 us
    pallas_call x13, Pallas kernels, call(): pl.pallas_call(kernel, out_shape=[jax.ShapeDtypeStruct(shape, dtype) for...  20.3 us
    all_to_all x3, starting transfers between devices, exchange(): return lax.all_to_all(parts, axis, 0, 0, tiled=True)  17.9 us
    all_to_all x3, waiting for transfers between devices, exchange(): return lax.all_to_all(parts, axis, 0, 0, tiled=True)  17.5 us
    ppermute x3, waiting for transfers between devices, on_device(): lines.append(lax.ppermute(pay, 'y', route))  8.23 us
    ppermute x3, starting transfers between devices, on_device(): lines.append(lax.ppermute(pay, 'y', route))  5.83 us
    ppermute x1, waiting for transfers between devices, on_device(): beside = lax.ppermute(pair, 'proto', apart)  5.77 us
    ppermute x3, starting transfers between devices, on_device(): all_rows.append(lax.ppermute(rows, 'proto', routes[-away % half]))  3.63 us
  transfers between devices with their start and end apart: 19, of which 10 were waited for; matrix products, arithmetic and copies ran while one was open for 2% of the time, Pallas kernels for 5%

profile of v6, /device:TPU:32, one launch (start us, length us, event | category | flops | bytes accessed | tf_op | source)
XLA Modules:
  0.0 159.4 jit_solution(8576309077673946970)
XLA Ops:
  0.6 0.1 collective-permute-start.3
  1.4 2.7 %shard_map.68 = bf16[8,64,256]{2,1,0:T(8,128)(2,1)} custom-call(s32[1]{0:T(128)S(6)} %copy.7.count_ref, s32[1,512]{1,0:T(1,128)} %mask_ref.3, bf16[512,256]{1,0:T(8,128)(2,1)} %teacher_ref.1, bf16[512,256]{1,0:T(8,128)(2,1)} %student_ref.1), custom_call_target="tpu_custom_call" | custom-call | tf_op jit(solution)/shard_map/pallas_call | solution.py:410
  4.1 8.6 %all-to-all-start = ((bf16[8,64,256]{2,1,0:T(8,128)(2,1)}), bf16[8,64,256]{2,1,0:T(8,128)(2,1)S(1)}, u32[]{:S(2)}, u32[]{:S(2)}) async-start(bf16[8,64,256]{2,1,0:T(8,128)(2,1)} %shard_map.68), calls=%async_computation | async-start | bytes 524288 | tf_op jit(solution)/shard_map/all_to_all | solution.py:392
  12.7 0.0 collective-permute-done.3
  12.7 0.9 pad_maximum_fusion.here_ref
  13.6 2.8 %collective-permute-start.4 = (bf16[2,256,256]{2,1,0:T(8,128)(2,1)S(1)}, bf16[2,256,256]{2,1,0:T(8,128)(2,1)S(1)}, u32[]{:S(2)}, u32[]{:S(2)}) collective-permute-start(bf16[2,256,256]{2,1,0:T(8,128)(2,1)S(1)} %pad_maximum_fusion.here_ref), channel_id=1, source_target_pairs={{0,6},{1,3},{2,0},{3,5},{4,2},{5,7},{6,4},{7,1},{8,14},{9,11},{10,... | collective-permute-start | bytes 786440 | tf_op jit(solution)/shard_map/ppermute | solution.py:432
  16.5 0.8 collective-permute-start.6
  17.3 5.8 %collective-permute-done.4.next_ref = bf16[2,256,256]{2,1,0:T(8,128)(2,1)S(1)} collective-permute-done((bf16[2,256,256]{2,1,0:T(8,128)(2,1)S(1)}, bf16[2,256,256]{2,1,0:T(8,128)(2,1)S(1)}, u32[]{:S(2)}, u32[]{:S(2)}) %collective-permute-start.4) | collective-permute-done | bytes 262176 | tf_op jit(solution)/shard_map/ppermute | solution.py:432
  23.1 0.0 collective-permute-start.5
  23.1 0.7 all-to-all-done.refs_1_
  23.8 1.6 collective-permute-start.2
  25.4 2.9 %collective-permute-start.1 = (bf16[8,64,256]{2,1,0:T(8,128)(2,1)S(1)}, bf16[8,64,256]{2,1,0:T(8,128)(2,1)S(1)}, u32[]{:S(2)}, u32[]{:S(2)}) collective-permute-start(bf16[8,64,256]{2,1,0:T(8,128)(2,1)S(1)} %all-to-all-done.refs_1_), channel_id=1, source_target_pairs={{0,128},{64,192},{128,0},{192,64},{1,129},{65,193},{129,1},{193,65... | collective-permute-start | bytes 786440 | tf_op jit(solution)/shard_map/ppermute | solution.py:429
  28.3 1.3 collective-permute-start
  29.6 0.0 collective-permute-done.6.own_ref
  29.6 0.0 collective-permute-start.7
  29.6 0.1 pad_add_fusion.place_ref.refs_0_
  29.7 1.3 collective-permute-done.7.other_ref
  31.0 0.0 collective-permute-done.5.last_ref
  31.0 0.6 shard_map.69.refs_5_.refs_6_.protos_ref
  31.6 1.5 collective-permute-done.2.refs_4_
  33.1 6.7 %collective-permute-done.1.refs_3_ = bf16[8,64,256]{2,1,0:T(8,128)(2,1)S(1)} collective-permute-done((bf16[8,64,256]{2,1,0:T(8,128)(2,1)S(1)}, bf16[8,64,256]{2,1,0:T(8,128)(2,1)S(1)}, u32[]{:S(2)}, u32[]{:S(2)}) %collective-permute-start.1) | collective-permute-done | bytes 262176 | tf_op jit(solution)/shard_map/ppermute | solution.py:429
  39.8 0.0 collective-permute-done.refs_2_
  39.8 3.7 %shard_map.70 = (bf16[528,256]{1,0:T(8,128)(2,1)S(1)}, f32[8,1024]{1,0:T(8,128)S(1)}, f32[8,128]{1,0:T(8,128)S(1)}, s32[8,128]{1,0:T(8,128)S(1)}, f32[8,16,128]{2,1,0:T(8,128)}) custom-call(s32[3]{0:T(128)S(1)} %pad_add_fusion.place_ref.refs_0_, bf16[8,64,256]{2,1,0:T(8,128)(2,1)S(1)} %all-to-all-done.refs_1_, ...), custom_call_target="tpu_custom_call" | custom-call | flops 553648128 | bytes 8650752 | tf_op jit(solution)/shard_map/pallas_call | solution.py:375
  43.6 4.9 %all-to-all-start.1 = ((f32[8,16,128]{2,1,0:T(8,128)}), f32[8,16,128]{2,1,0:T(8,128)S(1)}, u32[]{:S(2)}, u32[]{:S(2)}) async-start(f32[8,16,128]{2,1,0:T(8,128)} %get-tuple-element.23), calls=%async_computation.1 | async-start | bytes 131072 | tf_op jit(solution)/shard_map/all_to_all | solution.py:392
  48.5 3.2 %shard_map.71 = (bf16[528,256]{1,0:T(8,128)(2,1)S(1)}, f32[8,128]{1,0:T(8,128)S(1)}) custom-call(s32[3]{0:T(128)S(1)} %pad_add_fusion.place_ref.refs_0_, bf16[8,64,256]{2,1,0:T(8,128)(2,1)S(1)} %all-to-all-done.refs_1_, bf16[8,64,256]{2,1,0:T(8,128)(2,1)S(1)} %collective-permute-done.refs_2_, bf16[8,64,256]{2,1,0:T(8,128)(2,1)S(1)} %collective-permute-done.1.refs_3_, ...), custom_call_target="tpu_custom_call" | custom-call | flops 553648128 | bytes 8650752 | tf_op jit(solution)/shard_map/pallas_call | solution.py:375
  51.7 2.4 %all-to-all-done.1.col_ref = f32[8,16,128]{2,1,0:T(8,128)S(1)} async-done(((f32[8,16,128]{2,1,0:T(8,128)}), f32[8,16,128]{2,1,0:T(8,128)S(1)}, u32[]{:S(2)}, u32[]{:S(2)}) %all-to-all-start.1) | async-done | bytes 65568 | tf_op jit(solution)/shard_map/all_to_all | solution.py:392
  54.1 1.8 %shard_map.72 = (f32[528,2048]{1,0:T(8,128)S(1)}, f32[8,128]{1,0:T(8,128)S(1)}, f32[32,8,128]{2,1,0:T(8,128)S(1)}, f32[8,128]{1,0:T(8,128)S(1)}) custom-call(bf16[528,256]{1,0:T(8,128)(2,1)S(1)} %get-tuple-element.22.teach_ref, bf16[2048,256]{1,0:T(8,128)(2,1)S(1)} %shard_map.69.refs_5_.refs_6_.protos_ref, f32[8,16,128]{2,1,0:T(8,128)S(1)} %all-to-all-done.1.col_ref, ...), custom_call_target="tpu_custom_call" | custom-call | flops 553648128 | bytes 8650752 | tf_op jit(solution)/shard_map/pallas_call | solution.py:375
  55.9 18.9 %all_to_all.40.row_ref = f32[32,8,128]{2,1,0:T(8,128)S(1)} all-to-all(f32[32,8,128]{2,1,0:T(8,128)S(1)} %get-tuple-element.29), channel_id=1, replica_groups=mesh['y'=4,'z'=8,'proto'=8] {'y','z'}, dimensions={0} | all-to-all | bytes 262144 | tf_op jit(solution)/shard_map/all_to_all | solution.py:392
  74.9 0.6 shard_map.73
  75.5 8.1 %all_to_all.41.col_ref = f32[8,16,128]{2,1,0:T(8,128)S(1)} all-to-all(f32[8,16,128]{2,1,0:T(8,128)S(1)} %get-tuple-element.31), channel_id=1, replica_groups=mesh['y'=4,'z'=8,'proto'=8] {'proto'}, dimensions={0} | all-to-all | bytes 131072 | tf_op jit(solution)/shard_map/all_to_all | solution.py:392
  83.6 0.6 shard_map.74
  84.2 13.9 %all_to_all.42.row_ref.early_ref = f32[32,8,128]{2,1,0:T(8,128)S(1)} all-to-all(f32[32,8,128]{2,1,0:T(8,128)S(1)} %shard_map.74), channel_id=1, replica_groups=mesh['y'=4,'z'=8,'proto'=8] {'y','z'}, dimensions={0} | all-to-all | bytes 262144 | tf_op jit(solution)/shard_map/all_to_all | solution.py:392
  98.1 0.6 shard_map.75
  98.6 8.0 %all_to_all.43.col_ref = f32[8,16,128]{2,1,0:T(8,128)S(1)} all-to-all(f32[8,16,128]{2,1,0:T(8,128)S(1)} %shard_map.75), channel_id=1, replica_groups=mesh['y'=4,'z'=8,'proto'=8] {'proto'}, dimensions={0} | all-to-all | bytes 131072 | tf_op jit(solution)/shard_map/all_to_all | solution.py:392
  106.6 0.6 shard_map.76
  107.3 13.9 %all_to_all.44.row_ref = f32[32,8,128]{2,1,0:T(8,128)S(1)} all-to-all(f32[32,8,128]{2,1,0:T(8,128)S(1)} %shard_map.76), channel_id=1, replica_groups=mesh['y'=4,'z'=8,'proto'=8] {'y','z'}, dimensions={0} | all-to-all | bytes 262144 | tf_op jit(solution)/shard_map/all_to_all | solution.py:392
  121.1 3.9 %shard_map.77 = (bf16[32,32,256]{2,1,0:T(8,128)(2,1)}, bf16[528,2048]{1,0:T(8,128)(2,1)S(1)}) custom-call(s32[8,128]{1,0:T(8,128)S(1)} %get-tuple-element.21.base_ref, f32[528,2048]{1,0:T(8,128)S(1)} %get-tuple-element.26.exp_ref, f32[8,128]{1,0:T(8,128)S(1)} %get-tuple-element.30.factor_ref, f32[8,128]{1,0:T(8,128)S(1)} %get-tuple-element.28.valid_ref, ...), custom_call_target="tpu_custom_call" | custom-call | flops 553648128 | bytes 8650752 | tf_op jit(solution)/shard_map/pallas_call | solution.py:375
  125.0 0.0 copy-start
  125.0 1.6 %shard_map.78 = (f32[4,256,256]{2,1,0:T(8,128)S(1)}, f32[4,256,256]{2,1,0:T(8,128)S(1)}) custom-call(s32[3]{0:T(128)S(1)} %pad_add_fusion.place_ref.refs_0_, bf16[528,2048]{1,0:T(8,128)(2,1)S(1)} %get-tuple-element.34.grad_ref, bf16[528,256]{1,0:T(8,128)(2,1)S(1)} %get-tuple-element.33.stud_ref), custom_call_target="tpu_custom_call" | custom-call | flops 553648128 | bytes 8650752 | tf_op jit(solution)/shard_map/pallas_call | solution.py:375
  126.6 0.1 collective-permute-start.8
  126.7 4.3 %all-to-all-start.7 = ((bf16[32,32,256]{2,1,0:T(8,128)(2,1)}), bf16[32,32,256]{2,1,0:T(8,128)(2,1)S(1)}, u32[]{:S(2)}, u32[]{:S(2)}) async-start(bf16[32,32,256]{2,1,0:T(8,128)(2,1)} %get-tuple-element.38), calls=%async_computation.7 | async-start | bytes 1048576 | tf_op jit(solution)/shard_map/all_to_all | solution.py:392
  131.1 0.0 collective-permute-done.8
  131.1 1.4 add.7.near_ref
  132.4 0.1 slice_bitcast_fusion
  132.5 1.2 collective-permute-start.11
  133.7 1.5 collective-permute-start.10
  135.2 0.0 collective-permute-start.9
  135.2 14.3 %all-to-all-done.7.parts_ref = bf16[32,32,256]{2,1,0:T(8,128)(2,1)S(1)} async-done(((bf16[32,32,256]{2,1,0:T(8,128)(2,1)}), bf16[32,32,256]{2,1,0:T(8,128)(2,1)S(1)}, u32[]{:S(2)}, u32[]{:S(2)}) %all-to-all-start.7) | async-done | bytes 524320 | tf_op jit(solution)/shard_map/all_to_all | solution.py:392
  149.5 0.1 shard_map.80
  149.6 0.1 collective-permute-start.12
  149.7 1.2 collective-permute-done.12
  150.9 0.6 collective-permute-start.15
  151.5 2.0 %collective-permute-start.14 = (f32[2,32,256]{2,1,0:T(8,128)S(1)}, f32[2,32,256]{2,1,0:T(8,128)S(1)}, u32[]{:S(2)}, u32[]{:S(2)}) collective-permute-start(f32[2,32,256]{2,1,0:T(8,128)S(1)} %pad_maximum_fusion.1.refs_0_), channel_id=1, source_target_pairs={{0,4},{1,5},{2,6},{3,7},{4,0},{5,1},{6,2},{7,3},{8,12},{9,13},{10,... | collective-permute-start | bytes 196616 | tf_op jit(solution)/shard_map/ppermute | solution.py:523
  153.5 0.0 collective-permute-done.11.refs_2_
  153.5 1.0 collective-permute-start.13
  154.5 0.0 collective-permute-done.10.refs_1_
  154.6 0.0 collective-permute-done.9.refs_0_
  154.6 0.0 copy-done
  154.6 1.8 %shard_map.79 = (bf16[512,256]{1,0:T(8,128)(2,1)S(1)}, f32[256,256]{1,0:T(8,128)}) custom-call(s32[3]{0:T(128)S(1)} %pad_add_fusion.place_ref.refs_0_, s32[1]{0:T(128)S(6)} %copy.7.count_ref, s32[1,512]{1,0:T(1,128)S(1)} %copy-done, f32[4,256,256]{2,1,0:T(8,128)S(1)} %add.7.near_ref, f32[256,256]{1,0:T(8,128)S(1)} %collective-permute-done.9.refs_0_, ...), custom_call_target="tpu_custom_call" | custom-call | tf_op jit(solution)/shard_map/pallas_call | solution.py:375
  156.4 1.3 collective-permute-done.15.refs_3_
  157.7 0.0 collective-permute-done.14.refs_2_
  157.7 0.6 collective-permute-done.13.refs_1_
  158.3 1.2 shard_map.81
  (1 shorter events, 0.0 us)
Async XLA Ops:
  0.6 12.1 %collective-permute-start.3 = (bf16[256,256]{1,0:T(8,128)(2,1)}, bf16[256,256]{1,0:T(8,128)(2,1)S(1)}, u32[]{:S(2)}, u32[]{:S(2)}) collective-permute-start(bf16[256,256]{1,0:T(8,128)(2,1)} %param.7), channel_id=1, source_target_pairs={{0,1},{1,0},{2,3},{3,2},{4,5},{5,4},{6,7},{7,6},{8,9},{9,8},{10,11... | collective-permute-start | bytes 393224 | tf_op jit(solution)/shard_map/ppermute | solution.py:430
  4.1 19.7 %all-to-all-start = ((bf16[8,64,256]{2,1,0:T(8,128)(2,1)}), bf16[8,64,256]{2,1,0:T(8,128)(2,1)S(1)}, u32[]{:S(2)}, u32[]{:S(2)}) async-start(bf16[8,64,256]{2,1,0:T(8,128)(2,1)} %shard_map.68), calls=%async_computation | async-start | bytes 524288 | tf_op jit(solution)/shard_map/all_to_all | solution.py:392
  13.6 9.4 %collective-permute-start.4 = (bf16[2,256,256]{2,1,0:T(8,128)(2,1)S(1)}, bf16[2,256,256]{2,1,0:T(8,128)(2,1)S(1)}, u32[]{:S(2)}, u32[]{:S(2)}) collective-permute-start(bf16[2,256,256]{2,1,0:T(8,128)(2,1)S(1)} %pad_maximum_fusion.here_ref), channel_id=1, source_target_pairs={{0,6},{1,3},{2,0},{3,5},{4,2},{5,7},{6,4},{7,1},{8,14},{9,11},{10,... | collective-permute-start | bytes 786440 | tf_op jit(solution)/shard_map/ppermute | solution.py:432
  16.5 13.1 %collective-permute-start.6 = (bf16[256,256]{1,0:T(8,128)(2,1)}, bf16[256,256]{1,0:T(8,128)(2,1)S(1)}, u32[]{:S(2)}, u32[]{:S(2)}) collective-permute-start(bf16[256,256]{1,0:T(8,128)(2,1)} %param.7), channel_id=1, source_target_pairs={{0,4},{1,5},{2,6},{3,7},{4,0},{5,1},{6,2},{7,3},{8,12},{9,13},{10,... | collective-permute-start | bytes 393224 | tf_op jit(solution)/shard_map/ppermute | solution.py:433
  23.1 7.9 %collective-permute-start.5 = (bf16[2,256,256]{2,1,0:T(8,128)(2,1)S(1)}, bf16[2,256,256]{2,1,0:T(8,128)(2,1)S(1)}, u32[]{:S(2)}, u32[]{:S(2)}) collective-permute-start(bf16[2,256,256]{2,1,0:T(8,128)(2,1)S(1)} %collective-permute-done.4.next_ref), channel_id=1, source_target_pairs={{0,1},{1,0},{2,3},{3,2},{4,5},{5,4},{6,7},{7,6},{8,9},{9,8},{10,11... | collective-permute-start | bytes 786440 | tf_op jit(solution)/shard_map/ppermute | solution.py:441
  23.8 9.3 %collective-permute-start.2 = (bf16[8,64,256]{2,1,0:T(8,128)(2,1)S(1)}, bf16[8,64,256]{2,1,0:T(8,128)(2,1)S(1)}, u32[]{:S(2)}, u32[]{:S(2)}) collective-permute-start(bf16[8,64,256]{2,1,0:T(8,128)(2,1)S(1)} %all-to-all-done.refs_1_), channel_id=1, source_target_pairs={{0,64},{64,128},{128,192},{192,0},{1,65},{65,129},{129,193},{193,1... | collective-permute-start | bytes 786440 | tf_op jit(solution)/shard_map/ppermute | solution.py:429
  25.4 14.5 %collective-permute-start.1 = (bf16[8,64,256]{2,1,0:T(8,128)(2,1)S(1)}, bf16[8,64,256]{2,1,0:T(8,128)(2,1)S(1)}, u32[]{:S(2)}, u32[]{:S(2)}) collective-permute-start(bf16[8,64,256]{2,1,0:T(8,128)(2,1)S(1)} %all-to-all-done.refs_1_), channel_id=1, source_target_pairs={{0,128},{64,192},{128,0},{192,64},{1,129},{65,193},{129,1},{193,65... | collective-permute-start | bytes 786440 | tf_op jit(solution)/shard_map/ppermute | solution.py:429
  28.3 11.6 %collective-permute-start = (bf16[8,64,256]{2,1,0:T(8,128)(2,1)S(1)}, bf16[8,64,256]{2,1,0:T(8,128)(2,1)S(1)}, u32[]{:S(2)}, u32[]{:S(2)}) collective-permute-start(bf16[8,64,256]{2,1,0:T(8,128)(2,1)S(1)} %all-to-all-done.refs_1_), channel_id=1, source_target_pairs={{0,192},{64,0},{128,64},{192,128},{1,193},{65,1},{129,65},{193,129... | collective-permute-start | bytes 786440 | tf_op jit(solution)/shard_map/ppermute | solution.py:429
  29.6 1.3 collective-permute-start.7
  43.6 10.6 %all-to-all-start.1 = ((f32[8,16,128]{2,1,0:T(8,128)}), f32[8,16,128]{2,1,0:T(8,128)S(1)}, u32[]{:S(2)}, u32[]{:S(2)}) async-start(f32[8,16,128]{2,1,0:T(8,128)} %get-tuple-element.23), calls=%async_computation.1 | async-start | bytes 131072 | tf_op jit(solution)/shard_map/all_to_all | solution.py:392
  125.0 29.6 %copy-start = (s32[1,512]{1,0:T(1,128)S(1)}, s32[1,512]{1,0:T(1,128)}, u32[]{:S(2)}) copy-start(s32[1,512]{1,0:T(1,128)} %mask_ref.3) | copy-start | bytes 6148
  126.6 4.4 %collective-permute-start.8 = (f32[4,256,256]{2,1,0:T(8,128)S(1)}, f32[4,256,256]{2,1,0:T(8,128)}, u32[]{:S(2)}, u32[]{:S(2)}) collective-permute-start(f32[4,256,256]{2,1,0:T(8,128)S(1)} %get-tuple-element.36), channel_id=1, source_target_pairs={{0,1},{1,0},{2,3},{3,2},{4,5},{5,4},{6,7},{7,6},{8,9},{9,8},{10,11... | collective-permute-start | bytes 3145736 | tf_op jit(solution)/shard_map/ppermute | solution.py:517
  126.7 22.8 %all-to-all-start.7 = ((bf16[32,32,256]{2,1,0:T(8,128)(2,1)}), bf16[32,32,256]{2,1,0:T(8,128)(2,1)S(1)}, u32[]{:S(2)}, u32[]{:S(2)}) async-start(bf16[32,32,256]{2,1,0:T(8,128)(2,1)} %get-tuple-element.38), calls=%async_computation.7 | async-start | bytes 1048576 | tf_op jit(solution)/shard_map/all_to_all | solution.py:392
  132.5 21.0 %collective-permute-start.11 = (f32[256,256]{1,0:T(8,128)S(1)}, f32[256,256]{1,0:T(8,128)S(1)}, u32[]{:S(2)}, u32[]{:S(2)}) collective-permute-start(f32[256,256]{1,0:T(8,128)S(1)} %get-tuple-element.40), channel_id=1, source_target_pairs={{0,6},{1,7},{2,0},{3,1},{4,2},{5,3},{6,4},{7,5},{8,14},{9,15},{10,... | collective-permute-start | bytes 786440 | tf_op jit(solution)/shard_map/ppermute | solution.py:518
  133.7 20.8 %collective-permute-start.10 = (f32[256,256]{1,0:T(8,128)S(1)}, f32[256,256]{1,0:T(8,128)S(1)}, u32[]{:S(2)}, u32[]{:S(2)}) collective-permute-start(f32[256,256]{1,0:T(8,128)S(1)} %get-tuple-element.41), channel_id=1, source_target_pairs={{0,4},{1,5},{2,6},{3,7},{4,0},{5,1},{6,2},{7,3},{8,12},{9,13},{10,... | collective-permute-start | bytes 786440 | tf_op jit(solution)/shard_map/ppermute | solution.py:518
  135.2 19.3 %collective-permute-start.9 = (f32[256,256]{1,0:T(8,128)S(1)}, f32[256,256]{1,0:T(8,128)S(1)}, u32[]{:S(2)}, u32[]{:S(2)}) collective-permute-start(f32[256,256]{1,0:T(8,128)S(1)} %get-tuple-element.42), channel_id=1, source_target_pairs={{0,2},{1,3},{2,4},{3,5},{4,6},{5,7},{6,0},{7,1},{8,10},{9,11},{10,... | collective-permute-start | bytes 786440 | tf_op jit(solution)/shard_map/ppermute | solution.py:518
  149.6 1.3 collective-permute-start.12
  150.9 6.8 %collective-permute-start.15 = (f32[2,32,256]{2,1,0:T(8,128)S(1)}, f32[2,32,256]{2,1,0:T(8,128)S(1)}, u32[]{:S(2)}, u32[]{:S(2)}) collective-permute-start(f32[2,32,256]{2,1,0:T(8,128)S(1)} %pad_maximum_fusion.1.refs_0_), channel_id=1, source_target_pairs={{0,2},{1,3},{2,4},{3,5},{4,6},{5,7},{6,0},{7,1},{8,10},{9,11},{10,... | collective-permute-start | bytes 196616 | tf_op jit(solution)/shard_map/ppermute | solution.py:523
  151.5 6.2 %collective-permute-start.14 = (f32[2,32,256]{2,1,0:T(8,128)S(1)}, f32[2,32,256]{2,1,0:T(8,128)S(1)}, u32[]{:S(2)}, u32[]{:S(2)}) collective-permute-start(f32[2,32,256]{2,1,0:T(8,128)S(1)} %pad_maximum_fusion.1.refs_0_), channel_id=1, source_target_pairs={{0,4},{1,5},{2,6},{3,7},{4,0},{5,1},{6,2},{7,3},{8,12},{9,13},{10,... | collective-permute-start | bytes 196616 | tf_op jit(solution)/shard_map/ppermute | solution.py:523
  153.5 4.7 %collective-permute-start.13 = (f32[2,32,256]{2,1,0:T(8,128)S(1)}, f32[2,32,256]{2,1,0:T(8,128)S(1)}, u32[]{:S(2)}, u32[]{:S(2)}) collective-permute-start(f32[2,32,256]{2,1,0:T(8,128)S(1)} %pad_maximum_fusion.1.refs_0_), channel_id=1, source_target_pairs={{0,6},{1,7},{2,0},{3,1},{4,2},{5,3},{6,4},{7,5},{8,14},{9,15},{10,... | collective-permute-start | bytes 196616 | tf_op jit(solution)/shard_map/ppermute | solution.py:523

commit v7 on v4

--- a/solution.py
+++ b/solution.py
@@ -315,16 +315,13 @@
         tok_ref[device, :, :] = rows[:SLOTS, :].astype(BF16)
 
 
-def proto_kernel(place_ref, grad_ref, stud_ref, near_ref, far_ref):
-    share = near_ref.shape[1]
+def proto_kernel(other, place_ref, grad_ref, stud_ref, out_ref):
+    share = out_ref.shape[1]
     group = place_ref[0]
     for away in range(PROTO // 2):
         x = lax.rem(group // 2 + away, PROTO // 2)
-        core = lax.rem(group, 2)
-        start = pl.multiple_of((2 * x + 1 - core) * share, share)
-        far_ref[away, :, :] = dot_tn(grad_ref[:, pl.ds(start, share)], stud_ref[...])
-        start = pl.multiple_of((2 * x + core) * share, share)
-        near_ref[away, :, :] = dot_tn(grad_ref[:, pl.ds(start, share)], stud_ref[...])
+        start = pl.multiple_of((2 * x + lax.rem(group + other, 2)) * share, share)
+        out_ref[away, :, :] = dot_tn(grad_ref[:, pl.ds(start, share)], stud_ref[...])
 
 
 def sum_kernel(parts_ref, out_ref):
@@ -489,13 +486,16 @@
         ),
         cost=work,
     )
-    near, far = call(
-        proto_kernel,
-        [((half, share, width), F32), ((half, share, width), F32)],
-        (place, grads, stud),
-        scalars=1,
-        cost=work,
-    )
+    far, near = [
+        call(
+            functools.partial(proto_kernel, other),
+            [((half, share, width), F32)],
+            (place, grads, stud),
+            scalars=1,
+            cost=work,
+        )[0]
+        for other in (1, 0)
+    ]
     mine = near + lax.ppermute(far, "proto", swap)
     arrived = [lax.ppermute(mine[away], "proto", routes[away]) for away in range(1, half)]
     (rows,) = call(sum_kernel, [((SLOTS, width), F32)], (exchange(grad_slots, TOK),))

time: 156 us -> 157 us (level)
    pallas_call x13 -> x14, Pallas kernels: 20.5 us -> 21.5 us  [call(): pl.pallas_call(kernel, out_shape=[jax.ShapeDtypeStruct(shape, dtype) for...]
  transfers between devices with their start and end apart: 18 -> 18, of which waited for: 8 -> 8; matrix products, arithmetic and copies ran while one was open for 2% -> 2% of each run, Pallas kernels for 5% -> 7%
where the time goes in v7:
time: 157 us; the launch traced here: 156 us
  blocking collectives  60.9 us (39%)
  starting transfers between devices  36 us (23%)
  waiting for transfers between devices  30.9 us (20%)
  Pallas kernels  24.2 us (15%)
  other arithmetic  2.37 us (2%)
    all_to_all x5, blocking collectives, exchange(): return lax.all_to_all(parts, axis, 0, 0, tiled=True)  60.9 us
    pallas_call x14, Pallas kernels, call(): pl.pallas_call(kernel, out_shape=[jax.ShapeDtypeStruct(shape, dtype) for...  21.5 us
    all_to_all x3, waiting for transfers between devices, exchange(): return lax.all_to_all(parts, axis, 0, 0, tiled=True)  20 us
    all_to_all x3, starting transfers between devices, exchange(): return lax.all_to_all(parts, axis, 0, 0, tiled=True)  17.9 us
    ppermute x3, waiting for transfers between devices, on_device(): lines.append(lax.ppermute(pay, 'y', route))  7.74 us
    ppermute x3, starting transfers between devices, on_device(): lines.append(lax.ppermute(pay, 'y', route))  5.83 us
    ppermute x3, starting transfers between devices, on_device(): pairs_held.append(lax.ppermute(pair, 'proto', routes[-away % half]))  5.73 us
    ppermute x3, starting transfers between devices, on_device(): all_rows.append(lax.ppermute(rows, 'proto', routes[-away % half]))  3.63 us
  transfers between devices with their start and end apart: 18, of which 8 were waited for; matrix products, arithmetic and copies ran while one was open for 2% of the time, Pallas kernels for 7%

profile of v7, /device:TPU:32, one launch (start us, length us, event | category | flops | bytes accessed | tf_op | source)
XLA Modules:
  0.0 155.9 jit_solution(13948219056948659108)
XLA Ops:
  0.6 0.1 collective-permute-start.3
  1.4 2.7 %shard_map.68 = bf16[8,64,256]{2,1,0:T(8,128)(2,1)} custom-call(s32[1]{0:T(128)S(6)} %copy.7.count_ref, s32[1,512]{1,0:T(1,128)} %mask_ref.3, bf16[512,256]{1,0:T(8,128)(2,1)} %teacher_ref.1, bf16[512,256]{1,0:T(8,128)(2,1)} %student_ref.1), custom_call_target="tpu_custom_call" | custom-call | tf_op jit(solution)/shard_map/pallas_call | solution.py:400
  4.1 8.6 %all-to-all-start = ((bf16[8,64,256]{2,1,0:T(8,128)(2,1)}), bf16[8,64,256]{2,1,0:T(8,128)(2,1)S(1)}, u32[]{:S(2)}, u32[]{:S(2)}) async-start(bf16[8,64,256]{2,1,0:T(8,128)(2,1)} %shard_map.68), calls=%async_computation | async-start | bytes 524288 | tf_op jit(solution)/shard_map/all_to_all | solution.py:382
  12.7 0.0 collective-permute-done.3
  12.7 0.9 pad_maximum_fusion.refs_0_
  13.6 1.6 %collective-permute-start.6 = (bf16[2,256,256]{2,1,0:T(8,128)(2,1)S(1)}, bf16[2,256,256]{2,1,0:T(8,128)(2,1)S(1)}, u32[]{:S(2)}, u32[]{:S(2)}) collective-permute-start(bf16[2,256,256]{2,1,0:T(8,128)(2,1)S(1)} %pad_maximum_fusion.refs_0_), channel_id=1, source_target_pairs={{0,2},{1,3},{2,4},{3,5},{4,6},{5,7},{6,0},{7,1},{8,10},{9,11},{10,... | collective-permute-start | bytes 786440 | tf_op jit(solution)/shard_map/ppermute | solution.py:423
  15.2 2.7 %collective-permute-start.5 = (bf16[2,256,256]{2,1,0:T(8,128)(2,1)S(1)}, bf16[2,256,256]{2,1,0:T(8,128)(2,1)S(1)}, u32[]{:S(2)}, u32[]{:S(2)}) collective-permute-start(bf16[2,256,256]{2,1,0:T(8,128)(2,1)S(1)} %pad_maximum_fusion.refs_0_), channel_id=1, source_target_pairs={{0,4},{1,5},{2,6},{3,7},{4,0},{5,1},{6,2},{7,3},{8,12},{9,13},{10,... | collective-permute-start | bytes 786440 | tf_op jit(solution)/shard_map/ppermute | solution.py:423
  17.9 1.4 collective-permute-start.4
  19.4 4.4 %all-to-all-done.refs_1_ = bf16[8,64,256]{2,1,0:T(8,128)(2,1)S(1)} async-done(((bf16[8,64,256]{2,1,0:T(8,128)(2,1)}), bf16[8,64,256]{2,1,0:T(8,128)(2,1)S(1)}, u32[]{:S(2)}, u32[]{:S(2)}) %all-to-all-start) | async-done | bytes 262176 | tf_op jit(solution)/shard_map/all_to_all | solution.py:382
  23.8 1.6 %collective-permute-start.2 = (bf16[8,64,256]{2,1,0:T(8,128)(2,1)S(1)}, bf16[8,64,256]{2,1,0:T(8,128)(2,1)S(1)}, u32[]{:S(2)}, u32[]{:S(2)}) collective-permute-start(bf16[8,64,256]{2,1,0:T(8,128)(2,1)S(1)} %all-to-all-done.refs_1_), channel_id=1, source_target_pairs={{0,64},{64,128},{128,192},{192,0},{1,65},{65,129},{129,193},{193,1... | collective-permute-start | bytes 786440 | tf_op jit(solution)/shard_map/ppermute | solution.py:419
  25.4 2.9 %collective-permute-start.1 = (bf16[8,64,256]{2,1,0:T(8,128)(2,1)S(1)}, bf16[8,64,256]{2,1,0:T(8,128)(2,1)S(1)}, u32[]{:S(2)}, u32[]{:S(2)}) collective-permute-start(bf16[8,64,256]{2,1,0:T(8,128)(2,1)S(1)} %all-to-all-done.refs_1_), channel_id=1, source_target_pairs={{0,128},{64,192},{128,0},{192,64},{1,129},{65,193},{129,1},{193,65... | collective-permute-start | bytes 786440 | tf_op jit(solution)/shard_map/ppermute | solution.py:419
  28.3 0.0 collective-permute-done.6.refs_3_
  28.3 1.3 collective-permute-start
  29.6 0.1 pad_add_fusion.place_ref.refs_0_
  29.7 0.0 collective-permute-done.5.refs_2_
  29.7 0.0 collective-permute-done.4.refs_1_
  29.7 0.6 shard_map.69.refs_5_.refs_6_.protos_ref
  30.3 3.0 %collective-permute-done.2.refs_4_ = bf16[8,64,256]{2,1,0:T(8,128)(2,1)S(1)} collective-permute-done((bf16[8,64,256]{2,1,0:T(8,128)(2,1)S(1)}, bf16[8,64,256]{2,1,0:T(8,128)(2,1)S(1)}, u32[]{:S(2)}, u32[]{:S(2)}) %collective-permute-start.2) | collective-permute-done | bytes 262176 | tf_op jit(solution)/shard_map/ppermute | solution.py:419
  33.3 4.8 %collective-permute-done.1.refs_3_ = bf16[8,64,256]{2,1,0:T(8,128)(2,1)S(1)} collective-permute-done((bf16[8,64,256]{2,1,0:T(8,128)(2,1)S(1)}, bf16[8,64,256]{2,1,0:T(8,128)(2,1)S(1)}, u32[]{:S(2)}, u32[]{:S(2)}) %collective-permute-start.1) | collective-permute-done | bytes 262176 | tf_op jit(solution)/shard_map/ppermute | solution.py:419
  38.1 0.0 collective-permute-done.refs_2_
  38.1 3.7 %shard_map.70 = (bf16[528,256]{1,0:T(8,128)(2,1)S(1)}, f32[8,1024]{1,0:T(8,128)S(1)}, f32[8,128]{1,0:T(8,128)S(1)}, s32[8,128]{1,0:T(8,128)S(1)}, f32[8,16,128]{2,1,0:T(8,128)}) custom-call(s32[3]{0:T(128)S(1)} %pad_add_fusion.place_ref.refs_0_, bf16[8,64,256]{2,1,0:T(8,128)(2,1)S(1)} %all-to-all-done.refs_1_, ...), custom_call_target="tpu_custom_call" | custom-call | flops 553648128 | bytes 8650752 | tf_op jit(solution)/shard_map/pallas_call | solution.py:365
  41.8 4.3 %all-to-all-start.1 = ((f32[8,16,128]{2,1,0:T(8,128)}), f32[8,16,128]{2,1,0:T(8,128)S(1)}, u32[]{:S(2)}, u32[]{:S(2)}) async-start(f32[8,16,128]{2,1,0:T(8,128)} %get-tuple-element.21), calls=%async_computation.1 | async-start | bytes 131072 | tf_op jit(solution)/shard_map/all_to_all | solution.py:382
  46.1 3.2 %shard_map.71 = (bf16[528,256]{1,0:T(8,128)(2,1)S(1)}, f32[8,128]{1,0:T(8,128)S(1)}) custom-call(s32[3]{0:T(128)S(1)} %pad_add_fusion.place_ref.refs_0_, bf16[8,64,256]{2,1,0:T(8,128)(2,1)S(1)} %all-to-all-done.refs_1_, bf16[8,64,256]{2,1,0:T(8,128)(2,1)S(1)} %collective-permute-done.refs_2_, bf16[8,64,256]{2,1,0:T(8,128)(2,1)S(1)} %collective-permute-done.1.refs_3_, ...), custom_call_target="tpu_custom_call" | custom-call | flops 553648128 | bytes 8650752 | tf_op jit(solution)/shard_map/pallas_call | solution.py:365
  49.2 2.5 %all-to-all-done.1.col_ref = f32[8,16,128]{2,1,0:T(8,128)S(1)} async-done(((f32[8,16,128]{2,1,0:T(8,128)}), f32[8,16,128]{2,1,0:T(8,128)S(1)}, u32[]{:S(2)}, u32[]{:S(2)}) %all-to-all-start.1) | async-done | bytes 65568 | tf_op jit(solution)/shard_map/all_to_all | solution.py:382
  51.7 1.9 %shard_map.72 = (f32[528,2048]{1,0:T(8,128)S(1)}, f32[8,128]{1,0:T(8,128)S(1)}, f32[32,8,128]{2,1,0:T(8,128)S(1)}, f32[8,128]{1,0:T(8,128)S(1)}) custom-call(bf16[528,256]{1,0:T(8,128)(2,1)S(1)} %get-tuple-element.20.teach_ref, bf16[2048,256]{1,0:T(8,128)(2,1)S(1)} %shard_map.69.refs_5_.refs_6_.protos_ref, f32[8,16,128]{2,1,0:T(8,128)S(1)} %all-to-all-done.1.col_ref, ...), custom_call_target="tpu_custom_call" | custom-call | flops 553648128 | bytes 8650752 | tf_op jit(solution)/shard_map/pallas_call | solution.py:365
  53.6 17.0 %all_to_all.40.row_ref = f32[32,8,128]{2,1,0:T(8,128)S(1)} all-to-all(f32[32,8,128]{2,1,0:T(8,128)S(1)} %get-tuple-element.27), channel_id=1, replica_groups=mesh['y'=4,'z'=8,'proto'=8] {'y','z'}, dimensions={0} | all-to-all | bytes 262144 | tf_op jit(solution)/shard_map/all_to_all | solution.py:382
  70.6 0.7 shard_map.73
  71.3 8.1 %all_to_all.41.col_ref = f32[8,16,128]{2,1,0:T(8,128)S(1)} all-to-all(f32[8,16,128]{2,1,0:T(8,128)S(1)} %get-tuple-element.29), channel_id=1, replica_groups=mesh['y'=4,'z'=8,'proto'=8] {'proto'}, dimensions={0} | all-to-all | bytes 131072 | tf_op jit(solution)/shard_map/all_to_all | solution.py:382
  79.4 0.6 shard_map.74
  80.0 13.9 %all_to_all.42.row_ref.early_ref = f32[32,8,128]{2,1,0:T(8,128)S(1)} all-to-all(f32[32,8,128]{2,1,0:T(8,128)S(1)} %shard_map.74), channel_id=1, replica_groups=mesh['y'=4,'z'=8,'proto'=8] {'y','z'}, dimensions={0} | all-to-all | bytes 262144 | tf_op jit(solution)/shard_map/all_to_all | solution.py:382
  93.9 0.6 shard_map.75
  94.5 8.0 %all_to_all.43.col_ref = f32[8,16,128]{2,1,0:T(8,128)S(1)} all-to-all(f32[8,16,128]{2,1,0:T(8,128)S(1)} %shard_map.75), channel_id=1, replica_groups=mesh['y'=4,'z'=8,'proto'=8] {'proto'}, dimensions={0} | all-to-all | bytes 131072 | tf_op jit(solution)/shard_map/all_to_all | solution.py:382
  102.5 0.6 shard_map.76
  103.1 13.9 %all_to_all.44.row_ref = f32[32,8,128]{2,1,0:T(8,128)S(1)} all-to-all(f32[32,8,128]{2,1,0:T(8,128)S(1)} %shard_map.76), channel_id=1, replica_groups=mesh['y'=4,'z'=8,'proto'=8] {'y','z'}, dimensions={0} | all-to-all | bytes 262144 | tf_op jit(solution)/shard_map/all_to_all | solution.py:382
  117.0 3.1 %shard_map.77 = (bf16[32,32,256]{2,1,0:T(8,128)(2,1)S(1)}, bf16[528,2048]{1,0:T(8,128)(2,1)S(1)}) custom-call(s32[8,128]{1,0:T(8,128)S(1)} %get-tuple-element.19.base_ref, f32[528,2048]{1,0:T(8,128)S(1)} %get-tuple-element.24.exp_ref, f32[8,128]{1,0:T(8,128)S(1)} %get-tuple-element.28.factor_ref, f32[8,128]{1,0:T(8,128)S(1)} %get-tuple-element.26.valid_ref, ...), custom_call_target="tpu_custom_call" | custom-call | flops 553648128 | bytes 8650752 | tf_op jit(solution)/shard_map/pallas_call | solution.py:365
  120.1 0.0 copy-start
  120.1 1.2 shard_map.79
  121.3 0.1 collective-permute-start.7
  121.4 0.0 copy-done
  121.4 5.0 %all-to-all-start.7 = ((bf16[32,32,256]{2,1,0:T(8,128)(2,1)}), bf16[32,32,256]{2,1,0:T(8,128)(2,1)}, u32[]{:S(2)}, u32[]{:S(2)}) async-start(bf16[32,32,256]{2,1,0:T(8,128)(2,1)} %copy-done), calls=%async_computation.7 | async-start | bytes 1048576 | tf_op jit(solution)/shard_map/all_to_all | solution.py:382
  126.4 0.0 copy-start.1
  126.4 1.2 shard_map.78
  127.6 0.0 collective-permute-done.7
  127.6 1.4 add.7.near_ref
  129.0 0.1 slice_bitcast_fusion
  129.1 1.2 collective-permute-start.10
  130.3 1.5 collective-permute-start.9
  131.8 0.0 collective-permute-start.8
  131.8 13.2 %all-to-all-done.7.parts_ref = bf16[32,32,256]{2,1,0:T(8,128)(2,1)} async-done(((bf16[32,32,256]{2,1,0:T(8,128)(2,1)}), bf16[32,32,256]{2,1,0:T(8,128)(2,1)}, u32[]{:S(2)}, u32[]{:S(2)}) %all-to-all-start.7) | async-done | bytes 524320 | tf_op jit(solution)/shard_map/all_to_all | solution.py:382
  144.9 1.1 shard_map.81
  146.1 0.1 collective-permute-start.11
  146.2 1.2 collective-permute-done.11
  147.4 0.6 collective-permute-start.14
  147.9 2.1 %collective-permute-start.13 = (f32[2,32,256]{2,1,0:T(8,128)S(1)}, f32[2,32,256]{2,1,0:T(8,128)S(1)}, u32[]{:S(2)}, u32[]{:S(2)}) collective-permute-start(f32[2,32,256]{2,1,0:T(8,128)S(1)} %pad_maximum_fusion.1.refs_0_), channel_id=1, source_target_pairs={{0,4},{1,5},{2,6},{3,7},{4,0},{5,1},{6,2},{7,3},{8,12},{9,13},{10,... | collective-permute-start | bytes 196616 | tf_op jit(solution)/shard_map/ppermute | solution.py:505
  150.0 0.0 collective-permute-done.10.refs_2_
  150.0 1.0 collective-permute-start.12
  151.0 0.0 collective-permute-done.9.refs_1_
  151.0 0.0 collective-permute-done.8.refs_0_
  151.0 0.0 copy-done.1
  151.0 1.8 %shard_map.80 = (bf16[512,256]{1,0:T(8,128)(2,1)S(1)}, f32[256,256]{1,0:T(8,128)}) custom-call(s32[3]{0:T(128)S(1)} %pad_add_fusion.place_ref.refs_0_, s32[1]{0:T(128)S(6)} %copy.7.count_ref, s32[1,512]{1,0:T(1,128)S(1)} %copy-done.1, f32[4,256,256]{2,1,0:T(8,128)S(1)} %add.7.near_ref, f32[256,256]{1,0:T(8,128)S(1)} %collective-permute-done.8.refs_0_, ...), custom_call_target="tpu_custom_call" | custom-call | tf_op jit(solution)/shard_map/pallas_call | solution.py:365
  152.8 1.3 collective-permute-done.14.refs_3_
  154.1 0.0 collective-permute-done.13.refs_2_
  154.1 0.6 collective-permute-done.12.refs_1_
  154.7 1.2 shard_map.82
  (1 shorter events, 0.0 us)
Async XLA Ops:
  0.6 12.1 %collective-permute-start.3 = (bf16[256,256]{1,0:T(8,128)(2,1)}, bf16[256,256]{1,0:T(8,128)(2,1)S(1)}, u32[]{:S(2)}, u32[]{:S(2)}) collective-permute-start(bf16[256,256]{1,0:T(8,128)(2,1)} %param.7), channel_id=1, source_target_pairs={{0,1},{1,0},{2,3},{3,2},{4,5},{5,4},{6,7},{7,6},{8,9},{9,8},{10,11... | collective-permute-start | bytes 393224 | tf_op jit(solution)/shard_map/ppermute | solution.py:420
  4.1 19.7 %all-to-all-start = ((bf16[8,64,256]{2,1,0:T(8,128)(2,1)}), bf16[8,64,256]{2,1,0:T(8,128)(2,1)S(1)}, u32[]{:S(2)}, u32[]{:S(2)}) async-start(bf16[8,64,256]{2,1,0:T(8,128)(2,1)} %shard_map.68), calls=%async_computation | async-start | bytes 524288 | tf_op jit(solution)/shard_map/all_to_all | solution.py:382
  13.6 14.6 %collective-permute-start.6 = (bf16[2,256,256]{2,1,0:T(8,128)(2,1)S(1)}, bf16[2,256,256]{2,1,0:T(8,128)(2,1)S(1)}, u32[]{:S(2)}, u32[]{:S(2)}) collective-permute-start(bf16[2,256,256]{2,1,0:T(8,128)(2,1)S(1)} %pad_maximum_fusion.refs_0_), channel_id=1, source_target_pairs={{0,2},{1,3},{2,4},{3,5},{4,6},{5,7},{6,0},{7,1},{8,10},{9,11},{10,... | collective-permute-start | bytes 786440 | tf_op jit(solution)/shard_map/ppermute | solution.py:423
  15.2 14.5 %collective-permute-start.5 = (bf16[2,256,256]{2,1,0:T(8,128)(2,1)S(1)}, bf16[2,256,256]{2,1,0:T(8,128)(2,1)S(1)}, u32[]{:S(2)}, u32[]{:S(2)}) collective-permute-start(bf16[2,256,256]{2,1,0:T(8,128)(2,1)S(1)} %pad_maximum_fusion.refs_0_), channel_id=1, source_target_pairs={{0,4},{1,5},{2,6},{3,7},{4,0},{5,1},{6,2},{7,3},{8,12},{9,13},{10,... | collective-permute-start | bytes 786440 | tf_op jit(solution)/shard_map/ppermute | solution.py:423
  17.9 11.8 %collective-permute-start.4 = (bf16[2,256,256]{2,1,0:T(8,128)(2,1)S(1)}, bf16[2,256,256]{2,1,0:T(8,128)(2,1)S(1)}, u32[]{:S(2)}, u32[]{:S(2)}) collective-permute-start(bf16[2,256,256]{2,1,0:T(8,128)(2,1)S(1)} %pad_maximum_fusion.refs_0_), channel_id=1, source_target_pairs={{0,6},{1,7},{2,0},{3,1},{4,2},{5,3},{6,4},{7,5},{8,14},{9,15},{10,... | collective-permute-start | bytes 786440 | tf_op jit(solution)/shard_map/ppermute | solution.py:423
  23.8 9.5 %collective-permute-start.2 = (bf16[8,64,256]{2,1,0:T(8,128)(2,1)S(1)}, bf16[8,64,256]{2,1,0:T(8,128)(2,1)S(1)}, u32[]{:S(2)}, u32[]{:S(2)}) collective-permute-start(bf16[8,64,256]{2,1,0:T(8,128)(2,1)S(1)} %all-to-all-done.refs_1_), channel_id=1, source_target_pairs={{0,64},{64,128},{128,192},{192,0},{1,65},{65,129},{129,193},{193,1... | collective-permute-start | bytes 786440 | tf_op jit(solution)/shard_map/ppermute | solution.py:419
  25.4 12.7 %collective-permute-start.1 = (bf16[8,64,256]{2,1,0:T(8,128)(2,1)S(1)}, bf16[8,64,256]{2,1,0:T(8,128)(2,1)S(1)}, u32[]{:S(2)}, u32[]{:S(2)}) collective-permute-start(bf16[8,64,256]{2,1,0:T(8,128)(2,1)S(1)} %all-to-all-done.refs_1_), channel_id=1, source_target_pairs={{0,128},{64,192},{128,0},{192,64},{1,129},{65,193},{129,1},{193,65... | collective-permute-start | bytes 786440 | tf_op jit(solution)/shard_map/ppermute | solution.py:419
  28.3 9.8 %collective-permute-start = (bf16[8,64,256]{2,1,0:T(8,128)(2,1)S(1)}, bf16[8,64,256]{2,1,0:T(8,128)(2,1)S(1)}, u32[]{:S(2)}, u32[]{:S(2)}) collective-permute-start(bf16[8,64,256]{2,1,0:T(8,128)(2,1)S(1)} %all-to-all-done.refs_1_), channel_id=1, source_target_pairs={{0,192},{64,0},{128,64},{192,128},{1,193},{65,1},{129,65},{193,129... | collective-permute-start | bytes 786440 | tf_op jit(solution)/shard_map/ppermute | solution.py:419
  41.8 9.9 %all-to-all-start.1 = ((f32[8,16,128]{2,1,0:T(8,128)}), f32[8,16,128]{2,1,0:T(8,128)S(1)}, u32[]{:S(2)}, u32[]{:S(2)}) async-start(f32[8,16,128]{2,1,0:T(8,128)} %get-tuple-element.21), calls=%async_computation.1 | async-start | bytes 131072 | tf_op jit(solution)/shard_map/all_to_all | solution.py:382
  120.1 1.3 copy-start
  121.3 6.3 %collective-permute-start.7 = (f32[4,256,256]{2,1,0:T(8,128)S(1)}, f32[4,256,256]{2,1,0:T(8,128)}, u32[]{:S(2)}, u32[]{:S(2)}) collective-permute-start(f32[4,256,256]{2,1,0:T(8,128)S(1)} %shard_map.79), channel_id=1, source_target_pairs={{0,1},{1,0},{2,3},{3,2},{4,5},{5,4},{6,7},{7,6},{8,9},{9,8},{10,11... | collective-permute-start | bytes 3145736 | tf_op jit(solution)/shard_map/ppermute | solution.py:499
  121.4 23.5 %all-to-all-start.7 = ((bf16[32,32,256]{2,1,0:T(8,128)(2,1)}), bf16[32,32,256]{2,1,0:T(8,128)(2,1)}, u32[]{:S(2)}, u32[]{:S(2)}) async-start(bf16[32,32,256]{2,1,0:T(8,128)(2,1)} %copy-done), calls=%async_computation.7 | async-start | bytes 1048576 | tf_op jit(solution)/shard_map/all_to_all | solution.py:382
  126.4 24.6 %copy-start.1 = (s32[1,512]{1,0:T(1,128)S(1)}, s32[1,512]{1,0:T(1,128)}, u32[]{:S(2)}) copy-start(s32[1,512]{1,0:T(1,128)} %mask_ref.3) | copy-start | bytes 6148
  129.1 20.9 %collective-permute-start.10 = (f32[256,256]{1,0:T(8,128)S(1)}, f32[256,256]{1,0:T(8,128)S(1)}, u32[]{:S(2)}, u32[]{:S(2)}) collective-permute-start(f32[256,256]{1,0:T(8,128)S(1)} %get-tuple-element.36), channel_id=1, source_target_pairs={{0,6},{1,7},{2,0},{3,1},{4,2},{5,3},{6,4},{7,5},{8,14},{9,15},{10,... | collective-permute-start | bytes 786440 | tf_op jit(solution)/shard_map/ppermute | solution.py:500
  130.3 20.7 %collective-permute-start.9 = (f32[256,256]{1,0:T(8,128)S(1)}, f32[256,256]{1,0:T(8,128)S(1)}, u32[]{:S(2)}, u32[]{:S(2)}) collective-permute-start(f32[256,256]{1,0:T(8,128)S(1)} %get-tuple-element.37), channel_id=1, source_target_pairs={{0,4},{1,5},{2,6},{3,7},{4,0},{5,1},{6,2},{7,3},{8,12},{9,13},{10,... | collective-permute-start | bytes 786440 | tf_op jit(solution)/shard_map/ppermute | solution.py:500
  131.8 19.2 %collective-permute-start.8 = (f32[256,256]{1,0:T(8,128)S(1)}, f32[256,256]{1,0:T(8,128)S(1)}, u32[]{:S(2)}, u32[]{:S(2)}) collective-permute-start(f32[256,256]{1,0:T(8,128)S(1)} %get-tuple-element.38), channel_id=1, source_target_pairs={{0,2},{1,3},{2,4},{3,5},{4,6},{5,7},{6,0},{7,1},{8,10},{9,11},{10,... | collective-permute-start | bytes 786440 | tf_op jit(solution)/shard_map/ppermute | solution.py:500
  146.1 1.3 collective-permute-start.11
  147.4 6.8 %collective-permute-start.14 = (f32[2,32,256]{2,1,0:T(8,128)S(1)}, f32[2,32,256]{2,1,0:T(8,128)S(1)}, u32[]{:S(2)}, u32[]{:S(2)}) collective-permute-start(f32[2,32,256]{2,1,0:T(8,128)S(1)} %pad_maximum_fusion.1.refs_0_), channel_id=1, source_target_pairs={{0,2},{1,3},{2,4},{3,5},{4,6},{5,7},{6,0},{7,1},{8,10},{9,11},{10,... | collective-permute-start | bytes 196616 | tf_op jit(solution)/shard_map/ppermute | solution.py:505
  147.9 6.2 %collective-permute-start.13 = (f32[2,32,256]{2,1,0:T(8,128)S(1)}, f32[2,32,256]{2,1,0:T(8,128)S(1)}, u32[]{:S(2)}, u32[]{:S(2)}) collective-permute-start(f32[2,32,256]{2,1,0:T(8,128)S(1)} %pad_maximum_fusion.1.refs_0_), channel_id=1, source_target_pairs={{0,4},{1,5},{2,6},{3,7},{4,0},{5,1},{6,2},{7,3},{8,12},{9,13},{10,... | collective-permute-start | bytes 196616 | tf_op jit(solution)/shard_map/ppermute | solution.py:505
  150.0 4.7 %collective-permute-start.12 = (f32[2,32,256]{2,1,0:T(8,128)S(1)}, f32[2,32,256]{2,1,0:T(8,128)S(1)}, u32[]{:S(2)}, u32[]{:S(2)}) collective-permute-start(f32[2,32,256]{2,1,0:T(8,128)S(1)} %pad_maximum_fusion.1.refs_0_), channel_id=1, source_target_pairs={{0,6},{1,7},{2,0},{3,1},{4,2},{5,3},{6,4},{7,5},{8,14},{9,15},{10,... | collective-permute-start | bytes 196616 | tf_op jit(solution)/shard_map/ppermute | solution.py:505
